TPU v7x, 256 devices: a whole 4x4x8 slice. The times are simulated.
256 devices in a mesh: dom: 64 (over z, x, core), tp: 4 (over y).
Axes of the slice: x: 4, y: 4, z: 8, core: 2. Of those that a mesh axis runs over, the one named last changes fastest.
Arguments:
- prefix_cache: bfloat16 [4, 2, 8192, 1024], P(None, None, 'dom', 'tp'), may hold values from -9 to 9
- suffix_cache: bfloat16 [128, 2, 512, 1024], P('dom', None, None, 'tp'), may hold values from -9 to 9
- queries: bfloat16 [128, 2, 8192], P('dom', None, 'tp'), may hold values from -170 to 170
- step_kv: bfloat16 [128, 2, 2, 1024], P('dom', None, None, 'tp'), may hold values from -9 to 9
- twist_weight: float32 [8192], P('tp'), may hold values from -0.24 to 0.24
- prior_weights: float32 [128], P('dom'), may hold values from -6 to 6
- prompt_ids: int32 [128], P('dom'), may hold values from 0 to 3, as said below
- ancestors: int32 [128], P('dom'), may hold values from 0 to 127, as said below
Outputs:
- log_weights: float32 [128], P('dom')
- copied_cache: bfloat16 [128, 2, 512, 1024], P('dom', None, None, 'tp')
- carried_kv: bfloat16 [128, 2, 1024], P('dom', None, 'tp')
- step_two_out: bfloat16 [128, 8192], P('dom', 'tp')
- twist_two: float32 [128], P('dom')
Inputs may be any that keep to these rules, and one draw needn't show every extreme that they name: `prompt_ids`: prompt ids never fall along the particles; every prompt holds between 16 and 48 particles. `ancestors`: each slot's ancestor has the slot's prompt and lies at most 2 particles away from it; that distance is reached.
All inputs are finite; a program needn't handle non-finite values.
Results may differ from a plain program's by a relative error of at most 0.0075.
Values may be sent and summed in bfloat16 or wider, within the bound.
No kernel may reach another device: no remote copies, remote signals or barrier semaphores. Data moves between devices by JAX's collectives and lax.ppermute only.
A program may use at most 128 MiB of HBM per device.

v0:
```python
import math

import jax
import jax.numpy as jnp
from jax import lax
from jax.sharding import PartitionSpec as P

HEADS = 64
KV_HEADS = 8
HEAD_DIM = 128
REACH = 2


def padded(block, sides, width):
    for axis, dim in sides:
        count = lax.axis_size(axis)
        forward = [(i, i + 1) for i in range(count - 1)]
        backward = [(target, source) for source, target in forward]
        low = lax.ppermute(
            lax.slice_in_dim(block, block.shape[dim] - width, None, axis=dim), axis, forward
        )
        high = lax.ppermute(lax.slice_in_dim(block, 0, width, axis=dim), axis, backward)
        block = jnp.concatenate([low, block, high], axis=dim)
    return block


def combine_parts(first_part, second_part):
    high_a, weighted_a, totals_a = first_part
    high_b, weighted_b, totals_b = second_part
    highest = jnp.maximum(high_a, high_b)
    scale_a = jnp.exp(high_a - highest)
    scale_b = jnp.exp(high_b - highest)
    upper = weighted_a * scale_a[..., None] + weighted_b * scale_b[..., None]
    lower = totals_a * scale_a + totals_b * scale_b
    return upper / lower[..., None]


def local_part(queries_rows, key_rows, value_rows, fresh_keys, fresh_values):
    particles, length, features = key_rows.shape
    kv_count = features // HEAD_DIM
    fresh_count = fresh_keys.shape[1]
    factor = 1.0 / math.sqrt(HEAD_DIM)
    key_heads = key_rows.reshape(particles, length, kv_count, HEAD_DIM)
    value_heads = value_rows.reshape(particles, length, kv_count, HEAD_DIM)
    fresh_key_heads = fresh_keys.reshape(particles, fresh_count, kv_count, HEAD_DIM)
    fresh_value_heads = fresh_values.reshape(particles, fresh_count, kv_count, HEAD_DIM)
    scores = (
        jnp.einsum("pcgd,ptcd->pcgt", queries_rows, key_heads, preferred_element_type=jnp.float32)
        * factor
    )
    fresh_scores = (
        jnp.einsum(
            "pcgd,pncd->pcgn", queries_rows, fresh_key_heads, preferred_element_type=jnp.float32
        )
        * factor
    )
    highest = jnp.maximum(jnp.max(scores, axis=-1), jnp.max(fresh_scores, axis=-1))
    shifted = jnp.exp(scores - highest[..., None])
    fresh_shifted = jnp.exp(fresh_scores - highest[..., None])
    weighted = jnp.einsum(
        "pcgt,ptcd->pcgd",
        shifted.astype(jnp.bfloat16),
        value_heads,
        preferred_element_type=jnp.float32,
    )
    weighted = weighted + jnp.einsum(
        "pcgn,pncd->pcgd",
        fresh_shifted.astype(jnp.bfloat16),
        fresh_value_heads,
        preferred_element_type=jnp.float32,
    )
    totals = jnp.sum(shifted, axis=-1) + jnp.sum(fresh_shifted, axis=-1)
    return (highest, weighted, totals)


def score_all(all_queries, all_ids, prefix_cache):
    prompts, _, positions, features = prefix_cache.shape
    kv_count = features // HEAD_DIM
    group = HEADS // KV_HEADS
    factor = 1.0 / math.sqrt(HEAD_DIM)
    particles = all_queries.shape[0]
    key_table = prefix_cache[:, 0].reshape(prompts, positions, kv_count, HEAD_DIM)
    block_rows = math.gcd(particles, 64)
    query_blocks = all_queries.reshape(
        particles // block_rows, block_rows, 2, kv_count, group, HEAD_DIM
    )

    def score_block(pieces):
        query_piece, id_piece = pieces
        key_piece = jnp.take(key_table, id_piece, axis=0)
        return (
            jnp.einsum(
                "bscgd,btcd->bscgt", query_piece, key_piece, preferred_element_type=jnp.float32
            )
            * factor
        )

    scores = lax.map(
        score_block, (query_blocks, all_ids.reshape(particles // block_rows, block_rows))
    )
    return scores.reshape(particles, 2, kv_count, group, positions)


def weigh_rows(score_rows, high_rows, id_rows, prefix_cache):
    prompts, _, positions, features = prefix_cache.shape
    kv_count = features // HEAD_DIM
    group = HEADS // KV_HEADS
    value_table = prefix_cache[:, 1].reshape(prompts, positions, kv_count, HEAD_DIM)
    row_count = score_rows.shape[0]
    inner_rows = math.gcd(row_count, 64)
    blocks = row_count // inner_rows

    def value_block(pieces):
        score_piece, high_piece, id_piece = pieces
        shifted = jnp.exp(score_piece - high_piece[..., None])
        value_piece = jnp.take(value_table, id_piece, axis=0)
        weighted = jnp.einsum(
            "bscgt,btcd->bscgd",
            shifted.astype(jnp.bfloat16),
            value_piece,
            preferred_element_type=jnp.float32,
        )
        return (weighted, jnp.sum(shifted, axis=-1))

    weighted, totals = lax.map(
        value_block,
        (
            score_rows.reshape(blocks, inner_rows, 2, kv_count, group, positions),
            high_rows.reshape(blocks, inner_rows, 2, kv_count, group),
            id_rows.reshape(blocks, inner_rows),
        ),
    )
    return (
        weighted.reshape(row_count, 2, kv_count, group, HEAD_DIM),
        totals.reshape(row_count, 2, kv_count, group),
    )


def prefix_by_queries(queries, prompt_ids, prefix_cache):
    local_rows = queries.shape[0]
    all_queries, all_ids = (
        lax.all_gather(queries, "dom", axis=0, tiled=True),
        lax.all_gather(prompt_ids, "dom", axis=0, tiled=True),
    )
    scores = score_all(all_queries, all_ids, prefix_cache)
    highest = lax.pmax(jnp.max(scores, axis=-1), "dom")
    weighted, totals = lax.psum_scatter(
        weigh_rows(scores, highest, all_ids, prefix_cache), "dom", scatter_dimension=0, tiled=True
    )
    high_mine = lax.dynamic_slice_in_dim(highest, lax.axis_index("dom") * local_rows, local_rows, 0)
    return (high_mine, weighted, totals)


def twist_value(attention, twist_weight):
    return lax.psum(jnp.sum(attention * twist_weight, axis=-1), "tp")


def body(
    prefix_cache, suffix_cache, queries, step_kv, twist_weight, prior_weights, prompt_ids, ancestors
):
    local_rows = queries.shape[0]
    features = suffix_cache.shape[3]
    kv_count = features // HEAD_DIM
    group = HEADS // KV_HEADS
    prompts = prefix_cache.shape[0]
    pre_high, pre_weighted, pre_totals = prefix_by_queries(queries, prompt_ids, prefix_cache)
    query_heads = queries.reshape(local_rows, 2, kv_count, group, HEAD_DIM)
    first_local = local_part(
        query_heads[:, 0],
        suffix_cache[:, 0],
        suffix_cache[:, 1],
        step_kv[:, 0, 0][:, None],
        step_kv[:, 0, 1][:, None],
    )
    first_attn = combine_parts(
        (pre_high[:, 0], pre_weighted[:, 0], pre_totals[:, 0]), first_local
    ).reshape(local_rows, -1)
    twist_one = twist_value(first_attn, twist_weight)
    raised = prior_weights + twist_one
    table = prompt_ids[:, None] == jnp.arange(prompts, dtype=jnp.int32)[None, :]
    prompt_top = lax.pmax(jnp.max(jnp.where(table, raised[:, None], -1e30), axis=0), "dom")
    prompt_total = lax.psum(
        jnp.sum(jnp.where(table, jnp.exp(raised[:, None] - prompt_top[None, :]), 0.0), axis=0),
        "dom",
    )
    normalizer = jnp.log(prompt_total) + prompt_top
    log_weights = raised - jnp.sum(jnp.where(table, normalizer[None, :], 0.0), axis=1)
    wide_cache, wide_kv = (
        padded(suffix_cache, (("dom", 0),), REACH),
        padded(step_kv[:, 0], (("dom", 0),), REACH),
    )
    local_index = ancestors - (lax.axis_index("dom") * local_rows - REACH)
    copied_cache = jnp.take(wide_cache, local_index, axis=0)
    carried_kv = jnp.take(wide_kv, local_index, axis=0)
    fresh_keys = jnp.stack([carried_kv[:, 0], step_kv[:, 1, 0]], axis=1)
    fresh_values = jnp.stack([carried_kv[:, 1], step_kv[:, 1, 1]], axis=1)
    second_local = local_part(
        query_heads[:, 1], copied_cache[:, 0], copied_cache[:, 1], fresh_keys, fresh_values
    )
    second_attn = combine_parts(
        (pre_high[:, 1], pre_weighted[:, 1], pre_totals[:, 1]), second_local
    ).reshape(local_rows, -1)
    twist_two = twist_value(second_attn, twist_weight)
    return (log_weights, copied_cache, carried_kv, second_attn.astype(jnp.bfloat16), twist_two)


def solution(mesh):
    placed = (
        P(None, None, "dom", "tp"),
        P("dom", None, None, "tp"),
        P("dom", None, "tp"),
        P("dom", None, None, "tp"),
        P("tp"),
        P("dom"),
        P("dom"),
        P("dom"),
    )
    return jax.shard_map(
        body,
        mesh=mesh,
        in_specs=placed,
        out_specs=(
            P("dom"),
            P("dom", None, None, "tp"),
            P("dom", None, "tp"),
            P("dom", "tp"),
            P("dom"),
        ),
        check_vma=False,
    )
```

profile of v0, /device:TPU:1, one launch (start us, length us, event | category | flops | bytes accessed | tf_op | source)
XLA Modules:
  0.0 964.4 jit_solution(177741340950481942)
XLA Ops:
  7.9 4.5 collective-permute-start.2
  14.4 3.6 collective-permute-start
  26.1 20.8 %all-reduce = s32[128]{0:T(128)S(1)} all-reduce(s32[128]{0:T(128)S(1)} %dynamic-update-slice), channel_id=1, replica_groups=mesh['dom'=64,'tp'=4] {'dom'}, use_global_device_ids=true, to_apply=%add | all-reduce | flops 128 | bytes 1024
  49.8 3.2 pad_maximum_fusion
  53.0 3.5 gather_fusion.2
  58.8 45.2 %all-gather.2.cloned.1.call-done = bf16[128,2,2048]{2,1,0:T(2,128)(2,1)} async-done(((bf16[2,2,2048]{2,1,0:T(2,128)(2,1)}), bf16[128,2,2048]{2,1,0:T(2,128)(2,1)}) %all-gather.2.cloned.1.call-update) | async-done | bytes 1048592 | tf_op jit(solution)/shard_map/all_gather | solution.py:142
  104.0 2.5 reshape.221
  106.5 45.9 %while.22 = (s32[]{:T(128)}, f32[2,64,2,2,8,128]{5,4,2,3,1,0:T(8,128)S(1)}, s32[2,64]{1,0:T(2,128)S(1)}, bf16[4,128,2,128]{3,2,1,0:T(2,128)(2,1)S(1)}, bf16[2,64,2,2,8,128]{5,4,3,2,1,0:T(8,128)(2,1)}, /*index=5*/s32[]{:T(128)}) while((s32[]{:T(128)}, f32[2,64,2,2,8,128]{5,4,2,3,1,0:T(8,128)S(1)}, s32[2,64]{1,0:T(2,128)S(1)}, ...), condition=%wide.region_1.3_spmd, body=%wide.region_0.2_spmd.sunk | while | flops 69469568 | bytes 26745060 | solution.py:98
  106.6 10.5 %gather_fusion = bf16[64,128,2,128]{3,2,1,0:T(2,128)(2,1)} fusion(bf16[4,128,2,128]{3,2,1,0:T(2,128)(2,1)S(1)} %get-tuple-element.252, s32[1024]{0:T(1024)S(1)} %pad_clamp_fusion.5), kind=kCustom, calls=%fused_computation.clone.clone.1 | custom fusion | bytes 8388864 | tf_op jit(solution)/shard_map/while/body/eval_jaxpr/jit(_take)/gather | solution.py:90
  117.1 8.0 fusion.98
  125.0 4.4 fusion.99
  129.5 10.5 %gather_fusion = bf16[64,128,2,128]{3,2,1,0:T(2,128)(2,1)} fusion(bf16[4,128,2,128]{3,2,1,0:T(2,128)(2,1)S(1)} %get-tuple-element.252, s32[1024]{0:T(1024)S(1)} %pad_clamp_fusion.5), kind=kCustom, calls=%fused_computation.clone.clone.1 | custom fusion | bytes 8388864 | tf_op jit(solution)/shard_map/while/body/eval_jaxpr/jit(_take)/gather | solution.py:90
  140.1 8.0 fusion.98
  148.0 4.4 fusion.99
  153.5 243.4 %pmax.14 = f32[128,2,2,8]{3,2,0,1:T(2,128)S(1)} all-reduce(f32[128,2,2,8]{3,2,0,1:T(2,128)S(1)} %copy.60), channel_id=1, replica_groups=mesh['dom'=64,'tp'=4] {'dom'}, use_global_device_ids=true, to_apply=%region_3.5 | all-reduce | flops 4096 | bytes 32768 | tf_op jit(solution)/shard_map/pmax | solution.py:146
  397.8 42.4 %while.23 = (s32[]{:T(128)}, f32[2,64,2,2,8,128]{5,4,3,1,0,2:T(8,128)}, f32[2,64,2,2,8]{4,2,3,1,0:T(2,128)}, s32[2,64]{1,0:T(2,128)S(1)}, bf16[4,128,2,128]{3,2,...) while((s32[]{:T(128)}, ...), condition=%wide.region_6.8_spmd, body=%wide.region_4.7_spmd.sunk | while | flops 70253952 | bytes 43554140 | solution.py:125
  397.8 10.5 %gather_fusion.1 = bf16[64,128,2,128]{3,2,1,0:T(2,128)(2,1)} fusion(bf16[4,128,2,128]{3,2,1,0:T(2,128)(2,1)S(1)} %get-tuple-element.275, s32[1024]{0:T(1024)S(1)} %pad_clamp_fusion.6), kind=kCustom, calls=%fused_computation.1.clone.clone.1 | custom fusion | bytes 8388864 | tf_op jit(solution)/shard_map/while/body/eval_jaxpr/jit(_take)/gather | solution.py:116
  408.3 5.9 fusion.102
  419.0 10.5 %gather_fusion.1 = bf16[64,128,2,128]{3,2,1,0:T(2,128)(2,1)} fusion(bf16[4,128,2,128]{3,2,1,0:T(2,128)(2,1)S(1)} %get-tuple-element.275, s32[1024]{0:T(1024)S(1)} %pad_clamp_fusion.6), kind=kCustom, calls=%fused_computation.1.clone.clone.1 | custom fusion | bytes 8388864 | tf_op jit(solution)/shard_map/while/body/eval_jaxpr/jit(_take)/gather | solution.py:116
  429.5 5.9 fusion.102
  442.9 246.3 %all-reduce.2 = f32[128,2,2,8]{3,2,1,0:T(2,128)S(1)} all-reduce(f32[128,2,2,8]{3,2,1,0:T(2,128)S(1)} %copy.69), channel_id=3, replica_groups=mesh['dom'=64,'tp'=4] {'dom'}, use_global_device_ids=true, to_apply=%region_9.11.clone | all-reduce | flops 4096 | bytes 32768
  692.1 9.0 all-reduce.3
  701.1 131.0 %pmax.15 = f32[4]{0:T(128)S(1)} all-reduce(f32[4]{0:T(128)S(1)} %select_reduce_fusion.2), channel_id=1, replica_groups=mesh['dom'=64,'tp'=4] {'dom'}, use_global_device_ids=true, to_apply=%region_14.16 | all-reduce | flops 4 | bytes 32 | tf_op jit(solution)/shard_map/pmax | solution.py:181
  832.8 124.0 %psum.22 = f32[4]{0:T(128)S(1)} all-reduce(f32[4]{0:T(128)S(1)} %select_reduce_fusion.1), channel_id=1, replica_groups=mesh['dom'=64,'tp'=4] {'dom'}, use_global_device_ids=true, to_apply=%region_16.18 | all-reduce | flops 4 | bytes 32 | tf_op jit(solution)/shard_map/psum | solution.py:182
  (118 shorter events, 32.7 us)
Async XLA Ops:
  7.2 17.5 %copy-start.10 = (u32[256]{0:T(256)S(1)}, u32[256]{0:T(256)}, u32[]{:S(2)}) copy-start(u32[256]{0:T(256)} %constant.99) | copy-start | bytes 3076
  7.2 15.9 %copy-start.9 = (bf16[2,2,2,256]{3,2,1,0:T(2,128)(2,1)S(1)}, bf16[2,2,2,256]{3,2,1,0:T(2,128)(2,1)}, u32[]{:S(2)}) copy-start(bf16[2,2,2,256]{3,2,1,0:T(2,128)(2,1)} %param.17) | copy-start | bytes 12292
  7.2 16.2 %copy-start.11 = (s32[2]{0:T(128)S(1)}, s32[2]{0:T(128)}, u32[]{:S(2)}) copy-start(s32[2]{0:T(128)} %param.21) | copy-start | bytes 28
  7.2 18.7 %copy-start.12 = (s32[2]{0:T(128)S(1)}, s32[2]{0:T(128)}, u32[]{:S(2)}) copy-start(s32[2]{0:T(128)} %param.20) | copy-start | bytes 28
  7.2 96.8 %all-gather.2.cloned.1.call-start = ((), (), s32[]{:S(2)}) async-start(), calls=%async_computation | async-start | bytes 1064960 | tf_op jit(solution)/shard_map/all_gather | solution.py:142
  7.9 41.0 %collective-permute-start.2 = (bf16[2,2,256]{2,1,0:T(2,128)(2,1)S(1)}, bf16[2,2,256]{2,1,0:T(2,128)(2,1)S(1)}, u32[]{:S(2)}, u32[]{:S(2)}) collective-permute-start(bf16[2,2,256]{2,1,0:T(2,128)(2,1)S(1)} %slice_bitcast_fusion.10), channel_id=1, source_target_pairs={{0,4},{4,8},{8,12},{12,16},{16,20},{20,24},{24,28},{28,32},{32,36}... | collective-permute-start | bytes 6152 | tf_op jit(solution)/shard_map/ppermute | solution.py:19
  12.4 36.5 %collective-permute-start.3 = (bf16[2,2,256]{2,1,0:T(2,128)(2,1)S(1)}, bf16[2,2,256]{2,1,0:T(2,128)(2,1)S(1)}, u32[]{:S(2)}, u32[]{:S(2)}) collective-permute-start(bf16[2,2,256]{2,1,0:T(2,128)(2,1)S(1)} %slice_bitcast_fusion.10), channel_id=1, source_target_pairs={{4,0},{8,4},{12,8},{16,12},{20,16},{24,20},{28,24},{32,28},{36,32}... | collective-permute-start | bytes 6152 | tf_op jit(solution)/shard_map/ppermute | solution.py:22
  14.4 35.4 %collective-permute-start = (bf16[2,2,512,256]{3,2,1,0:T(8,128)(2,1)}, bf16[2,2,512,256]{3,2,1,0:T(8,128)(2,1)}, u32[]{:S(2)}, u32[]{:S(2)}) collective-permute-start(bf16[2,2,512,256]{3,2,1,0:T(8,128)(2,1)} %param.15), channel_id=1, source_target_pairs={{0,4},{4,8},{8,12},{12,16},{16,20},{20,24},{24,28},{28,32},{32,36}... | collective-permute-start | bytes 3145736 | tf_op jit(solution)/shard_map/ppermute | solution.py:19
  18.0 31.7 %collective-permute-start.1 = (bf16[2,2,512,256]{3,2,1,0:T(8,128)(2,1)}, bf16[2,2,512,256]{3,2,1,0:T(8,128)(2,1)}, u32[]{:S(2)}, u32[]{:S(2)}) collective-permute-start(bf16[2,2,512,256]{3,2,1,0:T(8,128)(2,1)} %param.15), channel_id=1, source_target_pairs={{4,0},{8,4},{12,8},{16,12},{20,16},{24,20},{28,24},{32,28},{36,32}... | collective-permute-start | bytes 3145736 | tf_op jit(solution)/shard_map/ppermute | solution.py:22
  20.0 670.0 %all-reduce.6.cloned.1.call-start = ((), (), s32[]{:S(2)}) async-start(), calls=%async_computation.1 | async-start | bytes 4194304
  49.6 3.4 copy-start.8
  117.1 8.0 copy-start.3
  140.1 8.0 copy-start.3
  396.9 0.9 copy-start.2
  415.2 1.6 copy-start
  416.5 1.7 copy-start.5
  416.9 1.3 copy-start.1
  436.4 1.6 copy-start
  437.7 1.7 copy-start.5
  438.1 1.3 copy-start.1
  440.2 2.6 copy-start.7
  440.2 249.8 %copy-start.13 = (f32[2048]{0:T(1024)S(1)}, f32[2048]{0:T(1024)}, u32[]{:S(2)}) copy-start(f32[2048]{0:T(1024)} %param.18) | copy-start | bytes 24580
  440.2 250.8 %copy-start.4 = (bf16[2,1,512,256]{2,3,0,1:T(8,128)(2,1)S(1)}, bf16[2,1,512,256]{2,3,0,1:T(8,128)(2,1)}, u32[]{:S(2)}) copy-start(bf16[2,1,512,256]{2,3,0,1:T(8,128)(2,1)} %copy.99) | copy-start | bytes 1572868
  441.5 259.5 %copy-start.14 = (f32[2]{0:T(128)S(1)}, f32[2]{0:T(128)}, u32[]{:S(2)}) copy-start(f32[2]{0:T(128)} %param.19) | copy-start | bytes 28
  (2 other events, 1.4 us)
Sparse Core Ops, SparseCore 0:
  20.1 83.8 all-gather.1
  440.3 190.6 all-reduce.5
where the time goes:
time: 965 us; the launch traced here: 964 us
  blocking collectives  775 us (80%)
  local copies, waits for them, and re-layouts  63.6 us (7%)
  waiting for transfers between devices  45.3 us (5%)
  other arithmetic  38.5 us (4%)
  between operations  15.7 us (2%)
  matrix products  14.6 us (2%)
  starting transfers between devices  12.1 us (1%)
    unnamed x2, blocking collectives  267 us
    pmax x1, blocking collectives, prefix_by_queries(): highest = lax.pmax(jnp.max(scores, axis=-1), 'dom')  243 us
    pmax x1, blocking collectives, body(): lax.pmax(jnp.max(jnp.where(table, raised[:, None], -1e+30), axis=0), 'dom')  131 us
    psum x1, blocking collectives, body(): lax.psum(jnp.sum(jnp.where(table, jnp.exp(raised[:, None] - prompt_top[No...  124 us
    all_gather x1, waiting for transfers between devices, prefix_by_queries(): lax.all_gather(queries, 'dom', axis=0, tiled=True)  45.2 us
    gather x2, local copies, waits for them, and re-layouts, score_block(): key_piece = jnp.take(key_table, id_piece, axis=0)  21 us
    gather x2, local copies, waits for them, and re-layouts, value_block(): value_piece = jnp.take(value_table, id_piece, axis=0)  21 us
  transfers between devices with their start and end apart: 6, of which 1 were waited for; matrix products, arithmetic and copies ran while one was open for 2% of the time, Pallas kernels for 0%

commit v1 on v0

v1 whole, which is shorter than its diff:
```python
import math

import jax
import jax.numpy as jnp
from jax import lax
from jax.experimental import pallas as pl
from jax.experimental.pallas import tpu as pltpu
from jax.sharding import Mesh
from jax.sharding import PartitionSpec as P

HEAD_DIM = 128
PROMPTS = 4
GROUP = 8
NZ, NX, NC, NT = 8, 4, 2, 4
RING = NZ * NX
DOM = ("z", "x", "core")
WIDE = ("z", "x", "core", "tp")
FACTOR = 1.0 / math.sqrt(HEAD_DIM)
FACTOR2 = FACTOR * math.log2(math.e)
Q_ROWS = 64
ID_ROWS = 16
BLOCK_ROWS = Q_ROWS + ID_ROWS
OUT_ROWS = 32
TAIL_ROWS = 16
CHUNK = 8
F32 = jnp.float32
BF16 = jnp.bfloat16
NT_DIMS = (((1,), (1,)), ((), ()))
VMEM = pl.BlockSpec(memory_space=pltpu.VMEM)
SMEM = pl.BlockSpec(memory_space=pltpu.SMEM)
PARAMS = pltpu.CompilerParams(vmem_limit_bytes=48 * 1024 * 1024)


def lanes(shape):
    return lax.broadcasted_iota(jnp.int32, shape, len(shape) - 1)


def prep_kernel(ids_ref, q_ref, out_ref, rows_ref):
    for p in range(2):
        both = q_ref[p].astype(F32)
        for s in range(2):
            for h in range(16):
                kv, g = divmod(h, GROUP)
                row = kv * 32 + p * 16 + s * 8 + g
                rows_ref[row : row + 1, :] = both[s : s + 1, h * 128 : (h + 1) * 128]
    for p in range(2):
        start = Q_ROWS + p * 8
        rows_ref[start : start + 8, :] = jnp.broadcast_to(ids_ref[p].astype(F32), (8, 128))
    block = rows_ref[...].astype(BF16)
    for i in range(RING):
        out_ref[i] = block


def prefix_kernel(q_ref, own_ref, other_ref, w_ref, out_ref):
    keys, values = [], []
    for kv in range(2):
        cols = slice(kv * 128, (kv + 1) * 128)
        for kind, into in ((0, keys), (1, values)):
            into.append(
                jnp.concatenate(
                    [
                        jnp.concatenate([own_ref[g, kind, :, cols], other_ref[g, kind, :, cols]], axis=0)
                        for g in range(PROMPTS)
                    ],
                    axis=1,
                )
            )
    count = CHUNK * 32
    row_id = lax.broadcasted_iota(jnp.int32, (CHUNK, 32, 128), 1)
    lane_id = lanes((CHUNK, 32, 128))
    tail_row = lax.broadcasted_iota(jnp.int32, (CHUNK, TAIL_ROWS, 128), 1)
    for start in range(0, RING, CHUNK):
        ids = q_ref[start : start + CHUNK, Q_ROWS:BLOCK_ROWS, :].astype(F32)
        ids = ids.reshape(CHUNK, 2, 1, 8, 128)
        ids = jnp.broadcast_to(ids, (CHUNK, 2, 2, 8, 128)).reshape(count, 128)
        picks = [ids == float(g) for g in range(PROMPTS)]
        outs, tops0, tops1, dots = [], [], [], []
        for kv in range(2):
            q = q_ref[start : start + CHUNK, kv * 32 : (kv + 1) * 32, :].astype(F32).reshape(count, 128)
            spread = jnp.concatenate([jnp.where(pick, q, 0.0).astype(BF16) for pick in picks], axis=1)
            scores = lax.dot_general(spread, keys[kv], NT_DIMS, preferred_element_type=F32)
            top = jnp.max(scores, axis=1, keepdims=True)
            weights = jnp.exp2((scores - top) * FACTOR2)
            total = jnp.sum(weights, axis=1, keepdims=True)
            sums = jnp.dot(weights.astype(BF16), values[kv], preferred_element_type=F32)
            num = sums[:, 384:512]
            for g in (2, 1, 0):
                num = jnp.where(picks[g], sums[:, g * 128 : (g + 1) * 128], num)
            mean = (num / total).reshape(CHUNK, 2, 2, 8, 128)
            level = (top * FACTOR + jnp.log(total)).reshape(CHUNK, 2, 2, 8, 1)
            w = w_ref[kv * 8 : (kv + 1) * 8, :].reshape(1, 1, 8, 128)
            dots.append(jnp.sum(mean[:, :, 0] * w, axis=-1, keepdims=True))
            tops0.append(level[:, :, 0])
            tops1.append(level[:, :, 1])
            outs.append(mean[:, :, 1])

        def merge(pair):
            width = pair[0].shape[-1]
            return jnp.stack(pair, axis=2).reshape(CHUNK, 32, width)

        out_ref[start : start + CHUNK, 0:OUT_ROWS, :] = merge(outs).astype(BF16)
        packed = jnp.where(lane_id == row_id, merge(tops1), 0.0)
        packed = jnp.where(lane_id == row_id + 32, merge(tops0), packed)
        packed = jnp.where(lane_id == row_id + 64, merge(dots), packed)
        flat = jnp.sum(packed, axis=1)
        high = flat.astype(BF16).astype(F32)
        rest = flat - high
        mid = rest.astype(BF16).astype(F32)
        low = rest - mid
        tail = jnp.where(tail_row == 0, high[:, None, :], 0.0)
        tail = jnp.where(tail_row == 1, mid[:, None, :], tail)
        tail = jnp.where(tail_row == 2, low[:, None, :], tail)
        out_ref[start : start + CHUNK, OUT_ROWS:, :] = tail.astype(BF16)


def local_attend(q, keys, values, fresh):
    q16 = q.astype(BF16)
    scores = lax.dot_general(q16, keys, NT_DIMS, preferred_element_type=F32)
    extra = [jnp.sum(q * k, axis=1, keepdims=True) for k, _ in fresh]
    top = jnp.max(scores, axis=1, keepdims=True)
    for e in extra:
        top = jnp.maximum(top, e)
    weights = jnp.exp2((scores - top) * FACTOR2)
    total = jnp.sum(weights, axis=1, keepdims=True)
    num = jnp.dot(weights.astype(BF16), values, preferred_element_type=F32)
    for e, (_, v) in zip(extra, fresh):
        weight = jnp.exp2((e - top) * FACTOR2)
        total = total + weight
        num = num + weight.astype(BF16).astype(F32) * v
    return num / total, top * FACTOR + jnp.log(total)


def finish_kernel(
    anc_ref, ids_ref, prior_ref, q_ref, part_ref, own_ref, pair_ref, far_ref, kv_ref, pair_kv_ref, far_kv_ref,
    w_ref, copied_ref, carried_ref, out_ref, send_ref,
):
    core = lax.axis_index("core")
    base = ((lax.axis_index("z") * NX + lax.axis_index("x")) * NC + core) * 2 - 2
    for slot in range(2):
        pos = anc_ref[slot] - base
        side, which = pos // 2, pos % 2
        from_own = side == 1
        from_pair = side == jnp.where(core == 0, 2, 0)
        from_far = side == jnp.where(core == 0, 0, 2)
        for j in range(2):
            for flag, cache, kvs in (
                (from_own, own_ref, kv_ref),
                (from_pair, pair_ref, pair_kv_ref),
                (from_far, far_ref, far_kv_ref),
            ):

                @pl.when(flag & (which == j))
                def _():
                    copied_ref[slot] = cache[j]
                    carried_ref[slot] = kvs[j, 0:2]

    queries = q_ref[0].astype(F32)
    step_kv = kv_ref[...].astype(F32)
    carried = carried_ref[...].astype(F32)
    outs0, outs1, tops0, tops1 = [], [], [], []
    for p in range(2):
        for kv in range(2):
            cols = slice(kv * 128, (kv + 1) * 128)
            row = kv * 32 + p * 16
            k0, v0 = step_kv[p, 0:1, cols], step_kv[p, 1:2, cols]
            k1, v1 = step_kv[p, 2:3, cols], step_kv[p, 3:4, cols]
            kc, vc = carried[p, 0:1, cols], carried[p, 1:2, cols]
            mean, level = local_attend(
                queries[row : row + 8], own_ref[p, 0, :, cols], own_ref[p, 1, :, cols], [(k0, v0)]
            )
            outs0.append(mean)
            tops0.append(level)
            mean, level = local_attend(
                queries[row + 8 : row + 16],
                copied_ref[p, 0, :, cols],
                copied_ref[p, 1, :, cols],
                [(kc, vc), (k1, v1)],
            )
            outs1.append(mean)
            tops1.append(level)
    w = w_ref[...]
    w_rows = jnp.concatenate([w, w], axis=0)
    mine0 = jnp.concatenate(outs0, axis=0)
    mine1 = jnp.concatenate(outs1, axis=0)
    top0 = jnp.concatenate(tops0, axis=0)
    top1 = jnp.concatenate(tops1, axis=0)
    dot0 = jnp.sum(mine0 * w_rows, axis=1, keepdims=True)
    row_id = lax.broadcasted_iota(jnp.int32, (32, 128), 0)
    lane_id = lanes((32, 128))
    packed = jnp.where(lane_id == row_id, top1, 0.0)
    packed = jnp.where(lane_id == row_id + 32, top0, packed)
    packed = jnp.where(lane_id == row_id + 64, dot0, packed)
    mine = jnp.sum(packed, axis=0, keepdims=True)
    theirs = jnp.sum(part_ref[:, OUT_ROWS:, :].astype(F32), axis=1)
    top = jnp.maximum(jnp.max(theirs, axis=0, keepdims=True), mine)
    scale = jnp.exp(theirs - top)
    my_scale = jnp.exp(mine - top)
    inverse = 1.0 / (jnp.sum(scale, axis=0, keepdims=True) + my_scale)
    scale = scale * inverse
    my_scale = my_scale * inverse
    aligned = pltpu.roll(theirs, 96, 1)
    my_aligned = pltpu.roll(jnp.broadcast_to(mine, (8, 128)), 96, 1)[0:1]
    first = jnp.sum(scale * aligned, axis=0, keepdims=True) + my_scale * my_aligned
    one = lanes((1, 128))
    twist0 = [
        jnp.sum(jnp.where((one >= 32 + 16 * p) & (one < 48 + 16 * p), first, 0.0), axis=1, keepdims=True)
        for p in range(2)
    ]
    table = jnp.concatenate([scale, jnp.broadcast_to(my_scale, (96, 128))], axis=0).T
    attn = mine1 * table[0:32, 32:33]
    for i in range(RING):
        attn = attn + table[0:32, i : i + 1] * part_ref[i, 0:OUT_ROWS, :].astype(F32)
    weighted = jnp.sum(attn * w_rows, axis=1, keepdims=True)
    twist1 = [jnp.sum(weighted[p * 16 : (p + 1) * 16], axis=0, keepdims=True) for p in range(2)]
    for p in range(2):
        for h in range(16):
            out_ref[p : p + 1, h * 128 : (h + 1) * 128] = attn[p * 16 + h : p * 16 + h + 1, :]
    line = jnp.where(one == 0, twist0[0], 0.0)
    line = jnp.where(one == 1, twist0[1], line)
    line = jnp.where(one == 2, twist1[0], line)
    line = jnp.where(one == 3, twist1[1], line)
    for p in range(2):
        line = jnp.where(one == 4 + p, prior_ref[p], line)
        line = jnp.where(one == 6 + p, ids_ref[p].astype(F32), line)
    send_ref[...] = jnp.broadcast_to(line, send_ref.shape)


def weight_kernel(ids_ref, all_ref, log_ref, twist_ref):
    dom = (lax.axis_index("z") * NX + lax.axis_index("x")) * NC + lax.axis_index("core")
    rows = all_ref[...]
    count = rows.shape[0]
    total = rows + pltpu.roll(rows, count - 1, 0)
    total = total + pltpu.roll(total, count - 2, 0)
    raised = total + pltpu.roll(rows, 124, 1)
    ids = pltpu.roll(rows, 122, 1)
    row_id = lax.broadcasted_iota(jnp.int32, rows.shape, 0)
    lane_id = lanes(rows.shape)
    valid = (row_id % NT == 0) & (lane_id < 2)
    for p in range(2):
        member = valid & (ids == ids_ref[p].astype(F32))
        top = jnp.max(jnp.where(member, raised, -1e30), keepdims=True)
        amount = jnp.sum(jnp.where(member, jnp.exp(raised - top), 0.0), keepdims=True)
        mine = jnp.sum(jnp.where((row_id == dom * NT) & (lane_id == p), raised, 0.0), keepdims=True)
        twist = jnp.sum(jnp.where((row_id == dom * NT) & (lane_id == 2 + p), total, 0.0), keepdims=True)
        value = mine - (jnp.log(amount) + top)
        log_ref[p] = value[0, 0]
        twist_ref[p] = twist[0, 0]


def body(
    prefix_cache, suffix_cache, queries, step_kv, twist_weight, prior_weights, prompt_ids, ancestors
):
    swap = [(0, 1), (1, 0)]
    cross = [(i, i + 1) for i in range(1, NZ * NX * NC - 1, 2)]
    cross = cross + [(b, a) for a, b in cross]
    first_kv = step_kv[:, 0]
    other_prefix = lax.ppermute(prefix_cache, "core", swap)
    pair_cache = lax.ppermute(suffix_cache, "core", swap)
    far_cache = lax.ppermute(suffix_cache, DOM, cross)
    pair_kv = lax.ppermute(first_kv, "core", swap)
    far_kv = lax.ppermute(first_kv, DOM, cross)
    weight_rows = twist_weight.reshape(16, 128)

    blocks = pl.pallas_call(
        prep_kernel,
        out_shape=jax.ShapeDtypeStruct((RING, BLOCK_ROWS, 128), BF16),
        in_specs=[SMEM, VMEM],
        out_specs=VMEM,
        scratch_shapes=[pltpu.VMEM((BLOCK_ROWS, 128), F32)],
        compiler_params=PARAMS,
        name="prep",
    )(prompt_ids, queries)
    gathered = lax.all_to_all(blocks, ("z", "x"), 0, 0, tiled=True)
    parts = pl.pallas_call(
        prefix_kernel,
        out_shape=jax.ShapeDtypeStruct((RING, OUT_ROWS + TAIL_ROWS, 128), BF16),
        in_specs=[VMEM] * 4,
        out_specs=VMEM,
        compiler_params=PARAMS,
        name="prefix",
    )(gathered, prefix_cache, other_prefix, weight_rows)
    received = lax.all_to_all(parts, ("z", "x"), 0, 0, tiled=True)
    copied, carried, attn, line = pl.pallas_call(
        finish_kernel,
        out_shape=(
            jax.ShapeDtypeStruct(suffix_cache.shape, BF16),
            jax.ShapeDtypeStruct(first_kv.shape, BF16),
            jax.ShapeDtypeStruct((2, 2048), F32),
            jax.ShapeDtypeStruct((NZ * NX * NC * NT, 128), F32),
        ),
        in_specs=[SMEM] * 3 + [VMEM] * 9,
        out_specs=(VMEM,) * 4,
        compiler_params=PARAMS,
        name="finish",
    )(
        ancestors, prompt_ids, prior_weights, blocks[0:1], received, suffix_cache, pair_cache, far_cache,
        step_kv.reshape(2, 4, 256), pair_kv, far_kv, weight_rows,
    )
    lines = lax.all_to_all(line, WIDE, 0, 0, tiled=True)
    log_weights, twist_two = pl.pallas_call(
        weight_kernel,
        out_shape=(jax.ShapeDtypeStruct((2,), F32), jax.ShapeDtypeStruct((2,), F32)),
        in_specs=[SMEM, VMEM],
        out_specs=(SMEM, SMEM),
        compiler_params=PARAMS,
        name="weights",
    )(prompt_ids, lines)
    return (log_weights, copied, carried, attn.astype(BF16), twist_two)


def solution(mesh):
    inner = Mesh(mesh.devices.reshape(NZ, NX, NC, NT), WIDE)
    placed = (
        P(None, None, DOM, "tp"),
        P(DOM, None, None, "tp"),
        P(DOM, None, "tp"),
        P(DOM, None, None, "tp"),
        P("tp"),
        P(DOM),
        P(DOM),
        P(DOM),
    )
    return jax.shard_map(
        body,
        mesh=inner,
        in_specs=placed,
        out_specs=(
            P(DOM),
            P(DOM, None, None, "tp"),
            P(DOM, None, "tp"),
            P(DOM, "tp"),
            P(DOM),
        ),
        check_vma=False,
    )
```

time: 965 us -> 89.1 us (0.09)
  blocking collectives: 775 us -> 0 us
  local copies, waits for them, and re-layouts: 63.6 us -> 4.08 us
  other arithmetic: 38.5 us -> 0.61 us
  starting transfers between devices: 12.1 us -> 40.2 us
  waiting for transfers between devices: 45.3 us -> 30.1 us
  between operations: 15.7 us -> 0.78 us
  matrix products: 14.6 us -> 0 us
  Pallas kernels: 0 us -> 12.9 us
    pmax x2 -> x0, blocking collectives: 374 us -> none  [the longest x1 243 us: prefix_by_queries(): highest = lax.pmax(jnp.max(scores, axis=-1), 'dom')]
    unnamed x2 -> x0, blocking collectives: 267 us -> none
    psum x2 -> x0, blocking collectives: 133 us -> none  [the longest x1 124 us: body(): lax.psum(jnp.sum(jnp.where(table, jnp.exp(raised[:, None] - prompt_top[No...]
    gather x6 -> x0, local copies, waits for them, and re-layouts: 46.1 us -> none  [the longest x2 21 us: score_block(): key_piece = jnp.take(key_table, id_piece, axis=0)]
    all_gather x1 -> x0, waiting for transfers between devices: 45.2 us -> none  [prefix_by_queries(): lax.all_gather(queries, 'dom', axis=0, tiled=True)]
    select_n x6 -> x0, other arithmetic: 30.2 us -> none  [the longest x2 15.9 us: score_block(): key_piece = jnp.take(key_table, id_piece, axis=0)]
    all_to_all x0 -> x3, starting transfers between devices: none -> 29.4 us  [the longest x1 12 us: body(): gathered = lax.all_to_all(blocks, ('z', 'x'), 0, 0, tiled=True)]
    all_to_all x0 -> x3, waiting for transfers between devices: none -> 29.4 us  [the longest x1 13 us: body(): gathered = lax.all_to_all(blocks, ('z', 'x'), 0, 0, tiled=True)]
  transfers between devices with their start and end apart: 6 -> 8, of which waited for: 1 -> 4; matrix products, arithmetic and copies ran while one was open for 2% -> 2% of each run, Pallas kernels for 0% -> 6%
where the time goes in v1:
time: 89.1 us; the launch traced here: 88.5 us
  starting transfers between devices  40.2 us (45%)
  waiting for transfers between devices  30.1 us (34%)
  Pallas kernels  12.9 us (14%)
  local copies, waits for them, and re-layouts  4.08 us (5%)
    all_to_all x1, waiting for transfers between devices, body(): gathered = lax.all_to_all(blocks, ('z', 'x'), 0, 0, tiled=True)  13 us
    all_to_all x1, waiting for transfers between devices, body(): lines = lax.all_to_all(line, WIDE, 0, 0, tiled=True)  12.1 us
    all_to_all x1, starting transfers between devices, body(): gathered = lax.all_to_all(blocks, ('z', 'x'), 0, 0, tiled=True)  12 us
    all_to_all x1, starting transfers between devices, body(): lines = lax.all_to_all(line, WIDE, 0, 0, tiled=True)  11.7 us
    ppermute x1, starting transfers between devices, body(): far_kv = lax.ppermute(first_kv, DOM, cross)  5.83 us
    all_to_all x1, starting transfers between devices, body(): received = lax.all_to_all(parts, ('z', 'x'), 0, 0, tiled=True)  5.65 us
    pallas_call x1, Pallas kernels, body(): pl.pallas_call(prefix_kernel, out_shape=jax.ShapeDtypeStruct((RING, OUT_R...  5.04 us
    pallas_call x1, Pallas kernels, body(): pl.pallas_call(finish_kernel, out_shape=(jax.ShapeDtypeStruct(suffix_cach...  4.63 us
  transfers between devices with their start and end apart: 8, of which 4 were waited for; matrix products, arithmetic and copies ran while one was open for 2% of the time, Pallas kernels for 6%

profile of v1, /device:TPU:1, one launch (start us, length us, event | category | flops | bytes accessed | tf_op | source)
XLA Modules:
  0.0 88.5 jit_solution(10802410856144985860)
XLA Ops:
  0.7 0.8 copy-done.5
  1.4 0.7 copy-done.6
  2.1 1.4 %prep.1 = bf16[32,80,128]{2,1,0:T(8,128)(2,1)} custom-call(s32[2]{0:T(128)S(1)} %copy-done.6, bf16[2,2,2048]{2,1,0:T(2,128)(2,1)S(1)} %copy-done.5), custom_call_target="tpu_custom_call" | custom-call | tf_op jit(solution)/shard_map/prep/pallas_call | solution.py:264
  3.5 12.0 %all-to-all-start = ((bf16[32,80,128]{2,1,0:T(8,128)(2,1)}), bf16[32,80,128]{2,1,0:T(8,128)(2,1)S(1)}, u32[]{:S(2)}, u32[]{:S(2)}) async-start(bf16[32,80,128]{2,1,0:T(8,128)(2,1)} %prep.1), calls=%async_computation | async-start | bytes 1310720 | tf_op jit(solution)/shard_map/all_to_all | solution.py:273
  15.6 1.0 %collective-permute-start = (bf16[4,2,128,256]{3,2,1,0:T(8,128)(2,1)S(1)}, bf16[4,2,128,256]{3,2,1,0:T(8,128)(2,1)S(1)}, u32[]{:S(2)}, u32[]{:S(2)}) collective-permute-start(bf16[4,2,128,256]{3,2,1,0:T(8,128)(2,1)S(1)} %copy-done.1), channel_id=1, source_target_pairs={{0,4},{4,0},{1,5},{5,1},{2,6},{6,2},{3,7},{7,3},{8,12},{12,8},{9,1... | collective-permute-start | bytes 1572872 | tf_op jit(solution)/shard_map/ppermute | solution.py:257
  16.6 0.1 collective-permute-start.1
  16.7 3.7 %collective-permute-start.2 = (bf16[2,2,512,256]{3,2,1,0:T(8,128)(2,1)S(1)}, bf16[2,2,512,256]{3,2,1,0:T(8,128)(2,1)}, u32[]{:S(2)}, u32[]{:S(2)}) collective-permute-start(bf16[2,2,512,256]{3,2,1,0:T(8,128)(2,1)S(1)} %copy-done), channel_id=1, source_target_pairs={{4,8},{12,16},{20,24},{28,32},{36,40},{44,48},{52,56},{60,64},{68,... | collective-permute-start | bytes 3145736 | tf_op jit(solution)/shard_map/ppermute | solution.py:259
  20.4 0.8 copy-done.2
  21.2 13.0 %all-to-all-done.q_ref = bf16[32,80,128]{2,1,0:T(8,128)(2,1)S(1)} async-done(((bf16[32,80,128]{2,1,0:T(8,128)(2,1)}), bf16[32,80,128]{2,1,0:T(8,128)(2,1)S(1)}, u32[]{:S(2)}, u32[]{:S(2)}) %all-to-all-start) | async-done | bytes 655392 | tf_op jit(solution)/shard_map/all_to_all | solution.py:273
  34.3 1.0 %copy-done.3 = bf16[4,2,128,256]{3,2,1,0:T(8,128)(2,1)S(1)} copy-done((bf16[4,2,128,256]{3,2,1,0:T(8,128)(2,1)S(1)}, bf16[4,2,128,256]{3,2,1,0:T(8,128)(2,1)}, u32[]{:S(2)}) %copy-start.3) | copy-done | bytes 524312
  35.3 5.0 %prefix.1 = bf16[32,48,128]{2,1,0:T(8,128)(2,1)} custom-call(bf16[32,80,128]{2,1,0:T(8,128)(2,1)S(1)} %all-to-all-done.q_ref, bf16[4,2,128,256]{3,2,1,0:T(8,128)(2,1)S(1)} %copy-done.1, bf16[4,2,128,256]{3,2,1,0:T(8,128)(2,1)S(1)} %copy-done.3, f32[16,128]{1,0:T(8,128)S(1)} %bitcast.10), custom_call_target="tpu_custom_call" | custom-call | tf_op jit(solution)/shard_map/prefix/pallas_call | solution.py:274
  40.3 5.7 %all-to-all-start.1 = ((bf16[32,48,128]{2,1,0:T(8,128)(2,1)}), bf16[32,48,128]{2,1,0:T(8,128)(2,1)S(1)}, u32[]{:S(2)}, u32[]{:S(2)}) async-start(bf16[32,48,128]{2,1,0:T(8,128)(2,1)} %prefix.1), calls=%async_computation.1 | async-start | bytes 786432 | tf_op jit(solution)/shard_map/all_to_all | solution.py:282
  46.0 5.8 %collective-permute-start.4 = (bf16[2,2,256]{2,1,0:T(2,128)(2,1)S(1)}, bf16[2,2,256]{2,1,0:T(2,128)(2,1)S(1)}, u32[]{:S(2)}, u32[]{:S(2)}) collective-permute-start(bf16[2,2,256]{2,1,0:T(2,128)(2,1)S(1)} %slice_bitcast_fusion), channel_id=1, source_target_pairs={{4,8},{12,16},{20,24},{28,32},{36,40},{44,48},{52,56},{60,64},{68,... | collective-permute-start | bytes 6152 | tf_op jit(solution)/shard_map/ppermute | solution.py:261
  51.9 0.1 collective-permute-start.3
  52.0 0.0 copy-start.7
  52.0 0.0 copy-start.9
  52.0 0.7 slice.8.q_ref
  52.8 0.7 collective-permute-done.4.far_kv_ref
  53.4 4.2 %all-to-all-done.1.part_ref = bf16[32,48,128]{2,1,0:T(8,128)(2,1)S(1)} async-done(((bf16[32,48,128]{2,1,0:T(8,128)(2,1)}), bf16[32,48,128]{2,1,0:T(8,128)(2,1)S(1)}, u32[]{:S(2)}, u32[]{:S(2)}) %all-to-all-start.1) | async-done | bytes 393248 | tf_op jit(solution)/shard_map/all_to_all | solution.py:282
  57.7 4.6 %finish.1 = (bf16[2,2,512,256]{3,2,1,0:T(8,128)(2,1)}, bf16[2,2,256]{2,1,0:T(2,128)(2,1)}, f32[2,2048]{1,0:T(2,128)S(1)}, f32[256,128]{1,0:T(8,128)}) custom-call(s32[2]{0:T(128)S(1)} %copy-done.8, s32[2]{0:T(128)S(1)} %copy-done.7, f32[2]{0:T(128)S(1)} %copy-done.9, bf16[1,80,128]{2,1,0:T(8,128)(2,1)S(1)} %slice.8.q_ref, ...), custom_call_target="tpu_custom_call" | custom-call | tf_op jit(solution)/shard_map/finish/pallas_call | solution.py:283
  62.3 11.7 %all-to-all-start.2 = ((f32[256,1,128]{2,1,0:T(1,128)}), f32[256,1,128]{2,1,0:T(1,128)S(1)}, u32[]{:S(2)}, u32[]{:S(2)}) async-start(f32[256,1,128]{2,1,0:T(1,128)} %bitcast.3), calls=%async_computation.2 | async-start | bytes 262144 | tf_op jit(solution)/shard_map/all_to_all | solution.py:299
  74.1 0.6 convert_element_type.3
  74.7 12.1 %all-to-all-done.2 = f32[256,1,128]{2,1,0:T(1,128)S(1)} async-done(((f32[256,1,128]{2,1,0:T(1,128)}), f32[256,1,128]{2,1,0:T(1,128)S(1)}, u32[]{:S(2)}, u32[]{:S(2)}) %all-to-all-start.2) | async-done | bytes 131104 | tf_op jit(solution)/shard_map/all_to_all | solution.py:299
  86.8 1.7 %weights.1 = (f32[2]{0:T(128)}, f32[2]{0:T(128)}) custom-call(s32[2]{0:T(128)S(1)} %copy-done.7, f32[256,128]{1,0:T(8,128)S(1)} %bitcast.9), custom_call_target="tpu_custom_call" | custom-call | tf_op jit(solution)/shard_map/weights/pallas_call | solution.py:300
  (22 shorter events, 0.1 us)
Async XLA Ops:
  0.6 16.0 %copy-start = (bf16[2,2,512,256]{3,2,1,0:T(8,128)(2,1)S(1)}, bf16[2,2,512,256]{3,2,1,0:T(8,128)(2,1)}, u32[]{:S(2)}) copy-start(bf16[2,2,512,256]{3,2,1,0:T(8,128)(2,1)} %own_ref.3) | copy-start | bytes 3145732
  0.6 0.8 copy-start.5
  1.4 0.7 copy-start.6
  3.5 12.0 %copy-start.1 = (bf16[4,2,128,256]{3,2,1,0:T(8,128)(2,1)S(1)}, bf16[4,2,128,256]{3,2,1,0:T(8,128)(2,1)}, u32[]{:S(2)}) copy-start(bf16[4,2,128,256]{3,2,1,0:T(8,128)(2,1)} %own_ref.2) | copy-start | bytes 1572868
  3.5 30.7 %copy-start.4 = (f32[2048]{0:T(1024)S(1)}, f32[2048]{0:T(1024)}, u32[]{:S(2)}) copy-start(f32[2048]{0:T(1024)} %param.12) | copy-start | bytes 24580
  3.5 30.7 %all-to-all-start = ((bf16[32,80,128]{2,1,0:T(8,128)(2,1)}), bf16[32,80,128]{2,1,0:T(8,128)(2,1)S(1)}, u32[]{:S(2)}, u32[]{:S(2)}) async-start(bf16[32,80,128]{2,1,0:T(8,128)(2,1)} %prep.1), calls=%async_computation | async-start | bytes 1310720 | tf_op jit(solution)/shard_map/all_to_all | solution.py:273
  15.6 4.9 %collective-permute-start = (bf16[4,2,128,256]{3,2,1,0:T(8,128)(2,1)S(1)}, bf16[4,2,128,256]{3,2,1,0:T(8,128)(2,1)S(1)}, u32[]{:S(2)}, u32[]{:S(2)}) collective-permute-start(bf16[4,2,128,256]{3,2,1,0:T(8,128)(2,1)S(1)} %copy-done.1), channel_id=1, source_target_pairs={{0,4},{4,0},{1,5},{5,1},{2,6},{6,2},{3,7},{7,3},{8,12},{12,8},{9,1... | collective-permute-start | bytes 1572872 | tf_op jit(solution)/shard_map/ppermute | solution.py:257
  16.6 36.8 %collective-permute-start.1 = (bf16[2,2,512,256]{3,2,1,0:T(8,128)(2,1)S(1)}, bf16[2,2,512,256]{3,2,1,0:T(8,128)(2,1)S(1)}, u32[]{:S(2)}, u32[]{:S(2)}) collective-permute-start(bf16[2,2,512,256]{3,2,1,0:T(8,128)(2,1)S(1)} %copy-done), channel_id=1, source_target_pairs={{0,4},{4,0},{1,5},{5,1},{2,6},{6,2},{3,7},{7,3},{8,12},{12,8},{9,1... | collective-permute-start | bytes 3145736 | tf_op jit(solution)/shard_map/ppermute | solution.py:258
  16.7 36.7 %collective-permute-start.2 = (bf16[2,2,512,256]{3,2,1,0:T(8,128)(2,1)S(1)}, bf16[2,2,512,256]{3,2,1,0:T(8,128)(2,1)}, u32[]{:S(2)}, u32[]{:S(2)}) collective-permute-start(bf16[2,2,512,256]{3,2,1,0:T(8,128)(2,1)S(1)} %copy-done), channel_id=1, source_target_pairs={{4,8},{12,16},{20,24},{28,32},{36,40},{44,48},{52,56},{60,64},{68,... | collective-permute-start | bytes 3145736 | tf_op jit(solution)/shard_map/ppermute | solution.py:259
  20.4 0.8 copy-start.2
  34.3 1.0 %copy-start.3 = (bf16[4,2,128,256]{3,2,1,0:T(8,128)(2,1)S(1)}, bf16[4,2,128,256]{3,2,1,0:T(8,128)(2,1)}, u32[]{:S(2)}) copy-start(bf16[4,2,128,256]{3,2,1,0:T(8,128)(2,1)} %copy-done.2) | copy-start | bytes 1572868
  40.3 5.7 %copy-start.10 = (bf16[2,2,2,256]{3,2,1,0:T(2,128)(2,1)S(1)}, bf16[2,2,2,256]{3,2,1,0:T(2,128)(2,1)}, u32[]{:S(2)}) copy-start(bf16[2,2,2,256]{3,2,1,0:T(2,128)(2,1)} %param.11) | copy-start | bytes 12292
  40.3 17.3 %all-to-all-start.1 = ((bf16[32,48,128]{2,1,0:T(8,128)(2,1)}), bf16[32,48,128]{2,1,0:T(8,128)(2,1)S(1)}, u32[]{:S(2)}, u32[]{:S(2)}) async-start(bf16[32,48,128]{2,1,0:T(8,128)(2,1)} %prefix.1), calls=%async_computation.1 | async-start | bytes 786432 | tf_op jit(solution)/shard_map/all_to_all | solution.py:282
  46.0 7.4 %collective-permute-start.4 = (bf16[2,2,256]{2,1,0:T(2,128)(2,1)S(1)}, bf16[2,2,256]{2,1,0:T(2,128)(2,1)S(1)}, u32[]{:S(2)}, u32[]{:S(2)}) collective-permute-start(bf16[2,2,256]{2,1,0:T(2,128)(2,1)S(1)} %slice_bitcast_fusion), channel_id=1, source_target_pairs={{4,8},{12,16},{20,24},{28,32},{36,40},{44,48},{52,56},{60,64},{68,... | collective-permute-start | bytes 6152 | tf_op jit(solution)/shard_map/ppermute | solution.py:261
  51.9 1.6 %collective-permute-start.3 = (bf16[2,2,256]{2,1,0:T(2,128)(2,1)S(1)}, bf16[2,2,256]{2,1,0:T(2,128)(2,1)S(1)}, u32[]{:S(2)}, u32[]{:S(2)}) collective-permute-start(bf16[2,2,256]{2,1,0:T(2,128)(2,1)S(1)} %slice_bitcast_fusion), channel_id=1, source_target_pairs={{0,4},{4,0},{1,5},{5,1},{2,6},{6,2},{3,7},{7,3},{8,12},{12,8},{9,1... | collective-permute-start | bytes 6152 | tf_op jit(solution)/shard_map/ppermute | solution.py:260
  52.0 5.7 %copy-start.7 = (s32[2]{0:T(128)S(1)}, s32[2]{0:T(128)}, u32[]{:S(2)}) copy-start(s32[2]{0:T(128)} %ids_ref.5) | copy-start | bytes 28
  52.0 5.7 %copy-start.8 = (s32[2]{0:T(128)S(1)}, s32[2]{0:T(128)}, u32[]{:S(2)}) copy-start(s32[2]{0:T(128)} %anc_ref.1) | copy-start | bytes 28
  52.0 5.7 %copy-start.9 = (f32[2]{0:T(128)S(1)}, f32[2]{0:T(128)}, u32[]{:S(2)}) copy-start(f32[2]{0:T(128)} %prior_ref.1) | copy-start | bytes 28
  62.3 24.5 %all-to-all-start.2 = ((f32[256,1,128]{2,1,0:T(1,128)}), f32[256,1,128]{2,1,0:T(1,128)S(1)}, u32[]{:S(2)}, u32[]{:S(2)}) async-start(f32[256,1,128]{2,1,0:T(1,128)} %bitcast.3), calls=%async_computation.2 | async-start | bytes 262144 | tf_op jit(solution)/shard_map/all_to_all | solution.py:299

commit v2 on v1

v2 whole, which is shorter than its diff:
```python
import math

import jax
import jax.numpy as jnp
from jax import lax
from jax.experimental import pallas as pl
from jax.experimental.pallas import tpu as pltpu
from jax.sharding import Mesh
from jax.sharding import PartitionSpec as P

HEAD_DIM = 128
PROMPTS = 4
GROUP = 8
NZ, NX, NC, NT = 8, 4, 2, 4
RING = NZ * NX
DOM = ("z", "x1", "x0", "core")
WIDE = ("z", "x1", "x0", "core", "tp")
PEERS = ("x0", "x1", "z")
FACTOR = 1.0 / math.sqrt(HEAD_DIM)
FACTOR2 = FACTOR * math.log2(math.e)
Q_ROWS = 64
ID_ROWS = 8
BLOCK_ROWS = Q_ROWS + ID_ROWS
OUT_ROWS = 32
PART_ROWS = OUT_ROWS + 40
CHUNK = 8
F32 = jnp.float32
BF16 = jnp.bfloat16
NT_DIMS = (((1,), (1,)), ((), ()))
VMEM = pl.BlockSpec(memory_space=pltpu.VMEM)
SMEM = pl.BlockSpec(memory_space=pltpu.SMEM)
LONG = pl.CostEstimate(flops=2 * 10**10, bytes_accessed=8 * 10**7, transcendentals=0)
PARAMS = pltpu.CompilerParams(vmem_limit_bytes=48 * 1024 * 1024)


def lanes(shape):
    return lax.broadcasted_iota(jnp.int32, shape, len(shape) - 1)


def ring_place():
    return (lax.axis_index("x0") * 2 + lax.axis_index("x1")) * NZ + lax.axis_index("z")


def prep_kernel(ids_ref, q_ref, out_ref, rows_ref):
    for p in range(2):
        both = q_ref[p].astype(F32)
        for s in range(2):
            for h in range(16):
                kv, g = divmod(h, GROUP)
                row = kv * 32 + p * 16 + s * 8 + g
                rows_ref[row : row + 1, :] = both[s : s + 1, h * 128 : (h + 1) * 128]
    first, second = ids_ref[0].astype(F32), ids_ref[1].astype(F32)
    rows_ref[Q_ROWS:BLOCK_ROWS, :] = jnp.where(lanes((ID_ROWS, 128)) < 64, first, second)
    block = rows_ref[...].astype(BF16)
    for i in range(RING):
        out_ref[i] = block


def prefix_kernel(ids_ref, prior_ref, q_ref, own_ref, other_ref, w_ref, level_ref, dot_ref, out_ref):
    keys, values = [], []
    for kv in range(2):
        cols = slice(kv * 128, (kv + 1) * 128)
        for kind, into in ((0, keys), (1, values)):
            into.append(
                jnp.concatenate(
                    [
                        jnp.concatenate([own_ref[g, kind, :, cols], other_ref[g, kind, :, cols]], axis=0)
                        for g in range(PROMPTS)
                    ],
                    axis=1,
                )
            )
    count = CHUNK * 32
    shape = (CHUNK, 32, 128)
    row_id = lax.broadcasted_iota(jnp.int32, shape, 1)
    lane_id = lanes(shape)
    spot = row_id + 32 * (lax.broadcasted_iota(jnp.int32, shape, 0) % 4)
    levels, dots, heads, bodies = [], [], [], []
    head_row = lax.broadcasted_iota(jnp.int32, (CHUNK, 8, 128), 1)
    place = ring_place()
    one = lanes((1, 128))
    prior = jnp.zeros((1, 128), F32)
    ids_row = jnp.zeros((1, 128), F32)
    for p in range(2):
        here = one // 16 == (place % 4) * 2 + p
        prior = jnp.where(here, prior_ref[p], prior)
        ids_row = jnp.where(here, ids_ref[p].astype(F32), ids_row)
    prior_parts = split(prior)
    for start in range(0, RING, CHUNK):
        block = q_ref[start : start + CHUNK].astype(F32)
        both = block[:, Q_ROWS:BLOCK_ROWS].reshape(CHUNK * ID_ROWS, 128)
        turned = pltpu.roll(both, 64, 1)
        left = lanes(both.shape) < 64
        ids = jnp.stack(
            [
                jnp.where(left, both, turned).reshape(CHUNK, 1, ID_ROWS, 128),
                jnp.where(left, turned, both).reshape(CHUNK, 1, ID_ROWS, 128),
            ],
            axis=1,
        )
        ids = jnp.broadcast_to(ids, (CHUNK, 2, 2, 8, 128)).reshape(count, 128)
        picks = [ids == float(g) for g in range(PROMPTS)]
        means, tops0, tops1, firsts = [], [], [], []
        for kv in range(2):
            q = block[:, kv * 32 : (kv + 1) * 32].reshape(count, 128)
            spread = jnp.concatenate([jnp.where(pick, q, 0.0).astype(BF16) for pick in picks], axis=1)
            scores = lax.dot_general(spread, keys[kv], NT_DIMS, preferred_element_type=F32)
            top = jnp.max(scores, axis=1, keepdims=True)
            weights = jnp.exp2((scores - top) * FACTOR2)
            total = jnp.sum(weights, axis=1, keepdims=True)
            sums = jnp.dot(weights.astype(BF16), values[kv], preferred_element_type=F32)
            num = sums[:, 384:512]
            for g in (2, 1, 0):
                num = jnp.where(picks[g], sums[:, g * 128 : (g + 1) * 128], num)
            mean = (num / total).reshape(CHUNK, 2, 2, 8, 128)
            level = (top * FACTOR + jnp.log(total)).reshape(CHUNK, 2, 2, 8, 1)
            w = w_ref[kv * 8 : (kv + 1) * 8, :].reshape(1, 1, 8, 128)
            firsts.append(jnp.sum(mean[:, :, 0] * w, axis=-1, keepdims=True))
            tops0.append(level[:, :, 0])
            tops1.append(level[:, :, 1])
            means.append(mean[:, :, 1])

        def merge(pair):
            return jnp.stack(pair, axis=2).reshape(CHUNK, 32, pair[0].shape[-1])

        def pack(pair):
            wide = jnp.where(lane_id == spot, merge(pair), 0.0)
            return jnp.sum(wide.reshape(CHUNK // 4, 128, 128), axis=1)

        bodies.append(merge(means))
        levels.append(pack(tops0))
        dots.append(pack(firsts))
        high, mid, low = split(jnp.sum(jnp.where(lane_id == row_id, merge(tops1), 0.0), axis=1))
        line = high + pltpu.roll(mid, 32, 1) + pltpu.roll(low, 64, 1)
        head = jnp.where(head_row == 0, line[:, None, :], 0.0)
        for r, row in enumerate((*prior_parts, ids_row)):
            head = jnp.where(head_row == r + 1, row[None], head)
        heads.append(head)
    level, dot = jnp.concatenate(levels, axis=0), jnp.concatenate(dots, axis=0)
    top = jnp.maximum(level, level_ref[...])
    old, new = jnp.exp(level - top), jnp.exp(level_ref[...] - top)
    dot = (dot * old + dot_ref[...] * new) / (old + new)
    level = top + jnp.log(old + new)
    for start, mean, head in zip(range(0, RING, CHUNK), bodies, heads):
        common = jnp.broadcast_to(jnp.concatenate([*split(level), dot], axis=0)[None], (CHUNK, 32, 128))
        out_ref[start : start + CHUNK] = jnp.concatenate([mean, head, common], axis=1).astype(BF16)


def split(value):
    high = value.astype(BF16).astype(F32)
    rest = value - high
    mid = rest.astype(BF16).astype(F32)
    return high, mid, rest - mid


def local_attend(q, keys, values, fresh):
    q16 = q.astype(BF16)
    scores = lax.dot_general(q16, keys, NT_DIMS, preferred_element_type=F32)
    extra = [jnp.sum(q * k, axis=1, keepdims=True) for k, _ in fresh]
    top = jnp.max(scores, axis=1, keepdims=True)
    for e in extra:
        top = jnp.maximum(top, e)
    weights = jnp.exp2((scores - top) * FACTOR2)
    total = jnp.sum(weights, axis=1, keepdims=True)
    num = jnp.dot(weights.astype(BF16), values, preferred_element_type=F32)
    for e, (_, v) in zip(extra, fresh):
        weight = jnp.exp2((e - top) * FACTOR2)
        total = total + weight
        num = num + weight.astype(BF16).astype(F32) * v
    return num / total, top * FACTOR + jnp.log(total)


def first_kernel(q_ref, own_ref, kv_ref, w_ref, level_ref, dot_ref):
    queries = q_ref[0].astype(F32)
    step_kv = kv_ref[...].astype(F32)
    means, tops = [], []
    for p in range(2):
        for kv in range(2):
            cols = slice(kv * 128, (kv + 1) * 128)
            row = kv * 32 + p * 16
            mean, top = local_attend(
                queries[row : row + 8],
                own_ref[p, 0, :, cols],
                own_ref[p, 1, :, cols],
                [(step_kv[p, 0:1, cols], step_kv[p, 1:2, cols])],
            )
            means.append(mean)
            tops.append(top)
    w = w_ref[...]
    dot = jnp.sum(jnp.concatenate(means, axis=0) * jnp.concatenate([w, w], axis=0), axis=1, keepdims=True)
    top = jnp.concatenate(tops, axis=0)
    place = ring_place()
    spot = lax.broadcasted_iota(jnp.int32, (32, 128), 0) + 32 * (place % 4)
    lane_id = lanes((32, 128))
    level_row = jnp.sum(jnp.where(lane_id == spot, top, 0.0), axis=0, keepdims=True)
    dot_row = jnp.sum(jnp.where(lane_id == spot, dot, 0.0), axis=0, keepdims=True)
    here = (lax.broadcasted_iota(jnp.int32, (8, 128), 0) == place // 4) & (lanes((8, 128)) // 32 == place % 4)
    level_ref[...] = jnp.where(here, level_row, -1e30)
    dot_ref[...] = jnp.where(here, dot_row, 0.0)


def second_kernel(
    anc_ref, q_ref, own_ref, pair_ref, far_ref, kv_ref, pair_kv_ref, far_kv_ref,
    copied_ref, carried_ref, mean_ref, level_ref,
):
    core = lax.axis_index("core")
    base = lax.axis_index("z") * NX + lax.axis_index("x1") * 2 + lax.axis_index("x0")
    base = (base * NC + core) * 2 - 2
    for slot in range(2):
        pos = anc_ref[slot] - base
        side, which = pos // 2, pos % 2
        from_own = side == 1
        from_pair = side == jnp.where(core == 0, 2, 0)
        from_far = side == jnp.where(core == 0, 0, 2)
        for j in range(2):
            for flag, cache, kvs in (
                (from_own, own_ref, kv_ref),
                (from_pair, pair_ref, pair_kv_ref),
                (from_far, far_ref, far_kv_ref),
            ):

                @pl.when(flag & (which == j))
                def _():
                    copied_ref[slot] = cache[j]
                    carried_ref[slot] = kvs[j, 0:2]

    queries = q_ref[0].astype(F32)
    step_kv = kv_ref[...].astype(F32)
    carried = carried_ref[...].astype(F32)
    tops = []
    for p in range(2):
        for kv in range(2):
            cols = slice(kv * 128, (kv + 1) * 128)
            row = kv * 32 + p * 16 + 8
            mean, top = local_attend(
                queries[row : row + 8],
                copied_ref[p, 0, :, cols],
                copied_ref[p, 1, :, cols],
                [
                    (carried[p, 0:1, cols], carried[p, 1:2, cols]),
                    (step_kv[p, 2:3, cols], step_kv[p, 3:4, cols]),
                ],
            )
            mean_ref[p * 16 + kv * 8 : p * 16 + kv * 8 + 8, :] = mean
            tops.append(top)
    top = jnp.concatenate(tops, axis=0)
    row_id = lax.broadcasted_iota(jnp.int32, (32, 128), 0)
    row = jnp.sum(jnp.where(lanes((32, 128)) == row_id, top, 0.0), axis=0, keepdims=True)
    level_ref[...] = jnp.broadcast_to(row, (8, 128))


def finish_kernel(part_ref, mean_ref, level_ref, w_ref, out_ref, send_ref):
    parts = part_ref[...].astype(F32)
    heads = parts[:, OUT_ROWS : OUT_ROWS + 8]
    head_row = lax.broadcasted_iota(jnp.int32, heads.shape, 1)
    theirs = jnp.sum(jnp.where(head_row == 0, heads, 0.0), axis=1)
    theirs = theirs + pltpu.roll(theirs, 96, 1) + pltpu.roll(theirs, 64, 1)
    mine = level_ref[0:1, :]
    top = jnp.maximum(jnp.max(theirs, axis=0, keepdims=True), mine)
    scale = jnp.exp(theirs - top)
    my_scale = jnp.exp(mine - top)
    inverse = 1.0 / (jnp.sum(scale, axis=0, keepdims=True) + my_scale)
    table = jnp.concatenate([scale * inverse, jnp.broadcast_to(my_scale * inverse, (96, 128))], axis=0).T
    attn = mean_ref[...] * table[0:32, 32:33]
    for i in range(RING):
        attn = attn + table[0:32, i : i + 1] * parts[i, 0:OUT_ROWS]
    w = w_ref[...]
    weighted = jnp.sum(attn * jnp.concatenate([w, w], axis=0), axis=1, keepdims=True)
    for p in range(2):
        for h in range(16):
            out_ref[p : p + 1, h * 128 : (h + 1) * 128] = attn[p * 16 + h : p * 16 + h + 1, :]

    high, mid, low, dot = (parts[:, OUT_ROWS + 8 * t : OUT_ROWS + 8 * (t + 1)] for t in (1, 2, 3, 4))
    level = high + mid + low
    top = jnp.max(level, axis=0)
    scale = jnp.exp(level - top[None])
    twist = jnp.sum(scale * dot, axis=0) / jnp.sum(scale, axis=0)
    for shift in (8, 4, 2, 1):
        twist = twist + pltpu.roll(twist, 128 - shift, 1)
    facts = jnp.sum(heads.reshape(8, 4, 8, 128), axis=1)
    fact_row = lax.broadcasted_iota(jnp.int32, facts.shape, 1)
    prior = jnp.sum(jnp.where((fact_row >= 1) & (fact_row <= 3), facts, 0.0), axis=1)
    ids = jnp.sum(jnp.where(fact_row == 4, facts, 0.0), axis=1)
    kind = lanes((8, 128)) % 16
    line = jnp.where(kind == 0, twist, jnp.where(kind == 1, prior, jnp.where(kind == 2, ids, 0.0)))
    one = lanes((8, 128))
    second = jnp.zeros((8, 128), F32)
    for p in range(2):
        part = jnp.sum(weighted[p * 16 : (p + 1) * 16], axis=0, keepdims=True)
        second = jnp.where(one == p, part, second)
    block = jnp.concatenate([line, second], axis=0)
    for i in range(NC * NT):
        send_ref[i] = block


def weight_kernel(ids_ref, all_ref, log_ref, twist_ref):
    core = lax.axis_index("core")
    place = ring_place()
    kind = lanes((8, 128)) % 16
    raised, ids, seconds = [], [], []
    for c in range(NC):
        rows = [all_ref[c * NT + t] for t in range(NT)]
        total = rows[0] + rows[1] + rows[2] + rows[3]
        raised.append(total[0:8] + pltpu.roll(rows[0][0:8], 127, 1))
        ids.append(pltpu.roll(rows[0][0:8], 126, 1))
        seconds.append(total[8:16])
    own = jnp.where(core == 0, raised[0], raised[1])
    second = jnp.where(core == 0, seconds[0], seconds[1])
    row_id = lax.broadcasted_iota(jnp.int32, (8, 128), 0)
    lane_id = lanes((8, 128))
    for p in range(2):
        me = ids_ref[p].astype(F32)
        members = [(kind == 0) & (i == me) for i in ids]
        masked = [jnp.where(m, r, -1e30) for m, r in zip(members, raised)]
        top = jnp.max(jnp.maximum(masked[0], masked[1]), keepdims=True)
        shares = [jnp.where(m, jnp.exp(r - top), 0.0) for m, r in zip(members, raised)]
        amount = jnp.sum(shares[0] + shares[1], keepdims=True)
        here = (row_id == place // 4) & (lane_id == (place % 4) * 32 + p * 16)
        mine = jnp.sum(jnp.where(here, own, 0.0), keepdims=True)
        value = mine - (jnp.log(amount) + top)
        log_ref[p] = value[0, 0]
        twist = jnp.sum(jnp.where((row_id == 0) & (lane_id == p), second, 0.0), keepdims=True)
        twist_ref[p] = twist[0, 0]


def body(
    prefix_cache, suffix_cache, queries, step_kv, twist_weight, prior_weights, prompt_ids, ancestors
):
    swap = [(0, 1), (1, 0)]
    cross = [(i, i + 1) for i in range(1, NZ * NX * NC - 1, 2)]
    cross = cross + [(b, a) for a, b in cross]
    first_kv = step_kv[:, 0]
    other_prefix = lax.ppermute(prefix_cache, "core", swap)
    pair_cache = lax.ppermute(suffix_cache, "core", swap)
    far_cache = lax.ppermute(suffix_cache, DOM, cross)
    pair_kv = lax.ppermute(first_kv, "core", swap)
    far_kv = lax.ppermute(first_kv, DOM, cross)
    weight_rows = twist_weight.reshape(16, 128)

    blocks = pl.pallas_call(
        prep_kernel,
        out_shape=jax.ShapeDtypeStruct((RING, BLOCK_ROWS, 128), BF16),
        in_specs=[SMEM, VMEM],
        out_specs=VMEM,
        scratch_shapes=[pltpu.VMEM((BLOCK_ROWS, 128), F32)],
        compiler_params=PARAMS,
        name="prep",
    )(prompt_ids, queries)
    gathered = lax.all_to_all(blocks, PEERS, 0, 0, tiled=True)
    local_kv = step_kv.reshape(2, 4, 256)
    late = lax.optimization_barrier((ancestors, prior_weights, prompt_ids, gathered))
    ancestors, prior_weights, prompt_ids = late[:3]
    plane = jax.ShapeDtypeStruct((8, 128), F32)
    level, dot = pl.pallas_call(
        first_kernel,
        out_shape=(plane, plane),
        in_specs=[VMEM] * 4,
        out_specs=(VMEM, VMEM),
        compiler_params=PARAMS,
        name="first_local",
    )(blocks[0:1], suffix_cache, local_kv, weight_rows)
    parts = pl.pallas_call(
        prefix_kernel,
        out_shape=jax.ShapeDtypeStruct((RING, PART_ROWS, 128), BF16),
        in_specs=[SMEM] * 2 + [VMEM] * 6,
        out_specs=VMEM,
        compiler_params=PARAMS,
        name="prefix",
    )(prompt_ids, prior_weights, gathered, prefix_cache, other_prefix, weight_rows, level, dot)
    received = lax.all_to_all(parts, PEERS, 0, 0, tiled=True)
    copied, carried, mean, second_level = pl.pallas_call(
        second_kernel,
        out_shape=(
            jax.ShapeDtypeStruct(suffix_cache.shape, BF16),
            jax.ShapeDtypeStruct(first_kv.shape, BF16),
            jax.ShapeDtypeStruct((32, 128), F32),
            plane,
        ),
        in_specs=[SMEM] + [VMEM] * 7,
        out_specs=(VMEM,) * 4,
        compiler_params=PARAMS,
        cost_estimate=LONG,
        name="second_local",
    )(ancestors, blocks[0:1], suffix_cache, pair_cache, far_cache, local_kv, pair_kv, far_kv)
    attn, send = pl.pallas_call(
        finish_kernel,
        out_shape=(
            jax.ShapeDtypeStruct((2, 2048), F32),
            jax.ShapeDtypeStruct((NC * NT, 16, 128), F32),
        ),
        in_specs=[VMEM] * 4,
        out_specs=(VMEM,) * 2,
        compiler_params=PARAMS,
        name="finish",
    )(received, mean, second_level, weight_rows)
    lines = lax.all_to_all(send, ("core", "tp"), 0, 0, tiled=True)
    log_weights, twist_two = pl.pallas_call(
        weight_kernel,
        out_shape=(jax.ShapeDtypeStruct((2,), F32), jax.ShapeDtypeStruct((2,), F32)),
        in_specs=[SMEM, VMEM],
        out_specs=(SMEM, SMEM),
        compiler_params=PARAMS,
        name="weights",
    )(prompt_ids, lines)
    return (log_weights, copied, carried, attn.astype(BF16), twist_two)


def solution(mesh):
    inner = Mesh(mesh.devices.reshape(NZ, 2, 2, NC, NT), WIDE)
    placed = (
        P(None, None, DOM, "tp"),
        P(DOM, None, None, "tp"),
        P(DOM, None, "tp"),
        P(DOM, None, None, "tp"),
        P("tp"),
        P(DOM),
        P(DOM),
        P(DOM),
    )
    return jax.shard_map(
        body,
        mesh=inner,
        in_specs=placed,
        out_specs=(
            P(DOM),
            P(DOM, None, None, "tp"),
            P(DOM, None, "tp"),
            P(DOM, "tp"),
            P(DOM),
        ),
        check_vma=False,
    )
```

time: 89.1 us -> 78 us (0.88)
  waiting for transfers between devices: 30.1 us -> 21.6 us
  starting transfers between devices: 40.2 us -> 37.6 us
  local copies, waits for them, and re-layouts: 4.08 us -> 2.89 us
  Pallas kernels: 12.9 us -> 14 us
    all_to_all x3, waiting for transfers between devices: 29.4 us -> 21.6 us  [the longest x1 11.7 us: body(): received = lax.all_to_all(parts, PEERS, 0, 0, tiled=True)]
    ppermute x1, starting transfers between devices: 5.83 us -> 3.45 us  [body(): far_kv = lax.ppermute(first_kv, DOM, cross)]
    pallas_call x2 -> x4, Pallas kernels: 9.67 us -> 10.9 us  [the longest x1 5.72 us: body(): pl.pallas_call(prefix_kernel, out_shape=jax.ShapeDtypeStruct((RING, PART_...]
    unnamed x22 -> x18, local copies, waits for them, and re-layouts: 3.32 us -> 2.15 us
    ppermute x1, starting transfers between devices: 1.04 us -> 0.09 us  [body(): other_prefix = lax.ppermute(prefix_cache, 'core', swap)]
    ppermute x1, starting transfers between devices: 0.11 us -> 1.04 us  [body(): pair_cache = lax.ppermute(suffix_cache, 'core', swap)]
  transfers between devices with their start and end apart: 8 -> 8, of which waited for: 4 -> 3; matrix products, arithmetic and copies ran while one was open for 2% -> 2% of each run, Pallas kernels for 6% -> 13%
where the time goes in v2:
time: 78 us; the launch traced here: 77.4 us
  starting transfers between devices  37.6 us (48%)
  waiting for transfers between devices  21.6 us (28%)
  Pallas kernels  14 us (18%)
  local copies, waits for them, and re-layouts  2.89 us (4%)
  between operations  0.8 us (1%)
    all_to_all x1, starting transfers between devices, body(): gathered = lax.all_to_all(blocks, PEERS, 0, 0, tiled=True)  12 us
    all_to_all x1, waiting for transfers between devices, body(): received = lax.all_to_all(parts, PEERS, 0, 0, tiled=True)  11.7 us
    all_to_all x1, starting transfers between devices, body(): lines = lax.all_to_all(send, ('core', 'tp'), 0, 0, tiled=True)  9.73 us
    all_to_all x1, starting transfers between devices, body(): received = lax.all_to_all(parts, PEERS, 0, 0, tiled=True)  7.89 us
    pallas_call x1, Pallas kernels, body(): pl.pallas_call(prefix_kernel, out_shape=jax.ShapeDtypeStruct((RING, PART_...  5.72 us
    all_to_all x1, waiting for transfers between devices, body(): gathered = lax.all_to_all(blocks, PEERS, 0, 0, tiled=True)  5.54 us
    all_to_all x1, waiting for transfers between devices, body(): lines = lax.all_to_all(send, ('core', 'tp'), 0, 0, tiled=True)  4.36 us
    ppermute x1, starting transfers between devices, body(): far_kv = lax.ppermute(first_kv, DOM, cross)  3.45 us
  transfers between devices with their start and end apart: 8, of which 3 were waited for; matrix products, arithmetic and copies ran while one was open for 2% of the time, Pallas kernels for 13%

profile of v2, /device:TPU:1, one launch (start us, length us, event | category | flops | bytes accessed | tf_op | source)
XLA Modules:
  0.0 77.4 jit_solution(3065796255762734207)
XLA Ops:
  0.7 0.8 %copy-done.3 = bf16[2,2,2048]{2,1,0:T(2,128)(2,1)S(1)} copy-done((bf16[2,2,2048]{2,1,0:T(2,128)(2,1)S(1)}, bf16[2,2,2048]{2,1,0:T(2,128)(2,1)}, u32[]{:S(2)}) %copy-start.3) | copy-done | bytes 16408
  1.4 0.7 copy-done.4
  2.1 1.4 %prep.1 = bf16[32,72,128]{2,1,0:T(8,128)(2,1)} custom-call(s32[2]{0:T(128)S(1)} %copy-done.4, bf16[2,2,2048]{2,1,0:T(2,128)(2,1)S(1)} %copy-done.3), custom_call_target="tpu_custom_call" | custom-call | tf_op jit(solution)/shard_map/prep/pallas_call | solution.py:340
  3.5 12.0 %all-to-all-start = ((bf16[32,72,128]{2,1,0:T(8,128)(2,1)}), bf16[32,72,128]{2,1,0:T(8,128)(2,1)S(1)}, u32[]{:S(2)}, u32[]{:S(2)}) async-start(bf16[32,72,128]{2,1,0:T(8,128)(2,1)} %prep.1), calls=%async_computation | async-start | bytes 1179648 | tf_op jit(solution)/shard_map/all_to_all | solution.py:349
  15.5 1.0 %collective-permute-start.1 = (bf16[2,2,512,256]{3,2,1,0:T(8,128)(2,1)S(1)}, bf16[2,2,512,256]{3,2,1,0:T(8,128)(2,1)}, u32[]{:S(2)}, u32[]{:S(2)}) collective-permute-start(bf16[2,2,512,256]{3,2,1,0:T(8,128)(2,1)S(1)} %copy-done), channel_id=1, source_target_pairs={{0,4},{4,0},{1,5},{5,1},{2,6},{6,2},{3,7},{7,3},{8,12},{12,8},{9,1... | collective-permute-start | bytes 3145736 | tf_op jit(solution)/shard_map/ppermute | solution.py:334
  16.6 3.3 %collective-permute-start.2 = (bf16[2,2,512,256]{3,2,1,0:T(8,128)(2,1)S(1)}, bf16[2,2,512,256]{3,2,1,0:T(8,128)(2,1)}, u32[]{:S(2)}, u32[]{:S(2)}) collective-permute-start(bf16[2,2,512,256]{3,2,1,0:T(8,128)(2,1)S(1)} %copy-done), channel_id=1, source_target_pairs={{4,8},{12,16},{20,24},{28,32},{36,40},{44,48},{52,56},{60,64},{68,... | collective-permute-start | bytes 3145736 | tf_op jit(solution)/shard_map/ppermute | solution.py:335
  19.9 0.1 collective-permute-start
  20.1 3.4 %collective-permute-start.4 = (bf16[2,2,256]{2,1,0:T(2,128)(2,1)S(1)}, bf16[2,2,256]{2,1,0:T(2,128)(2,1)S(1)}, u32[]{:S(2)}, u32[]{:S(2)}) collective-permute-start(bf16[2,2,256]{2,1,0:T(2,128)(2,1)S(1)} %slice_bitcast_fusion), channel_id=1, source_target_pairs={{4,8},{12,16},{20,24},{28,32},{36,40},{44,48},{52,56},{60,64},{68,... | collective-permute-start | bytes 6152 | tf_op jit(solution)/shard_map/ppermute | solution.py:337
  23.5 0.1 collective-permute-start.3
  23.6 0.0 copy-start.2
  23.6 0.7 slice.9.q_ref
  24.4 1.1 %first_local.1 = (f32[8,128]{1,0:T(8,128)S(1)}, f32[8,128]{1,0:T(8,128)S(1)}) custom-call(bf16[1,72,128]{2,1,0:T(8,128)(2,1)S(1)} %slice.9.q_ref, bf16[2,2,512,256]{3,2,1,0:T(8,128)(2,1)S(1)} %copy-done, bf16[2,4,256]{2,1,0:T(4,128)(2,1)S(1)} %reshape.17.kv_ref, f32[16,128]{1,0:T(8,128)S(1)} %bitcast.5), custom_call_target="tpu_custom_call" | custom-call | tf_op jit(solution)/shard_map/first_local/pallas_call | solution.py:354
  25.5 5.5 %all-to-all-done.q_ref = bf16[32,72,128]{2,1,0:T(8,128)(2,1)S(1)} async-done(((bf16[32,72,128]{2,1,0:T(8,128)(2,1)}), bf16[32,72,128]{2,1,0:T(8,128)(2,1)S(1)}, u32[]{:S(2)}, u32[]{:S(2)}) %all-to-all-start) | async-done | bytes 589856 | tf_op jit(solution)/shard_map/all_to_all | solution.py:349
  31.1 0.7 copy-done.5
  31.7 0.0 copy-done.6
  31.7 5.7 %prefix.1 = bf16[32,72,128]{2,1,0:T(8,128)(2,1)} custom-call(s32[2]{0:T(128)S(1)} %copy-done.5, f32[2]{0:T(128)S(1)} %copy-done.6, bf16[32,72,128]{2,1,0:T(8,128)(2,1)S(1)} %all-to-all-done.q_ref, bf16[4,2,128,256]{3,2,1,0:T(8,128)(2,1)S(1)} %copy-done.1, bf16[4,2,128,256]{3,2,1,0:T(8,128)(2,1)S(1)} %collective-permute-done.other_ref, ...), custom_call_target="tpu_custom_call" | custom-call | tf_op jit(solution)/shard_map/prefix/pallas_call | solution.py:362
  37.4 7.9 %all-to-all-start.1 = ((bf16[32,72,128]{2,1,0:T(8,128)(2,1)}), bf16[32,72,128]{2,1,0:T(8,128)(2,1)S(1)}, u32[]{:S(2)}, u32[]{:S(2)}) async-start(bf16[32,72,128]{2,1,0:T(8,128)(2,1)} %prefix.1), calls=%async_computation.1 | async-start | bytes 1179648 | tf_op jit(solution)/shard_map/all_to_all | solution.py:370
  45.4 2.8 %second_local.1 = (bf16[2,2,512,256]{3,2,1,0:T(8,128)(2,1)}, bf16[2,2,256]{2,1,0:T(2,128)(2,1)}, f32[32,128]{1,0:T(8,128)S(1)}, f32[8,128]{1,0:T(8,128)S(1)}) custom-call(s32[2]{0:T(128)S(1)} %copy-done.7, bf16[1,72,128]{2,1,0:T(8,128)(2,1)S(1)} %slice.9.q_ref, bf16[2,2,512,256]{3,2,1,0:T(8,128)(2,1)S(1)} %copy-done, ...), custom_call_target="tpu_custom_call" | custom-call | flops 20000000000 | bytes 80000000 | tf_op jit(solution)/shard_map/second_local/pallas_call | solution.py:371
  48.2 11.7 %all-to-all-done.1.part_ref = bf16[32,72,128]{2,1,0:T(8,128)(2,1)S(1)} async-done(((bf16[32,72,128]{2,1,0:T(8,128)(2,1)}), bf16[32,72,128]{2,1,0:T(8,128)(2,1)S(1)}, u32[]{:S(2)}, u32[]{:S(2)}) %all-to-all-start.1) | async-done | bytes 589856 | tf_op jit(solution)/shard_map/all_to_all | solution.py:370
  59.9 1.3 %finish.1 = (f32[2,2048]{1,0:T(2,128)S(1)}, f32[8,16,128]{2,1,0:T(8,128)}) custom-call(bf16[32,72,128]{2,1,0:T(8,128)(2,1)S(1)} %all-to-all-done.1.part_ref, f32[32,128]{1,0:T(8,128)S(1)} %get-tuple-element.23.mean_ref, f32[8,128]{1,0:T(8,128)S(1)} %get-tuple-element.24.level_ref, f32[16,128]{1,0:T(8,128)S(1)} %bitcast.7), custom_call_target="tpu_custom_call" | custom-call | tf_op jit(solution)/shard_map/finish/pallas_call | solution.py:385
  61.2 9.7 %all-to-all-start.2 = ((f32[8,16,128]{2,1,0:T(8,128)}), f32[8,16,128]{2,1,0:T(8,128)S(1)}, u32[]{:S(2)}, u32[]{:S(2)}) async-start(f32[8,16,128]{2,1,0:T(8,128)} %get-tuple-element.25), calls=%async_computation.2 | async-start | bytes 131072 | tf_op jit(solution)/shard_map/all_to_all | solution.py:396
  70.9 0.6 convert_element_type.3
  71.5 4.4 %all-to-all-done.2.all_ref = f32[8,16,128]{2,1,0:T(8,128)S(1)} async-done(((f32[8,16,128]{2,1,0:T(8,128)}), f32[8,16,128]{2,1,0:T(8,128)S(1)}, u32[]{:S(2)}, u32[]{:S(2)}) %all-to-all-start.2) | async-done | bytes 65568 | tf_op jit(solution)/shard_map/all_to_all | solution.py:396
  75.8 1.6 %weights.1 = (f32[2]{0:T(128)}, f32[2]{0:T(128)}) custom-call(s32[2]{0:T(128)S(1)} %copy-done.5, f32[8,16,128]{2,1,0:T(8,128)S(1)} %all-to-all-done.2.all_ref), custom_call_target="tpu_custom_call" | custom-call | tf_op jit(solution)/shard_map/weights/pallas_call | solution.py:397
  (20 shorter events, 0.1 us)
Async XLA Ops:
  0.6 14.9 %copy-start = (bf16[2,2,512,256]{3,2,1,0:T(8,128)(2,1)S(1)}, bf16[2,2,512,256]{3,2,1,0:T(8,128)(2,1)}, u32[]{:S(2)}) copy-start(bf16[2,2,512,256]{3,2,1,0:T(8,128)(2,1)} %own_ref.5) | copy-start | bytes 3145732
  0.6 0.8 %copy-start.3 = (bf16[2,2,2048]{2,1,0:T(2,128)(2,1)S(1)}, bf16[2,2,2048]{2,1,0:T(2,128)(2,1)}, u32[]{:S(2)}) copy-start(bf16[2,2,2048]{2,1,0:T(2,128)(2,1)} %q_ref.1) | copy-start | bytes 49156
  1.4 0.7 copy-start.4
  3.5 16.4 %copy-start.1 = (bf16[4,2,128,256]{3,2,1,0:T(8,128)(2,1)S(1)}, bf16[4,2,128,256]{3,2,1,0:T(8,128)(2,1)}, u32[]{:S(2)}) copy-start(bf16[4,2,128,256]{3,2,1,0:T(8,128)(2,1)} %own_ref.4) | copy-start | bytes 1572868
  3.5 16.5 %copy-start.8 = (bf16[2,2,2,256]{3,2,1,0:T(2,128)(2,1)S(1)}, bf16[2,2,2,256]{3,2,1,0:T(2,128)(2,1)}, u32[]{:S(2)}) copy-start(bf16[2,2,2,256]{3,2,1,0:T(2,128)(2,1)} %param.11) | copy-start | bytes 12292
  3.5 27.5 %all-to-all-start = ((bf16[32,72,128]{2,1,0:T(8,128)(2,1)}), bf16[32,72,128]{2,1,0:T(8,128)(2,1)S(1)}, u32[]{:S(2)}, u32[]{:S(2)}) async-start(bf16[32,72,128]{2,1,0:T(8,128)(2,1)} %prep.1), calls=%async_computation | async-start | bytes 1179648 | tf_op jit(solution)/shard_map/all_to_all | solution.py:349
  15.5 29.8 %collective-permute-start.1 = (bf16[2,2,512,256]{3,2,1,0:T(8,128)(2,1)S(1)}, bf16[2,2,512,256]{3,2,1,0:T(8,128)(2,1)}, u32[]{:S(2)}, u32[]{:S(2)}) collective-permute-start(bf16[2,2,512,256]{3,2,1,0:T(8,128)(2,1)S(1)} %copy-done), channel_id=1, source_target_pairs={{0,4},{4,0},{1,5},{5,1},{2,6},{6,2},{3,7},{7,3},{8,12},{12,8},{9,1... | collective-permute-start | bytes 3145736 | tf_op jit(solution)/shard_map/ppermute | solution.py:334
  16.6 28.8 %collective-permute-start.2 = (bf16[2,2,512,256]{3,2,1,0:T(8,128)(2,1)S(1)}, bf16[2,2,512,256]{3,2,1,0:T(8,128)(2,1)}, u32[]{:S(2)}, u32[]{:S(2)}) collective-permute-start(bf16[2,2,512,256]{3,2,1,0:T(8,128)(2,1)S(1)} %copy-done), channel_id=1, source_target_pairs={{4,8},{12,16},{20,24},{28,32},{36,40},{44,48},{52,56},{60,64},{68,... | collective-permute-start | bytes 3145736 | tf_op jit(solution)/shard_map/ppermute | solution.py:335
  19.9 11.1 %collective-permute-start = (bf16[4,2,128,256]{3,2,1,0:T(8,128)(2,1)S(1)}, bf16[4,2,128,256]{3,2,1,0:T(8,128)(2,1)S(1)}, u32[]{:S(2)}, u32[]{:S(2)}) collective-permute-start(bf16[4,2,128,256]{3,2,1,0:T(8,128)(2,1)S(1)} %copy-done.1), channel_id=1, source_target_pairs={{0,4},{4,0},{1,5},{5,1},{2,6},{6,2},{3,7},{7,3},{8,12},{12,8},{9,1... | collective-permute-start | bytes 1572872 | tf_op jit(solution)/shard_map/ppermute | solution.py:333
  20.1 25.3 %collective-permute-start.4 = (bf16[2,2,256]{2,1,0:T(2,128)(2,1)S(1)}, bf16[2,2,256]{2,1,0:T(2,128)(2,1)S(1)}, u32[]{:S(2)}, u32[]{:S(2)}) collective-permute-start(bf16[2,2,256]{2,1,0:T(2,128)(2,1)S(1)} %slice_bitcast_fusion), channel_id=1, source_target_pairs={{4,8},{12,16},{20,24},{28,32},{36,40},{44,48},{52,56},{60,64},{68,... | collective-permute-start | bytes 6152 | tf_op jit(solution)/shard_map/ppermute | solution.py:337
  23.5 21.9 %collective-permute-start.3 = (bf16[2,2,256]{2,1,0:T(2,128)(2,1)S(1)}, bf16[2,2,256]{2,1,0:T(2,128)(2,1)S(1)}, u32[]{:S(2)}, u32[]{:S(2)}) collective-permute-start(bf16[2,2,256]{2,1,0:T(2,128)(2,1)S(1)} %slice_bitcast_fusion), channel_id=1, source_target_pairs={{0,4},{4,0},{1,5},{5,1},{2,6},{6,2},{3,7},{7,3},{8,12},{12,8},{9,1... | collective-permute-start | bytes 6152 | tf_op jit(solution)/shard_map/ppermute | solution.py:336
  23.6 0.7 copy-start.2
  31.0 0.7 copy-start.5
  31.0 0.7 copy-start.6
  37.4 7.9 %copy-start.7 = (s32[2]{0:T(128)S(1)}, s32[2]{0:T(128)}, u32[]{:S(2)}) copy-start(s32[2]{0:T(128)} %anc_ref) | copy-start | bytes 28
  37.4 22.4 %all-to-all-start.1 = ((bf16[32,72,128]{2,1,0:T(8,128)(2,1)}), bf16[32,72,128]{2,1,0:T(8,128)(2,1)S(1)}, u32[]{:S(2)}, u32[]{:S(2)}) async-start(bf16[32,72,128]{2,1,0:T(8,128)(2,1)} %prefix.1), calls=%async_computation.1 | async-start | bytes 1179648 | tf_op jit(solution)/shard_map/all_to_all | solution.py:370
  61.2 14.7 %all-to-all-start.2 = ((f32[8,16,128]{2,1,0:T(8,128)}), f32[8,16,128]{2,1,0:T(8,128)S(1)}, u32[]{:S(2)}, u32[]{:S(2)}) async-start(f32[8,16,128]{2,1,0:T(8,128)} %get-tuple-element.25), calls=%async_computation.2 | async-start | bytes 131072 | tf_op jit(solution)/shard_map/all_to_all | solution.py:396

commit v3 on v2

v3 whole, which is shorter than its diff:
```python
import math

import jax
import jax.numpy as jnp
from jax import lax
from jax.experimental import pallas as pl
from jax.experimental.pallas import tpu as pltpu
from jax.sharding import Mesh
from jax.sharding import PartitionSpec as P

HEAD_DIM = 128
PROMPTS = 4
GROUP = 8
NZ, NX, NC, NT = 8, 4, 2, 4
RING = 16
PLANE = RING // 4
DOM = ("z2", "z1", "z0", "x1", "x0", "core")
WIDE = ("z2", "z1", "z0", "x1", "x0", "core", "tp")
SHARE = ("x0", "core")
PEERS = ("x1", "z2", "z1", "z0")
FACTOR = 1.0 / math.sqrt(HEAD_DIM)
FACTOR2 = FACTOR * math.log2(math.e)
Q_ROWS = 64
ID_ROWS = 8
BLOCK_ROWS = Q_ROWS + ID_ROWS
OUT_ROWS = 32
PART_ROWS = OUT_ROWS + 8 + 4 * PLANE
CHUNK = 8
F32 = jnp.float32
BF16 = jnp.bfloat16
NT_DIMS = (((1,), (1,)), ((), ()))
VMEM = pl.BlockSpec(memory_space=pltpu.VMEM)
SMEM = pl.BlockSpec(memory_space=pltpu.SMEM)
HBM = pl.BlockSpec(memory_space=pltpu.HBM)
LONG = pl.CostEstimate(flops=2 * 10**10, bytes_accessed=8 * 10**7, transcendentals=0)
PARAMS = pltpu.CompilerParams(vmem_limit_bytes=16 * 1024 * 1024)
WHOLE = pltpu.CompilerParams(vmem_limit_bytes=60 * 1024 * 1024)


def lanes(shape):
    return lax.broadcasted_iota(jnp.int32, shape, len(shape) - 1)


def ring_place():
    place = 0
    for axis in PEERS:
        place = place * 2 + lax.axis_index(axis)
    return place


def prep_kernel(ids_hbm, q_hbm, out_ref, own_ref, ids_ref, q_ref, rows_ref, sems):
    copies = [
        pltpu.make_async_copy(src, dst, sems.at[n])
        for n, (src, dst) in enumerate(((ids_hbm, ids_ref), (q_hbm, q_ref)))
    ]
    for copy in copies:
        copy.start()
    for copy in copies:
        copy.wait()
    for p in range(2):
        both = q_ref[p].astype(F32)
        for s in range(2):
            for h in range(16):
                kv, g = divmod(h, GROUP)
                row = kv * 32 + p * 16 + s * 8 + g
                rows_ref[row : row + 1, :] = both[s : s + 1, h * 128 : (h + 1) * 128]
    first, second = ids_ref[0].astype(F32), ids_ref[1].astype(F32)
    rows_ref[Q_ROWS:BLOCK_ROWS, :] = jnp.where(lanes((ID_ROWS, 128)) < 64, first, second)
    block = rows_ref[...].astype(BF16)
    for i in range(RING):
        out_ref[i] = block
    own_ref[...] = rows_ref[0:Q_ROWS, :]


def prefix_kernel(
    q_ref, own_hbm, pair_hbm, next_hbm, cross_hbm, facts_ref, w_ref, level_ref, dot_ref, out_ref, cache_ref, sems
):
    copies = [
        pltpu.make_async_copy(src, cache_ref.at[n], sems.at[n])
        for n, src in enumerate((own_hbm, pair_hbm, next_hbm, cross_hbm))
    ]
    for copy in copies:
        copy.start()
    for copy in copies:
        copy.wait()
    keys, values = [], []
    for kv in range(2):
        cols = slice(kv * 128, (kv + 1) * 128)
        for kind, into in ((0, keys), (1, values)):
            into.append(
                jnp.concatenate(
                    [
                        jnp.concatenate([cache_ref[n, g, kind, :, cols] for n in range(4)], axis=0)
                        for g in range(PROMPTS)
                    ],
                    axis=1,
                )
            )
    count = CHUNK * 32
    shape = (CHUNK, 32, 128)
    row_id = lax.broadcasted_iota(jnp.int32, shape, 1)
    lane_id = lanes(shape)
    spot = row_id + 32 * (lax.broadcasted_iota(jnp.int32, shape, 0) % 4)
    levels, dots, heads, bodies = [], [], [], []
    head_row = lax.broadcasted_iota(jnp.int32, (CHUNK, 8, 128), 1)
    facts = facts_ref[...][None]
    for start in range(0, RING, CHUNK):
        block = q_ref[start : start + CHUNK].astype(F32)
        both = block[:, Q_ROWS:BLOCK_ROWS].reshape(CHUNK * ID_ROWS, 128)
        turned = pltpu.roll(both, 64, 1)
        left = lanes(both.shape) < 64
        ids = jnp.stack(
            [
                jnp.where(left, both, turned).reshape(CHUNK, 1, ID_ROWS, 128),
                jnp.where(left, turned, both).reshape(CHUNK, 1, ID_ROWS, 128),
            ],
            axis=1,
        )
        ids = jnp.broadcast_to(ids, (CHUNK, 2, 2, 8, 128)).reshape(count, 128)
        picks = [ids == float(g) for g in range(PROMPTS)]
        means, tops0, tops1, firsts = [], [], [], []
        for kv in range(2):
            q = block[:, kv * 32 : (kv + 1) * 32].reshape(count, 128)
            spread = jnp.concatenate([jnp.where(pick, q, 0.0).astype(BF16) for pick in picks], axis=1)
            scores = lax.dot_general(spread, keys[kv], NT_DIMS, preferred_element_type=F32)
            top = jnp.max(scores, axis=1, keepdims=True)
            weights = jnp.exp2((scores - top) * FACTOR2)
            total = jnp.sum(weights, axis=1, keepdims=True)
            sums = jnp.dot(weights.astype(BF16), values[kv], preferred_element_type=F32)
            num = sums[:, 384:512]
            for g in (2, 1, 0):
                num = jnp.where(picks[g], sums[:, g * 128 : (g + 1) * 128], num)
            mean = (num / total).reshape(CHUNK, 2, 2, 8, 128)
            level = (top * FACTOR + jnp.log(total)).reshape(CHUNK, 2, 2, 8, 1)
            w = w_ref[kv * 8 : (kv + 1) * 8, :].reshape(1, 1, 8, 128)
            firsts.append(jnp.sum(mean[:, :, 0] * w, axis=-1, keepdims=True))
            tops0.append(level[:, :, 0])
            tops1.append(level[:, :, 1])
            means.append(mean[:, :, 1])

        def merge(pair):
            return jnp.stack(pair, axis=2).reshape(CHUNK, 32, pair[0].shape[-1])

        def pack(pair):
            wide = jnp.where(lane_id == spot, merge(pair), 0.0)
            return jnp.sum(wide.reshape(CHUNK // 4, 128, 128), axis=1)

        bodies.append(merge(means))
        levels.append(pack(tops0))
        dots.append(pack(firsts))
        high, mid, low = split(jnp.sum(jnp.where(lane_id == row_id, merge(tops1), 0.0), axis=1))
        line = high + pltpu.roll(mid, 32, 1) + pltpu.roll(low, 64, 1)
        head = jnp.where(head_row == 0, line[:, None, :], facts)
        heads.append(head)
    level, dot = jnp.concatenate(levels, axis=0), jnp.concatenate(dots, axis=0)
    top = jnp.maximum(level, level_ref[...])
    old, new = jnp.exp(level - top), jnp.exp(level_ref[...] - top)
    dot = (dot * old + dot_ref[...] * new) / (old + new)
    level = top + jnp.log(old + new)
    for start, mean, head in zip(range(0, RING, CHUNK), bodies, heads):
        common = jnp.concatenate([*split(level), dot], axis=0)
        common = jnp.broadcast_to(common[None], (CHUNK, 4 * PLANE, 128))
        out_ref[start : start + CHUNK] = jnp.concatenate([mean, head, common], axis=1).astype(BF16)


def split(value):
    high = value.astype(BF16).astype(F32)
    rest = value - high
    mid = rest.astype(BF16).astype(F32)
    return high, mid, rest - mid


def local_attend(q, keys, values, fresh):
    q16 = q.astype(BF16)
    scores = lax.dot_general(q16, keys, NT_DIMS, preferred_element_type=F32)
    extra = [jnp.sum(q * k, axis=1, keepdims=True) for k, _ in fresh]
    top = jnp.max(scores, axis=1, keepdims=True)
    for e in extra:
        top = jnp.maximum(top, e)
    weights = jnp.exp2((scores - top) * FACTOR2)
    total = jnp.sum(weights, axis=1, keepdims=True)
    num = jnp.dot(weights.astype(BF16), values, preferred_element_type=F32)
    for e, (_, v) in zip(extra, fresh):
        weight = jnp.exp2((e - top) * FACTOR2)
        total = total + weight
        num = num + weight.astype(BF16).astype(F32) * v
    return num / total, top * FACTOR + jnp.log(total)


def first_kernel(ids_ref, prior_ref, q_ref, own_ref, kv_ref, w_ref, level_ref, dot_ref, facts_ref):
    queries = q_ref[...]
    step_kv = kv_ref[...].astype(F32)
    means, tops = [], []
    for p in range(2):
        for kv in range(2):
            cols = slice(kv * 128, (kv + 1) * 128)
            row = kv * 32 + p * 16
            mean, top = local_attend(
                queries[row : row + 8],
                own_ref[p, 0, :, cols],
                own_ref[p, 1, :, cols],
                [(step_kv[p, 0, 0:1, cols], step_kv[p, 0, 1:2, cols])],
            )
            means.append(mean)
            tops.append(top)
    w = w_ref[...]
    dot = jnp.sum(jnp.concatenate(means, axis=0) * jnp.concatenate([w, w], axis=0), axis=1, keepdims=True)
    top = jnp.concatenate(tops, axis=0)
    place = ring_place()
    spot = lax.broadcasted_iota(jnp.int32, (32, 128), 0) + 32 * (place % 4)
    lane_id = lanes((32, 128))
    level_row = jnp.sum(jnp.where(lane_id == spot, top, 0.0), axis=0, keepdims=True)
    dot_row = jnp.sum(jnp.where(lane_id == spot, dot, 0.0), axis=0, keepdims=True)
    here = lax.broadcasted_iota(jnp.int32, (PLANE, 128), 0) == place // 4
    here = here & (lanes((PLANE, 128)) // 32 == place % 4)
    level_ref[...] = jnp.where(here, level_row, -1e30)
    dot_ref[...] = jnp.where(here, dot_row, 0.0)
    slot = lanes((8, 128)) // 16 - (place % 4) * 2
    prior = jnp.where(slot == 0, prior_ref[0], jnp.where(slot == 1, prior_ref[1], 0.0))
    first, second = ids_ref[0].astype(F32), ids_ref[1].astype(F32)
    ids = jnp.where(slot == 0, first, jnp.where(slot == 1, second, 0.0))
    row_id = lax.broadcasted_iota(jnp.int32, (8, 128), 0)
    facts = jnp.where(row_id == 4, ids, 0.0)
    for r, part in enumerate(split(prior)):
        facts = jnp.where(row_id == r + 1, part, facts)
    facts_ref[...] = facts


def second_kernel(
    anc_hbm, q_ref, own_ref, pair_ref, far_ref, kv_ref, pair_kv_ref, far_kv_ref,
    copied_ref, carried_ref, mean_ref, level_ref, anc_ref, sem,
):
    copy = pltpu.make_async_copy(anc_hbm, anc_ref, sem)
    copy.start()
    copy.wait()
    core = lax.axis_index("core")
    base = 0
    for axis in DOM:
        base = base * 2 + lax.axis_index(axis)
    base = base * 2 - 2
    for slot in range(2):
        pos = anc_ref[slot] - base
        side, which = pos // 2, pos % 2
        from_own = side == 1
        from_pair = side == jnp.where(core == 0, 2, 0)
        from_far = side == jnp.where(core == 0, 0, 2)
        for j in range(2):
            for flag, cache, kvs in (
                (from_own, own_ref, kv_ref),
                (from_pair, pair_ref, pair_kv_ref),
                (from_far, far_ref, far_kv_ref),
            ):

                @pl.when(flag & (which == j))
                def _():
                    copied_ref[slot] = cache[j]
                    carried_ref[slot] = kvs[j, 0]

    queries = q_ref[...]
    step_kv = kv_ref[...].astype(F32)
    carried = carried_ref[...].astype(F32)
    tops = []
    for p in range(2):
        for kv in range(2):
            cols = slice(kv * 128, (kv + 1) * 128)
            row = kv * 32 + p * 16 + 8
            mean, top = local_attend(
                queries[row : row + 8],
                copied_ref[p, 0, :, cols],
                copied_ref[p, 1, :, cols],
                [
                    (carried[p, 0:1, cols], carried[p, 1:2, cols]),
                    (step_kv[p, 1, 0:1, cols], step_kv[p, 1, 1:2, cols]),
                ],
            )
            mean_ref[p * 16 + kv * 8 : p * 16 + kv * 8 + 8, :] = mean
            tops.append(top)
    top = jnp.concatenate(tops, axis=0)
    row_id = lax.broadcasted_iota(jnp.int32, (32, 128), 0)
    row = jnp.sum(jnp.where(lanes((32, 128)) == row_id, top, 0.0), axis=0, keepdims=True)
    level_ref[...] = jnp.broadcast_to(row, (8, 128))


def finish_kernel(part_ref, mean_ref, level_ref, w_ref, out_ref, send_ref, wide_ref):
    parts = part_ref[...].astype(F32)
    heads = parts[:, OUT_ROWS : OUT_ROWS + 8]
    head_row = lax.broadcasted_iota(jnp.int32, heads.shape, 1)
    theirs = jnp.sum(jnp.where(head_row == 0, heads, 0.0), axis=1)
    theirs = theirs + pltpu.roll(theirs, 96, 1) + pltpu.roll(theirs, 64, 1)
    mine = level_ref[0:1, :]
    top = jnp.maximum(jnp.max(theirs, axis=0, keepdims=True), mine)
    scale = jnp.exp(theirs - top)
    my_scale = jnp.exp(mine - top)
    inverse = 1.0 / (jnp.sum(scale, axis=0, keepdims=True) + my_scale)
    table = jnp.concatenate([scale * inverse, jnp.broadcast_to(my_scale * inverse, (128 - RING, 128))], axis=0).T
    attn = mean_ref[...] * table[0:32, RING : RING + 1]
    for i in range(RING):
        attn = attn + table[0:32, i : i + 1] * parts[i, 0:OUT_ROWS]
    w = w_ref[...]
    weighted = jnp.sum(attn * jnp.concatenate([w, w], axis=0), axis=1, keepdims=True)
    for p in range(2):
        for h in range(16):
            wide_ref[p : p + 1, h * 128 : (h + 1) * 128] = attn[p * 16 + h : p * 16 + h + 1, :]
    out_ref[...] = wide_ref[...].astype(BF16)

    base = OUT_ROWS + 8
    high, mid, low, dot = (parts[:, base + PLANE * t : base + PLANE * (t + 1)] for t in range(4))
    level = high + mid + low
    top = jnp.max(level, axis=0)
    scale = jnp.exp(level - top[None])
    twist = jnp.sum(scale * dot, axis=0) / jnp.sum(scale, axis=0)
    for shift in (8, 4, 2, 1):
        twist = twist + pltpu.roll(twist, 128 - shift, 1)
    facts = jnp.sum(heads.reshape(PLANE, 4, 8, 128), axis=1)
    fact_row = lax.broadcasted_iota(jnp.int32, facts.shape, 1)
    prior = jnp.sum(jnp.where((fact_row >= 1) & (fact_row <= 3), facts, 0.0), axis=1)
    ids = jnp.sum(jnp.where(fact_row == 4, facts, 0.0), axis=1)
    kind = lanes((PLANE, 128)) % 16
    line = jnp.where(kind == 0, twist, jnp.where(kind == 1, prior, jnp.where(kind == 2, ids, 0.0)))
    one = lanes((8 - PLANE, 128))
    second = jnp.zeros((8 - PLANE, 128), F32)
    for p in range(2):
        part = jnp.sum(weighted[p * 16 : (p + 1) * 16], axis=0, keepdims=True)
        second = jnp.where(one == p, part, second)
    block = jnp.concatenate([line, second], axis=0)
    for i in range(4 * NT):
        send_ref[i] = block


def weight_kernel(all_ref, log_ref, twist_ref):
    member = lax.axis_index("x0") * NC + lax.axis_index("core")
    place = ring_place()
    row_id = lax.broadcasted_iota(jnp.int32, (8, 128), 0)
    lane_id = lanes((8, 128))
    valid = (lane_id % 16 == 0) & (row_id < PLANE)
    raised, ids = [], []
    own = jnp.zeros((8, 128), F32)
    own_ids = jnp.zeros((8, 128), F32)
    for m in range(4):
        rows = [all_ref[m * NT + t] for t in range(NT)]
        total = rows[0] + rows[1] + rows[2] + rows[3]
        total = jnp.where(row_id < PLANE, total + pltpu.roll(rows[0], 127, 1), total)
        own = jnp.where(member == m, total, own)
        raised.append(total)
        ids.append(pltpu.roll(rows[0], 126, 1))
        own_ids = jnp.where(member == m, ids[-1], own_ids)
    for p in range(2):
        here = (row_id == place // 4) & (lane_id == (place % 4) * 32 + p * 16)
        me = jnp.sum(jnp.where(here, own_ids, 0.0), keepdims=True)
        members = [valid & (i == me) for i in ids]
        masked = [jnp.where(m, r, -1e30) for m, r in zip(members, raised)]
        top = jnp.maximum(jnp.maximum(masked[0], masked[1]), jnp.maximum(masked[2], masked[3]))
        top = jnp.max(top, keepdims=True)
        shares = [jnp.where(m, jnp.exp(r - top), 0.0) for m, r in zip(members, raised)]
        amount = jnp.sum(shares[0] + shares[1] + shares[2] + shares[3], keepdims=True)
        mine = jnp.sum(jnp.where(here, own, 0.0), keepdims=True)
        value = mine - (jnp.log(amount) + top)
        log_ref[p] = value[0, 0]
        twist = jnp.sum(jnp.where((row_id == PLANE) & (lane_id == p), own, 0.0), keepdims=True)
        twist_ref[p] = twist[0, 0]


def body(
    prefix_cache, suffix_cache, queries, step_kv, twist_weight, prior_weights, prompt_ids, ancestors
):
    swap = [(0, 1), (1, 0)]
    cross = [(i, i + 1) for i in range(1, NZ * NX * NC - 1, 2)]
    cross = cross + [(b, a) for a, b in cross]
    next_prefix = lax.ppermute(prefix_cache, "x0", swap)
    pair_prefix = lax.ppermute(prefix_cache, "core", swap)
    cross_prefix = lax.ppermute(next_prefix, "core", swap)
    weight_rows = twist_weight.reshape(16, 128)

    blocks, rows = pl.pallas_call(
        prep_kernel,
        out_shape=(
            jax.ShapeDtypeStruct((RING, BLOCK_ROWS, 128), BF16),
            jax.ShapeDtypeStruct((Q_ROWS, 128), F32),
        ),
        in_specs=[HBM] * 2,
        out_specs=(VMEM, VMEM),
        scratch_shapes=[
            pltpu.SMEM((2,), jnp.int32),
            pltpu.VMEM(queries.shape, BF16),
            pltpu.VMEM((BLOCK_ROWS, 128), F32),
            pltpu.SemaphoreType.DMA((2,)),
        ],
        compiler_params=WHOLE,
        name="prep",
    )(prompt_ids, queries)
    gathered = lax.all_to_all(blocks, PEERS, 0, 0, tiled=True)
    held = lax.optimization_barrier((suffix_cache, step_kv, blocks, prompt_ids, prior_weights))
    pair_cache = lax.ppermute(held[0], "core", swap)
    far_cache = lax.ppermute(held[0], DOM, cross)
    pair_kv = lax.ppermute(held[1], "core", swap)
    far_kv = lax.ppermute(held[1], DOM, cross)
    plane = jax.ShapeDtypeStruct((PLANE, 128), F32)
    level, dot, facts = pl.pallas_call(
        first_kernel,
        out_shape=(plane, plane, jax.ShapeDtypeStruct((8, 128), F32)),
        in_specs=[SMEM] * 2 + [VMEM] * 4,
        out_specs=(VMEM,) * 3,
        compiler_params=PARAMS,
        cost_estimate=LONG,
        name="first_local",
    )(held[3], held[4], rows, suffix_cache, step_kv, weight_rows)
    parts = pl.pallas_call(
        prefix_kernel,
        out_shape=jax.ShapeDtypeStruct((RING, PART_ROWS, 128), BF16),
        in_specs=[VMEM] + [HBM] * 4 + [VMEM] * 4,
        out_specs=VMEM,
        scratch_shapes=[
            pltpu.VMEM((4, *prefix_cache.shape), BF16),
            pltpu.SemaphoreType.DMA((4,)),
        ],
        compiler_params=WHOLE,
        name="prefix",
    )(
        gathered, prefix_cache, pair_prefix, next_prefix, cross_prefix, facts, weight_rows, level, dot
    )
    received = lax.all_to_all(parts, PEERS, 0, 0, tiled=True)
    copied, carried, mean, second_level = pl.pallas_call(
        second_kernel,
        out_shape=(
            jax.ShapeDtypeStruct(suffix_cache.shape, BF16),
            jax.ShapeDtypeStruct((2, 2, 256), BF16),
            jax.ShapeDtypeStruct((32, 128), F32),
            jax.ShapeDtypeStruct((8, 128), F32),
        ),
        in_specs=[HBM] + [VMEM] * 7,
        out_specs=(VMEM,) * 4,
        scratch_shapes=[pltpu.SMEM((2,), jnp.int32), pltpu.SemaphoreType.DMA],
        compiler_params=PARAMS,
        name="second_local",
    )(ancestors, rows, suffix_cache, pair_cache, far_cache, step_kv, pair_kv, far_kv)
    attn, send = pl.pallas_call(
        finish_kernel,
        out_shape=(
            jax.ShapeDtypeStruct((2, 2048), BF16),
            jax.ShapeDtypeStruct((4 * NT, 8, 128), F32),
        ),
        in_specs=[VMEM] * 4,
        out_specs=(VMEM,) * 2,
        scratch_shapes=[pltpu.VMEM((2, 2048), F32)],
        compiler_params=PARAMS,
        name="finish",
    )(received, mean, second_level, weight_rows)
    lines = lax.all_to_all(send, SHARE + ("tp",), 0, 0, tiled=True)
    log_weights, twist_two = pl.pallas_call(
        weight_kernel,
        out_shape=(jax.ShapeDtypeStruct((2,), F32), jax.ShapeDtypeStruct((2,), F32)),
        in_specs=[VMEM],
        out_specs=(SMEM, SMEM),
        compiler_params=PARAMS,
        name="weights",
    )(lines)
    return (log_weights, copied, carried, attn, twist_two)


def solution(mesh):
    inner = Mesh(mesh.devices.reshape(2, 2, 2, 2, 2, NC, NT), WIDE)
    placed = (
        P(None, None, DOM, "tp"),
        P(DOM, None, None, "tp"),
        P(DOM, None, "tp"),
        P(DOM, None, None, "tp"),
        P("tp"),
        P(DOM),
        P(DOM),
        P(DOM),
    )
    return jax.shard_map(
        body,
        mesh=inner,
        in_specs=placed,
        out_specs=(
            P(DOM),
            P(DOM, None, None, "tp"),
            P(DOM, None, "tp"),
            P(DOM, "tp"),
            P(DOM),
        ),
        check_vma=False,
    )
```

time: 78 us -> 64.6 us (0.83)
  starting transfers between devices: 37.6 us -> 25 us
  waiting for transfers between devices: 21.6 us -> 9.29 us
  blocking collectives: 0 us -> 12.2 us
  Pallas kernels: 14 us -> 13 us
  local copies, waits for them, and re-layouts: 2.89 us -> 3.8 us
    all_to_all x0 -> x1, blocking collectives: none -> 12.2 us  [body(): lines = lax.all_to_all(send, SHARE + ('tp',), 0, 0, tiled=True)]
    all_to_all x1 -> x0, starting transfers between devices: 9.73 us -> none  [body(): lines = lax.all_to_all(send, ('core', 'tp'), 0, 0, tiled=True)]
    all_to_all x1, waiting for transfers between devices: 11.7 us -> 2.75 us  [body(): received = lax.all_to_all(parts, PEERS, 0, 0, tiled=True)]
    all_to_all x1 -> x0, waiting for transfers between devices: 4.36 us -> none  [body(): lines = lax.all_to_all(send, ('core', 'tp'), 0, 0, tiled=True)]
    ppermute x5 -> x7, waiting for transfers between devices: 0.01 us -> 2.71 us  [the longest x1 2.69 us: body(): far_kv = lax.ppermute(held[1], DOM, cross)]
    all_to_all x1, starting transfers between devices: 7.89 us -> 6.11 us  [body(): received = lax.all_to_all(parts, PEERS, 0, 0, tiled=True)]
    all_to_all x1, starting transfers between devices: 12 us -> 10.3 us  [body(): gathered = lax.all_to_all(blocks, PEERS, 0, 0, tiled=True)]
    all_to_all x1, waiting for transfers between devices: 5.54 us -> 3.84 us  [body(): gathered = lax.all_to_all(blocks, PEERS, 0, 0, tiled=True)]
  transfers between devices with their start and end apart: 8 -> 9, of which waited for: 3 -> 3; matrix products, arithmetic and copies ran while one was open for 2% -> 0% of each run, Pallas kernels for 13% -> 17%
where the time goes in v3:
time: 64.6 us; the launch traced here: 64.1 us
  starting transfers between devices  25 us (39%)
  Pallas kernels  13 us (20%)
  blocking collectives  12.2 us (19%)
  waiting for transfers between devices  9.29 us (14%)
  local copies, waits for them, and re-layouts  3.8 us (6%)
  between operations  0.82 us (1%)
    all_to_all x1, blocking collectives, body(): lines = lax.all_to_all(send, SHARE + ('tp',), 0, 0, tiled=True)  12.2 us
    all_to_all x1, starting transfers between devices, body(): gathered = lax.all_to_all(blocks, PEERS, 0, 0, tiled=True)  10.3 us
    all_to_all x1, starting transfers between devices, body(): received = lax.all_to_all(parts, PEERS, 0, 0, tiled=True)  6.11 us
    pallas_call x1, Pallas kernels, body(): pl.pallas_call(prefix_kernel, out_shape=jax.ShapeDtypeStruct((RING, PART_...  5.7 us
    all_to_all x1, waiting for transfers between devices, body(): gathered = lax.all_to_all(blocks, PEERS, 0, 0, tiled=True)  3.84 us
    unnamed x28, local copies, waits for them, and re-layouts  3.8 us
    all_to_all x1, waiting for transfers between devices, body(): received = lax.all_to_all(parts, PEERS, 0, 0, tiled=True)  2.75 us
    ppermute x1, waiting for transfers between devices, body(): far_kv = lax.ppermute(held[1], DOM, cross)  2.69 us
  transfers between devices with their start and end apart: 9, of which 3 were waited for; matrix products, arithmetic and copies ran while one was open for 0% of the time, Pallas kernels for 17%

profile of v3, /device:TPU:1, one launch (start us, length us, event | category | flops | bytes accessed | tf_op | source)
XLA Modules:
  0.0 64.1 jit_solution(17157232433802836993)
XLA Ops:
  0.6 2.1 %collective-permute-start.1 = (bf16[4,2,128,256]{3,2,1,0:T(8,128)(2,1)}, bf16[4,2,128,256]{3,2,1,0:T(8,128)(2,1)S(1)}, u32[]{:S(2)}, u32[]{:S(2)}) collective-permute-start(bf16[4,2,128,256]{3,2,1,0:T(8,128)(2,1)} %own_hbm.1), channel_id=1, source_target_pairs={{0,8},{8,0},{1,9},{9,1},{2,10},{10,2},{3,11},{11,3},{4,12},{12,4},... | collective-permute-start | bytes 1572872 | tf_op jit(solution)/shard_map/ppermute | solution.py:369
  2.8 1.3 %collective-permute-start = (bf16[4,2,128,256]{3,2,1,0:T(8,128)(2,1)}, bf16[4,2,128,256]{3,2,1,0:T(8,128)(2,1)}, u32[]{:S(2)}, u32[]{:S(2)}) collective-permute-start(bf16[4,2,128,256]{3,2,1,0:T(8,128)(2,1)} %own_hbm.1), channel_id=1, source_target_pairs={{0,4},{4,0},{1,5},{5,1},{2,6},{6,2},{3,7},{7,3},{8,12},{12,8},{9,1... | collective-permute-start | bytes 1572872 | tf_op jit(solution)/shard_map/ppermute | solution.py:370
  4.1 1.5 %prep.1 = (bf16[16,72,128]{2,1,0:T(8,128)(2,1)}, f32[64,128]{1,0:T(8,128)}) custom-call(s32[2]{0:T(128)} %ids_ref, bf16[2,2,2048]{2,1,0:T(2,128)(2,1)} %q_hbm.1), custom_call_target="tpu_custom_call" | custom-call | tf_op jit(solution)/shard_map/prep/pallas_call | solution.py:374
  5.6 10.3 %all-to-all-start = ((bf16[16,72,128]{2,1,0:T(8,128)(2,1)}), bf16[16,72,128]{2,1,0:T(8,128)(2,1)S(1)}, u32[]{:S(2)}, u32[]{:S(2)}) async-start(bf16[16,72,128]{2,1,0:T(8,128)(2,1)} %get-tuple-element.22), calls=%async_computation | async-start | bytes 589824 | tf_op jit(solution)/shard_map/all_to_all | solution.py:391
  15.9 2.0 %collective-permute-start.4 = (bf16[2,2,512,256]{3,2,1,0:T(8,128)(2,1)}, bf16[2,2,512,256]{3,2,1,0:T(8,128)(2,1)S(1)}, u32[]{:S(2)}, u32[]{:S(2)}) collective-permute-start(bf16[2,2,512,256]{3,2,1,0:T(8,128)(2,1)} %own_ref.3), channel_id=1, source_target_pairs={{4,8},{12,16},{20,24},{28,32},{36,40},{44,48},{52,56},{60,64},{68,... | collective-permute-start | bytes 3145736 | tf_op jit(solution)/shard_map/ppermute | solution.py:394
  17.9 0.1 collective-permute-start.3
  18.0 0.5 collective-permute-start.2
  18.5 0.6 copy-done.9
  19.2 1.2 %copy-done = bf16[2,2,512,256]{3,2,1,0:T(8,128)(2,1)S(1)} copy-done((bf16[2,2,512,256]{3,2,1,0:T(8,128)(2,1)S(1)}, bf16[2,2,512,256]{3,2,1,0:T(8,128)(2,1)}, u32[]{:S(2)}) %copy-start) | copy-done | bytes 1048600
  20.4 1.7 %first_local.1 = (f32[4,128]{1,0:T(4,128)S(1)}, f32[4,128]{1,0:T(4,128)S(1)}, f32[8,128]{1,0:T(8,128)S(1)}) custom-call(s32[2]{0:T(128)S(1)} %copy-done.9, f32[2]{0:T(128)S(1)} %copy-done.11, f32[64,128]{1,0:T(8,128)S(1)} %copy-done.2, bf16[2,2,512,256]{3,2,1,0:T(8,128)(2,1)S(1)} %copy-done, bf16[2,2,2,256]{3,2,1,0:T(2,128)(2,1)S(1)} %copy-done.5, ...), custom_call_target="tpu_custom_call" | custom-call | flops 20000000000 | bytes 80000000 | tf_op jit(solution)/shard_map/first_local/pallas_call | solution.py:398
  22.1 0.6 copy-done.6
  22.7 0.6 copy-done.7
  23.3 3.8 %all-to-all-done.q_ref = bf16[16,72,128]{2,1,0:T(8,128)(2,1)S(1)} async-done(((bf16[16,72,128]{2,1,0:T(8,128)(2,1)}), bf16[16,72,128]{2,1,0:T(8,128)(2,1)S(1)}, u32[]{:S(2)}, u32[]{:S(2)}) %all-to-all-start) | async-done | bytes 294944 | tf_op jit(solution)/shard_map/all_to_all | solution.py:391
  27.1 0.7 %copy-done.12 = bf16[16,72,128]{2,1,0:T(8,128)(2,1)} copy-done((bf16[16,72,128]{2,1,0:T(8,128)(2,1)}, bf16[16,72,128]{2,1,0:T(8,128)(2,1)S(1)}, u32[]{:S(2)}) %copy-start.12) | copy-done | bytes 294936
  27.8 5.7 %prefix.1 = bf16[16,56,128]{2,1,0:T(8,128)(2,1)} custom-call(bf16[16,72,128]{2,1,0:T(8,128)(2,1)} %copy-done.12, bf16[4,2,128,256]{3,2,1,0:T(8,128)(2,1)} %own_hbm.1, bf16[4,2,128,256]{3,2,1,0:T(8,128)(2,1)} %collective-permute-done.pair_hbm, bf16[4,2,128,256]{3,2,1,0:T(8,128)(2,1)} %copy-done.13, bf16[4,2,128,256]{3,2,1,0:T(8,128)(2,1)} %collective-permute-done.2.cross_hbm, ...), custom_call_target="tpu_custom_call" | custom-call | tf_op jit(solution)/shard_map/prefix/pallas_call | solution.py:407
  33.5 6.1 %all-to-all-start.1 = ((bf16[16,56,128]{2,1,0:T(8,128)(2,1)}), bf16[16,56,128]{2,1,0:T(8,128)(2,1)S(1)}, u32[]{:S(2)}, u32[]{:S(2)}) async-start(bf16[16,56,128]{2,1,0:T(8,128)(2,1)} %prefix.1), calls=%async_computation.1 | async-start | bytes 458752 | tf_op jit(solution)/shard_map/all_to_all | solution.py:421
  39.7 2.5 %collective-permute-start.6 = (bf16[2,2,2,256]{3,2,1,0:T(2,128)(2,1)S(1)}, bf16[2,2,2,256]{3,2,1,0:T(2,128)(2,1)S(1)}, u32[]{:S(2)}, u32[]{:S(2)}) collective-permute-start(bf16[2,2,2,256]{3,2,1,0:T(2,128)(2,1)S(1)} %copy-done.5), channel_id=1, source_target_pairs={{4,8},{12,16},{20,24},{28,32},{36,40},{44,48},{52,56},{60,64},{68,... | collective-permute-start | bytes 12296 | tf_op jit(solution)/shard_map/ppermute | solution.py:396
  42.2 0.1 collective-permute-start.5
  42.3 2.7 %collective-permute-done.6.far_kv_ref = bf16[2,2,2,256]{3,2,1,0:T(2,128)(2,1)S(1)} collective-permute-done((bf16[2,2,2,256]{3,2,1,0:T(2,128)(2,1)S(1)}, bf16[2,2,2,256]{3,2,1,0:T(2,128)(2,1)S(1)}, u32[]{:S(2)}, u32[]{:S(2)}) %collective-permute-start.6) | collective-permute-done | bytes 4128 | tf_op jit(solution)/shard_map/ppermute | solution.py:396
  45.0 1.8 %second_local.1 = (bf16[2,2,512,256]{3,2,1,0:T(8,128)(2,1)}, bf16[2,2,256]{2,1,0:T(2,128)(2,1)}, f32[32,128]{1,0:T(8,128)S(1)}, f32[8,128]{1,0:T(8,128)S(1)}) custom-call(s32[2]{0:T(128)S(1)} %copy-done.10, f32[64,128]{1,0:T(8,128)S(1)} %copy-done.2, bf16[2,2,512,256]{3,2,1,0:T(8,128)(2,1)S(1)} %copy-done.1, ...), custom_call_target="tpu_custom_call" | custom-call | tf_op jit(solution)/shard_map/second_local/pallas_call | solution.py:422
  46.9 2.7 %all-to-all-done.1.part_ref = bf16[16,56,128]{2,1,0:T(8,128)(2,1)S(1)} async-done(((bf16[16,56,128]{2,1,0:T(8,128)(2,1)}), bf16[16,56,128]{2,1,0:T(8,128)(2,1)S(1)}, u32[]{:S(2)}, u32[]{:S(2)}) %all-to-all-start.1) | async-done | bytes 229408 | tf_op jit(solution)/shard_map/all_to_all | solution.py:421
  49.6 1.0 %finish.1 = (bf16[2,2048]{1,0:T(2,128)(2,1)}, f32[16,8,128]{2,1,0:T(8,128)S(1)}) custom-call(bf16[16,56,128]{2,1,0:T(8,128)(2,1)S(1)} %all-to-all-done.1.part_ref, f32[32,128]{1,0:T(8,128)S(1)} %get-tuple-element.31.mean_ref, f32[8,128]{1,0:T(8,128)S(1)} %get-tuple-element.32.level_ref, f32[16,128]{1,0:T(8,128)S(1)} %bitcast.3), custom_call_target="tpu_custom_call" | custom-call | tf_op jit(solution)/shard_map/finish/pallas_call | solution.py:436
  50.6 12.2 %all_to_all.15.all_ref = f32[16,8,128]{2,1,0:T(8,128)S(1)} all-to-all(f32[16,8,128]{2,1,0:T(8,128)S(1)} %get-tuple-element.33), channel_id=1, replica_groups=mesh['z2'=2,'z1'=2,'z0'=2,'x1'=2,'x0'=2,'core'=2,'tp'=4] {'x0','core','tp'}, dimensions={0} | all-to-all | bytes 131072 | tf_op jit(solution)/shard_map/all_to_all | solution.py:448
  62.8 1.3 %weights.1 = (f32[2]{0:T(128)}, f32[2]{0:T(128)}) custom-call(f32[16,8,128]{2,1,0:T(8,128)S(1)} %all_to_all.15.all_ref), custom_call_target="tpu_custom_call" | custom-call | tf_op jit(solution)/shard_map/weights/pallas_call | solution.py:449
  (29 shorter events, 0.1 us)
Async XLA Ops:
  0.6 17.4 %collective-permute-start.1 = (bf16[4,2,128,256]{3,2,1,0:T(8,128)(2,1)}, bf16[4,2,128,256]{3,2,1,0:T(8,128)(2,1)S(1)}, u32[]{:S(2)}, u32[]{:S(2)}) collective-permute-start(bf16[4,2,128,256]{3,2,1,0:T(8,128)(2,1)} %own_hbm.1), channel_id=1, source_target_pairs={{0,8},{8,0},{1,9},{9,1},{2,10},{10,2},{3,11},{11,3},{4,12},{12,4},... | collective-permute-start | bytes 1572872 | tf_op jit(solution)/shard_map/ppermute | solution.py:369
  2.8 20.5 %collective-permute-start = (bf16[4,2,128,256]{3,2,1,0:T(8,128)(2,1)}, bf16[4,2,128,256]{3,2,1,0:T(8,128)(2,1)}, u32[]{:S(2)}, u32[]{:S(2)}) collective-permute-start(bf16[4,2,128,256]{3,2,1,0:T(8,128)(2,1)} %own_hbm.1), channel_id=1, source_target_pairs={{0,4},{4,0},{1,5},{5,1},{2,6},{6,2},{3,7},{7,3},{8,12},{12,8},{9,1... | collective-permute-start | bytes 1572872 | tf_op jit(solution)/shard_map/ppermute | solution.py:370
  5.6 12.9 %copy-start.2 = (f32[64,128]{1,0:T(8,128)S(1)}, f32[64,128]{1,0:T(8,128)}, u32[]{:S(2)}) copy-start(f32[64,128]{1,0:T(8,128)} %get-tuple-element.25.q_ref) | copy-start | bytes 98308
  5.6 12.9 %copy-start.3 = (f32[2048]{0:T(1024)S(1)}, f32[2048]{0:T(1024)}, u32[]{:S(2)}) copy-start(f32[2048]{0:T(1024)} %param.12) | copy-start | bytes 24580
  5.6 12.9 %copy-start.5 = (bf16[2,2,2,256]{3,2,1,0:T(2,128)(2,1)S(1)}, bf16[2,2,2,256]{3,2,1,0:T(2,128)(2,1)}, u32[]{:S(2)}) copy-start(bf16[2,2,2,256]{3,2,1,0:T(2,128)(2,1)} %kv_ref.3) | copy-start | bytes 12292
  5.6 21.5 %all-to-all-start = ((bf16[16,72,128]{2,1,0:T(8,128)(2,1)}), bf16[16,72,128]{2,1,0:T(8,128)(2,1)S(1)}, u32[]{:S(2)}, u32[]{:S(2)}) async-start(bf16[16,72,128]{2,1,0:T(8,128)(2,1)} %get-tuple-element.22), calls=%async_computation | async-start | bytes 589824 | tf_op jit(solution)/shard_map/all_to_all | solution.py:391
  15.9 29.1 %collective-permute-start.4 = (bf16[2,2,512,256]{3,2,1,0:T(8,128)(2,1)}, bf16[2,2,512,256]{3,2,1,0:T(8,128)(2,1)S(1)}, u32[]{:S(2)}, u32[]{:S(2)}) collective-permute-start(bf16[2,2,512,256]{3,2,1,0:T(8,128)(2,1)} %own_ref.3), channel_id=1, source_target_pairs={{4,8},{12,16},{20,24},{28,32},{36,40},{44,48},{52,56},{60,64},{68,... | collective-permute-start | bytes 3145736 | tf_op jit(solution)/shard_map/ppermute | solution.py:394
  17.9 27.1 %collective-permute-start.3 = (bf16[2,2,512,256]{3,2,1,0:T(8,128)(2,1)}, bf16[2,2,512,256]{3,2,1,0:T(8,128)(2,1)S(1)}, u32[]{:S(2)}, u32[]{:S(2)}) collective-permute-start(bf16[2,2,512,256]{3,2,1,0:T(8,128)(2,1)} %own_ref.3), channel_id=1, source_target_pairs={{0,4},{4,0},{1,5},{5,1},{2,6},{6,2},{3,7},{7,3},{8,12},{12,8},{9,1... | collective-permute-start | bytes 3145736 | tf_op jit(solution)/shard_map/ppermute | solution.py:393
  18.0 4.1 %copy-start.13 = (bf16[4,2,128,256]{3,2,1,0:T(8,128)(2,1)}, bf16[4,2,128,256]{3,2,1,0:T(8,128)(2,1)S(1)}, u32[]{:S(2)}) copy-start(bf16[4,2,128,256]{3,2,1,0:T(8,128)(2,1)S(1)} %collective-permute-done.1.next_hbm) | copy-start | bytes 1572868
  18.0 9.1 %collective-permute-start.2 = (bf16[4,2,128,256]{3,2,1,0:T(8,128)(2,1)S(1)}, bf16[4,2,128,256]{3,2,1,0:T(8,128)(2,1)}, u32[]{:S(2)}, u32[]{:S(2)}) collective-permute-start(bf16[4,2,128,256]{3,2,1,0:T(8,128)(2,1)S(1)} %collective-permute-done.1.next_hbm), channel_id=1, source_target_pairs={{0,4},{4,0},{1,5},{5,1},{2,6},{6,2},{3,7},{7,3},{8,12},{12,8},{9,1... | collective-permute-start | bytes 1572872 | tf_op jit(solution)/shard_map/ppermute | solution.py:371
  18.5 0.7 %copy-start.9 = (s32[2]{0:T(128)S(1)}, s32[2]{0:T(128)}, u32[]{:S(2)}) copy-start(s32[2]{0:T(128)} %ids_ref) | copy-start | bytes 28
  18.5 0.7 %copy-start.11 = (f32[2]{0:T(128)S(1)}, f32[2]{0:T(128)}, u32[]{:S(2)}) copy-start(f32[2]{0:T(128)} %prior_ref) | copy-start | bytes 28
  19.2 1.2 %copy-start = (bf16[2,2,512,256]{3,2,1,0:T(8,128)(2,1)S(1)}, bf16[2,2,512,256]{3,2,1,0:T(8,128)(2,1)}, u32[]{:S(2)}) copy-start(bf16[2,2,512,256]{3,2,1,0:T(8,128)(2,1)} %own_ref.3) | copy-start | bytes 3145732
  22.1 0.6 copy-start.6
  22.7 0.6 copy-start.7
  23.3 4.6 %copy-start.8 = (f32[4,128]{1,0:T(4,128)}, f32[4,128]{1,0:T(4,128)S(1)}, u32[]{:S(2)}) copy-start(f32[4,128]{1,0:T(4,128)S(1)} %get-tuple-element.28.dot_ref) | copy-start | bytes 6148
  27.1 0.7 %copy-start.12 = (bf16[16,72,128]{2,1,0:T(8,128)(2,1)}, bf16[16,72,128]{2,1,0:T(8,128)(2,1)S(1)}, u32[]{:S(2)}) copy-start(bf16[16,72,128]{2,1,0:T(8,128)(2,1)S(1)} %all-to-all-done.q_ref) | copy-start | bytes 884740
  27.8 17.2 %copy-start.1 = (bf16[2,2,512,256]{3,2,1,0:T(8,128)(2,1)S(1)}, bf16[2,2,512,256]{3,2,1,0:T(8,128)(2,1)}, u32[]{:S(2)}) copy-start(bf16[2,2,512,256]{3,2,1,0:T(8,128)(2,1)} %own_ref.3) | copy-start | bytes 3145732
  33.5 11.5 %copy-start.10 = (s32[2]{0:T(128)S(1)}, s32[2]{0:T(128)}, u32[]{:S(2)}) copy-start(s32[2]{0:T(128)} %anc_hbm.1) | copy-start | bytes 28
  33.5 16.1 %all-to-all-start.1 = ((bf16[16,56,128]{2,1,0:T(8,128)(2,1)}), bf16[16,56,128]{2,1,0:T(8,128)(2,1)S(1)}, u32[]{:S(2)}, u32[]{:S(2)}) async-start(bf16[16,56,128]{2,1,0:T(8,128)(2,1)} %prefix.1), calls=%async_computation.1 | async-start | bytes 458752 | tf_op jit(solution)/shard_map/all_to_all | solution.py:421
  39.7 5.3 %collective-permute-start.6 = (bf16[2,2,2,256]{3,2,1,0:T(2,128)(2,1)S(1)}, bf16[2,2,2,256]{3,2,1,0:T(2,128)(2,1)S(1)}, u32[]{:S(2)}, u32[]{:S(2)}) collective-permute-start(bf16[2,2,2,256]{3,2,1,0:T(2,128)(2,1)S(1)} %copy-done.5), channel_id=1, source_target_pairs={{4,8},{12,16},{20,24},{28,32},{36,40},{44,48},{52,56},{60,64},{68,... | collective-permute-start | bytes 12296 | tf_op jit(solution)/shard_map/ppermute | solution.py:396
  42.2 2.8 %collective-permute-start.5 = (bf16[2,2,2,256]{3,2,1,0:T(2,128)(2,1)S(1)}, bf16[2,2,2,256]{3,2,1,0:T(2,128)(2,1)S(1)}, u32[]{:S(2)}, u32[]{:S(2)}) collective-permute-start(bf16[2,2,2,256]{3,2,1,0:T(2,128)(2,1)S(1)} %copy-done.5), channel_id=1, source_target_pairs={{0,4},{4,0},{1,5},{5,1},{2,6},{6,2},{3,7},{7,3},{8,12},{12,8},{9,1... | collective-permute-start | bytes 12296 | tf_op jit(solution)/shard_map/ppermute | solution.py:395
  45.0 4.6 %copy-start.4 = (f32[2048]{0:T(1024)S(1)}, f32[2048]{0:T(1024)}, u32[]{:S(2)}) copy-start(f32[2048]{0:T(1024)} %param.12) | copy-start | bytes 24580

commit v4 on v3

--- a/solution.py
+++ b/solution.py
@@ -21,6 +21,8 @@
 FACTOR = 1.0 / math.sqrt(HEAD_DIM)
 FACTOR2 = FACTOR * math.log2(math.e)
 Q_ROWS = 64
+SUF = 512
+TAIL = 16
 ID_ROWS = 8
 BLOCK_ROWS = Q_ROWS + ID_ROWS
 OUT_ROWS = 32
@@ -34,6 +36,7 @@
 HBM = pl.BlockSpec(memory_space=pltpu.HBM)
 LONG = pl.CostEstimate(flops=2 * 10**10, bytes_accessed=8 * 10**7, transcendentals=0)
 PARAMS = pltpu.CompilerParams(vmem_limit_bytes=16 * 1024 * 1024)
+MOST = pltpu.CompilerParams(vmem_limit_bytes=52 * 1024 * 1024)
 WHOLE = pltpu.CompilerParams(vmem_limit_bytes=60 * 1024 * 1024)
 
 
@@ -72,30 +75,16 @@
     own_ref[...] = rows_ref[0:Q_ROWS, :]
 
 
-def prefix_kernel(
-    q_ref, own_hbm, pair_hbm, next_hbm, cross_hbm, facts_ref, w_ref, level_ref, dot_ref, out_ref, cache_ref, sems
-):
-    copies = [
-        pltpu.make_async_copy(src, cache_ref.at[n], sems.at[n])
-        for n, src in enumerate((own_hbm, pair_hbm, next_hbm, cross_hbm))
-    ]
-    for copy in copies:
-        copy.start()
-    for copy in copies:
-        copy.wait()
-    keys, values = [], []
-    for kv in range(2):
+def prefix_kernel(q_ref, own_ref, pair_ref, next_ref, cross_ref, local_ref, w_ref, out_ref):
+    caches = (own_ref, pair_ref, next_ref, cross_ref)
+
+    def table(kind, kv):
         cols = slice(kv * 128, (kv + 1) * 128)
-        for kind, into in ((0, keys), (1, values)):
-            into.append(
-                jnp.concatenate(
-                    [
-                        jnp.concatenate([cache_ref[n, g, kind, :, cols] for n in range(4)], axis=0)
-                        for g in range(PROMPTS)
-                    ],
-                    axis=1,
-                )
-            )
+        return jnp.concatenate(
+            [jnp.concatenate([cache[g, kind, :, cols] for cache in caches], axis=0) for g in range(PROMPTS)],
+            axis=1,
+        )
+
     count = CHUNK * 32
     shape = (CHUNK, 32, 128)
     row_id = lax.broadcasted_iota(jnp.int32, shape, 1)
@@ -103,7 +92,7 @@
     spot = row_id + 32 * (lax.broadcasted_iota(jnp.int32, shape, 0) % 4)
     levels, dots, heads, bodies = [], [], [], []
     head_row = lax.broadcasted_iota(jnp.int32, (CHUNK, 8, 128), 1)
-    facts = facts_ref[...][None]
+    facts = local_ref[0:8, :][None]
     for start in range(0, RING, CHUNK):
         block = q_ref[start : start + CHUNK].astype(F32)
         both = block[:, Q_ROWS:BLOCK_ROWS].reshape(CHUNK * ID_ROWS, 128)
@@ -122,11 +111,11 @@
         for kv in range(2):
             q = block[:, kv * 32 : (kv + 1) * 32].reshape(count, 128)
             spread = jnp.concatenate([jnp.where(pick, q, 0.0).astype(BF16) for pick in picks], axis=1)
-            scores = lax.dot_general(spread, keys[kv], NT_DIMS, preferred_element_type=F32)
+            scores = lax.dot_general(spread, table(0, kv), NT_DIMS, preferred_element_type=F32)
             top = jnp.max(scores, axis=1, keepdims=True)
             weights = jnp.exp2((scores - top) * FACTOR2)
             total = jnp.sum(weights, axis=1, keepdims=True)
-            sums = jnp.dot(weights.astype(BF16), values[kv], preferred_element_type=F32)
+            sums = jnp.dot(weights.astype(BF16), table(1, kv), preferred_element_type=F32)
             num = sums[:, 384:512]
             for g in (2, 1, 0):
                 num = jnp.where(picks[g], sums[:, g * 128 : (g + 1) * 128], num)
@@ -153,9 +142,10 @@
         head = jnp.where(head_row == 0, line[:, None, :], facts)
         heads.append(head)
     level, dot = jnp.concatenate(levels, axis=0), jnp.concatenate(dots, axis=0)
-    top = jnp.maximum(level, level_ref[...])
-    old, new = jnp.exp(level - top), jnp.exp(level_ref[...] - top)
-    dot = (dot * old + dot_ref[...] * new) / (old + new)
+    my_level, my_dot = local_ref[8 : 8 + PLANE, :], local_ref[8 + PLANE : 8 + 2 * PLANE, :]
+    top = jnp.maximum(level, my_level)
+    old, new = jnp.exp(level - top), jnp.exp(my_level - top)
+    dot = (dot * old + my_dot * new) / (old + new)
     level = top + jnp.log(old + new)
     for start, mean, head in zip(range(0, RING, CHUNK), bodies, heads):
         common = jnp.concatenate([*split(level), dot], axis=0)
@@ -187,9 +177,19 @@
     return num / total, top * FACTOR + jnp.log(total)
 
 
-def first_kernel(ids_ref, prior_ref, q_ref, own_ref, kv_ref, w_ref, level_ref, dot_ref, facts_ref):
+def first_kernel(ids_ref, prior_ref, q_ref, kv_ref, w_ref, cache_hbm, out_ref, wide_hbm, wide_ref, sems):
+    taken = pltpu.make_async_copy(cache_hbm, wide_ref.at[:, :, 0:SUF, :], sems.at[0])
+    taken.start()
     queries = q_ref[...]
     step_kv = kv_ref[...].astype(F32)
+    tail_row = lax.broadcasted_iota(jnp.int32, (TAIL, kv_ref.shape[-1]), 0)
+    for p in range(2):
+        for kind in range(2):
+            line = step_kv[p, 0, kind : kind + 1, :]
+            wide_ref[p, kind, SUF : SUF + TAIL, :] = jnp.where(tail_row == 0, line, 0.0).astype(BF16)
+    taken.wait()
+    given = pltpu.make_async_copy(wide_ref, wide_hbm, sems.at[1])
+    given.start()
     means, tops = [], []
     for p in range(2):
         for kv in range(2):
@@ -197,8 +197,8 @@
             row = kv * 32 + p * 16
             mean, top = local_attend(
                 queries[row : row + 8],
-                own_ref[p, 0, :, cols],
-                own_ref[p, 1, :, cols],
+                wide_ref[p, 0, 0:SUF, cols],
+                wide_ref[p, 1, 0:SUF, cols],
                 [(step_kv[p, 0, 0:1, cols], step_kv[p, 0, 1:2, cols])],
             )
             means.append(mean)
@@ -213,8 +213,8 @@
     dot_row = jnp.sum(jnp.where(lane_id == spot, dot, 0.0), axis=0, keepdims=True)
     here = lax.broadcasted_iota(jnp.int32, (PLANE, 128), 0) == place // 4
     here = here & (lanes((PLANE, 128)) // 32 == place % 4)
-    level_ref[...] = jnp.where(here, level_row, -1e30)
-    dot_ref[...] = jnp.where(here, dot_row, 0.0)
+    out_ref[8 : 8 + PLANE, :] = jnp.where(here, level_row, -1e30)
+    out_ref[8 + PLANE : 8 + 2 * PLANE, :] = jnp.where(here, dot_row, 0.0)
     slot = lanes((8, 128)) // 16 - (place % 4) * 2
     prior = jnp.where(slot == 0, prior_ref[0], jnp.where(slot == 1, prior_ref[1], 0.0))
     first, second = ids_ref[0].astype(F32), ids_ref[1].astype(F32)
@@ -223,21 +223,19 @@
     facts = jnp.where(row_id == 4, ids, 0.0)
     for r, part in enumerate(split(prior)):
         facts = jnp.where(row_id == r + 1, part, facts)
-    facts_ref[...] = facts
+    out_ref[0:8, :] = facts
+    given.wait()
 
 
 def second_kernel(
-    anc_hbm, q_ref, own_ref, pair_ref, far_ref, kv_ref, pair_kv_ref, far_kv_ref,
-    copied_ref, carried_ref, mean_ref, level_ref, anc_ref, sem,
+    anc_ref, q_ref, own_hbm, pair_hbm, far_hbm, kv_ref, copied_ref, carried_ref, mean_ref, wide_ref, sems
 ):
-    copy = pltpu.make_async_copy(anc_hbm, anc_ref, sem)
-    copy.start()
-    copy.wait()
     core = lax.axis_index("core")
     base = 0
     for axis in DOM:
         base = base * 2 + lax.axis_index(axis)
     base = base * 2 - 2
+    choices = []
     for slot in range(2):
         pos = anc_ref[slot] - base
         side, which = pos // 2, pos % 2
@@ -245,17 +243,18 @@
         from_pair = side == jnp.where(core == 0, 2, 0)
         from_far = side == jnp.where(core == 0, 0, 2)
         for j in range(2):
-            for flag, cache, kvs in (
-                (from_own, own_ref, kv_ref),
-                (from_pair, pair_ref, pair_kv_ref),
-                (from_far, far_ref, far_kv_ref),
-            ):
-
-                @pl.when(flag & (which == j))
-                def _():
-                    copied_ref[slot] = cache[j]
-                    carried_ref[slot] = kvs[j, 0]
-
+            for flag, cache in ((from_own, own_hbm), (from_pair, pair_hbm), (from_far, far_hbm)):
+                copy = pltpu.make_async_copy(cache.at[j], wide_ref.at[slot], sems.at[slot])
+                choices.append((flag & (which == j), copy))
+    for flag, copy in choices:
+        pl.when(flag)(copy.start)
+    for flag, copy in choices:
+        pl.when(flag)(copy.wait)
+    for slot in range(2):
+        copied_ref[slot] = wide_ref[slot, :, 0:SUF, :]
+        for kind in range(2):
+            tail = wide_ref[slot, kind, SUF : SUF + TAIL, :].astype(F32)
+            carried_ref[slot, kind : kind + 1, :] = tail[0:1].astype(BF16)
     queries = q_ref[...]
     step_kv = kv_ref[...].astype(F32)
     carried = carried_ref[...].astype(F32)
@@ -266,8 +265,8 @@
             row = kv * 32 + p * 16 + 8
             mean, top = local_attend(
                 queries[row : row + 8],
-                copied_ref[p, 0, :, cols],
-                copied_ref[p, 1, :, cols],
+                wide_ref[p, 0, 0:SUF, cols],
+                wide_ref[p, 1, 0:SUF, cols],
                 [
                     (carried[p, 0:1, cols], carried[p, 1:2, cols]),
                     (step_kv[p, 1, 0:1, cols], step_kv[p, 1, 1:2, cols]),
@@ -278,22 +277,22 @@
     top = jnp.concatenate(tops, axis=0)
     row_id = lax.broadcasted_iota(jnp.int32, (32, 128), 0)
     row = jnp.sum(jnp.where(lanes((32, 128)) == row_id, top, 0.0), axis=0, keepdims=True)
-    level_ref[...] = jnp.broadcast_to(row, (8, 128))
-
-
-def finish_kernel(part_ref, mean_ref, level_ref, w_ref, out_ref, send_ref, wide_ref):
+    mean_ref[32:40, :] = jnp.broadcast_to(row, (8, 128))
+
+
+def finish_kernel(part_ref, mean_ref, w_ref, out_ref, send_ref, wide_ref):
     parts = part_ref[...].astype(F32)
     heads = parts[:, OUT_ROWS : OUT_ROWS + 8]
     head_row = lax.broadcasted_iota(jnp.int32, heads.shape, 1)
     theirs = jnp.sum(jnp.where(head_row == 0, heads, 0.0), axis=1)
     theirs = theirs + pltpu.roll(theirs, 96, 1) + pltpu.roll(theirs, 64, 1)
-    mine = level_ref[0:1, :]
+    mine = mean_ref[32:33, :]
     top = jnp.maximum(jnp.max(theirs, axis=0, keepdims=True), mine)
     scale = jnp.exp(theirs - top)
     my_scale = jnp.exp(mine - top)
     inverse = 1.0 / (jnp.sum(scale, axis=0, keepdims=True) + my_scale)
     table = jnp.concatenate([scale * inverse, jnp.broadcast_to(my_scale * inverse, (128 - RING, 128))], axis=0).T
-    attn = mean_ref[...] * table[0:32, RING : RING + 1]
+    attn = mean_ref[0:32, :] * table[0:32, RING : RING + 1]
     for i in range(RING):
         attn = attn + table[0:32, i : i + 1] * parts[i, 0:OUT_ROWS]
     w = w_ref[...]
@@ -389,62 +388,60 @@
         name="prep",
     )(prompt_ids, queries)
     gathered = lax.all_to_all(blocks, PEERS, 0, 0, tiled=True)
-    held = lax.optimization_barrier((suffix_cache, step_kv, blocks, prompt_ids, prior_weights))
-    pair_cache = lax.ppermute(held[0], "core", swap)
-    far_cache = lax.ppermute(held[0], DOM, cross)
-    pair_kv = lax.ppermute(held[1], "core", swap)
-    far_kv = lax.ppermute(held[1], DOM, cross)
-    plane = jax.ShapeDtypeStruct((PLANE, 128), F32)
-    level, dot, facts = pl.pallas_call(
+    late_cache = lax.optimization_barrier((suffix_cache, blocks))[0]
+    local, wide_cache = pl.pallas_call(
         first_kernel,
-        out_shape=(plane, plane, jax.ShapeDtypeStruct((8, 128), F32)),
-        in_specs=[SMEM] * 2 + [VMEM] * 4,
-        out_specs=(VMEM,) * 3,
-        compiler_params=PARAMS,
+        out_shape=(
+            jax.ShapeDtypeStruct((8 + 2 * PLANE, 128), F32),
+            jax.ShapeDtypeStruct((2, 2, SUF + TAIL, 256), BF16),
+        ),
+        in_specs=[SMEM] * 2 + [VMEM] * 3 + [HBM],
+        out_specs=(VMEM, HBM),
+        scratch_shapes=[pltpu.VMEM((2, 2, SUF + TAIL, 256), BF16), pltpu.SemaphoreType.DMA((2,))],
+        compiler_params=WHOLE,
         cost_estimate=LONG,
         name="first_local",
-    )(held[3], held[4], rows, suffix_cache, step_kv, weight_rows)
+    )(prompt_ids, prior_weights, rows, step_kv, weight_rows, late_cache)
+    held = lax.optimization_barrier((wide_cache, blocks))[0]
+    pair_cache = lax.ppermute(held, "core", swap)
+    far_cache = lax.ppermute(held, DOM, cross)
     parts = pl.pallas_call(
         prefix_kernel,
         out_shape=jax.ShapeDtypeStruct((RING, PART_ROWS, 128), BF16),
-        in_specs=[VMEM] + [HBM] * 4 + [VMEM] * 4,
+        in_specs=[VMEM] * 7,
         out_specs=VMEM,
-        scratch_shapes=[
-            pltpu.VMEM((4, *prefix_cache.shape), BF16),
-            pltpu.SemaphoreType.DMA((4,)),
-        ],
-        compiler_params=WHOLE,
+        compiler_params=PARAMS,
+        cost_estimate=LONG,
         name="prefix",
     )(
-        gathered, prefix_cache, pair_prefix, next_prefix, cross_prefix, facts, weight_rows, level, dot
+        gathered, prefix_cache, pair_prefix, next_prefix, cross_prefix, local, weight_rows
     )
     received = lax.all_to_all(parts, PEERS, 0, 0, tiled=True)
-    copied, carried, mean, second_level = pl.pallas_call(
+    copied, carried, mean = pl.pallas_call(
         second_kernel,
         out_shape=(
             jax.ShapeDtypeStruct(suffix_cache.shape, BF16),
             jax.ShapeDtypeStruct((2, 2, 256), BF16),
-            jax.ShapeDtypeStruct((32, 128), F32),
-            jax.ShapeDtypeStruct((8, 128), F32),
+            jax.ShapeDtypeStruct((40, 128), F32),
         ),
-        in_specs=[HBM] + [VMEM] * 7,
-        out_specs=(VMEM,) * 4,
-        scratch_shapes=[pltpu.SMEM((2,), jnp.int32), pltpu.SemaphoreType.DMA],
-        compiler_params=PARAMS,
+        in_specs=[SMEM, VMEM] + [HBM] * 3 + [VMEM],
+        out_specs=(VMEM,) * 3,
+        scratch_shapes=[pltpu.VMEM((2, 2, SUF + TAIL, 256), BF16), pltpu.SemaphoreType.DMA((2,))],
+        compiler_params=MOST,
         name="second_local",
-    )(ancestors, rows, suffix_cache, pair_cache, far_cache, step_kv, pair_kv, far_kv)
+    )(ancestors, rows, wide_cache, pair_cache, far_cache, step_kv)
     attn, send = pl.pallas_call(
         finish_kernel,
         out_shape=(
             jax.ShapeDtypeStruct((2, 2048), BF16),
             jax.ShapeDtypeStruct((4 * NT, 8, 128), F32),
         ),
-        in_specs=[VMEM] * 4,
+        in_specs=[VMEM] * 3,
         out_specs=(VMEM,) * 2,
         scratch_shapes=[pltpu.VMEM((2, 2048), F32)],
         compiler_params=PARAMS,
         name="finish",
-    )(received, mean, second_level, weight_rows)
+    )(received, mean, weight_rows)
     lines = lax.all_to_all(send, SHARE + ("tp",), 0, 0, tiled=True)
     log_weights, twist_two = pl.pallas_call(
         weight_kernel,

time: 64.6 us -> 62.8 us (0.972)
  local copies, waits for them, and re-layouts: 3.8 us -> 0.71 us
  Pallas kernels: 13 us -> 14.5 us
  starting transfers between devices: 25 us -> 23.7 us
  blocking collectives: 12.2 us -> 13.3 us
    unnamed x28 -> x14, local copies, waits for them, and re-layouts: 3.8 us -> 0.71 us
    ppermute x4 -> x2, waiting for transfers between devices: 2.7 us -> 0.01 us  [the longest x1 0.01 us: body(): far_cache = lax.ppermute(held, DOM, cross)]
    all_to_all x1, waiting for transfers between devices: 2.75 us -> 5.37 us  [body(): received = lax.all_to_all(parts, PEERS, 0, 0, tiled=True)]
    pallas_call x1, Pallas kernels: 5.7 us -> 3.09 us  [body(): pl.pallas_call(prefix_kernel, out_shape=jax.ShapeDtypeStruct((RING, PART_...]
    pallas_call x1, Pallas kernels: 1.67 us -> 3.84 us  [body(): pl.pallas_call(first_kernel, out_shape=(jax.ShapeDtypeStruct((8 + 2 * PLA...]
    pallas_call x1, Pallas kernels: 1.83 us -> 3.78 us  [body(): pl.pallas_call(second_kernel, out_shape=(jax.ShapeDtypeStruct(suffix_cach...]
    ppermute x4 -> x2, starting transfers between devices: 4.72 us -> 3.12 us  [the longest x1 3.03 us: body(): far_cache = lax.ppermute(held, DOM, cross)]
    all_to_all x1, blocking collectives: 12.2 us -> 13.3 us  [body(): lines = lax.all_to_all(send, SHARE + ('tp',), 0, 0, tiled=True)]
  transfers between devices with their start and end apart: 9 -> 7, of which waited for: 3 -> 2; matrix products, arithmetic and copies ran while one was open for 0% -> 0% of each run, Pallas kernels for 17% -> 20%
where the time goes in v4:
time: 62.8 us; the launch traced here: 62.3 us
  starting transfers between devices  23.7 us (38%)
  Pallas kernels  14.5 us (23%)
  blocking collectives  13.3 us (21%)
  waiting for transfers between devices  9.25 us (15%)
  between operations  0.77 us (1%)
  local copies, waits for them, and re-layouts  0.71 us (1%)
    all_to_all x1, blocking collectives, body(): lines = lax.all_to_all(send, SHARE + ('tp',), 0, 0, tiled=True)  13.3 us
    all_to_all x1, starting transfers between devices, body(): gathered = lax.all_to_all(blocks, PEERS, 0, 0, tiled=True)  10.1 us
    all_to_all x1, starting transfers between devices, body(): received = lax.all_to_all(parts, PEERS, 0, 0, tiled=True)  6.62 us
    all_to_all x1, waiting for transfers between devices, body(): received = lax.all_to_all(parts, PEERS, 0, 0, tiled=True)  5.37 us
    all_to_all x1, waiting for transfers between devices, body(): gathered = lax.all_to_all(blocks, PEERS, 0, 0, tiled=True)  3.86 us
    pallas_call x1, Pallas kernels, body(): pl.pallas_call(first_kernel, out_shape=(jax.ShapeDtypeStruct((8 + 2 * PLA...  3.84 us
    pallas_call x1, Pallas kernels, body(): pl.pallas_call(second_kernel, out_shape=(jax.ShapeDtypeStruct(suffix_cach...  3.78 us
    pallas_call x1, Pallas kernels, body(): pl.pallas_call(prefix_kernel, out_shape=jax.ShapeDtypeStruct((RING, PART_...  3.09 us
  transfers between devices with their start and end apart: 7, of which 2 were waited for; matrix products, arithmetic and copies ran while one was open for 0% of the time, Pallas kernels for 20%

profile of v4, /device:TPU:1, one launch (start us, length us, event | category | flops | bytes accessed | tf_op | source)
XLA Modules:
  0.0 62.3 jit_solution(6701333147418716837)
XLA Ops:
  0.6 2.1 %collective-permute-start.1 = (bf16[4,2,128,256]{3,2,1,0:T(8,128)(2,1)}, bf16[4,2,128,256]{3,2,1,0:T(8,128)(2,1)S(1)}, u32[]{:S(2)}, u32[]{:S(2)}) collective-permute-start(bf16[4,2,128,256]{3,2,1,0:T(8,128)(2,1)} %own_ref.1), channel_id=1, source_target_pairs={{0,8},{8,0},{1,9},{9,1},{2,10},{10,2},{3,11},{11,3},{4,12},{12,4},... | collective-permute-start | bytes 1572872 | tf_op jit(solution)/shard_map/ppermute | solution.py:368
  2.8 1.3 %collective-permute-start = (bf16[4,2,128,256]{3,2,1,0:T(8,128)(2,1)}, bf16[4,2,128,256]{3,2,1,0:T(8,128)(2,1)S(1)}, u32[]{:S(2)}, u32[]{:S(2)}) collective-permute-start(bf16[4,2,128,256]{3,2,1,0:T(8,128)(2,1)} %own_ref.1), channel_id=1, source_target_pairs={{0,4},{4,0},{1,5},{5,1},{2,6},{6,2},{3,7},{7,3},{8,12},{12,8},{9,1... | collective-permute-start | bytes 1572872 | tf_op jit(solution)/shard_map/ppermute | solution.py:369
  4.1 1.5 %prep.1 = (bf16[16,72,128]{2,1,0:T(8,128)(2,1)}, f32[64,128]{1,0:T(8,128)}) custom-call(s32[2]{0:T(128)} %ids_ref.1, bf16[2,2,2048]{2,1,0:T(2,128)(2,1)} %q_hbm.1), custom_call_target="tpu_custom_call" | custom-call | tf_op jit(solution)/shard_map/prep/pallas_call | solution.py:373
  5.6 10.1 %all-to-all-start = ((bf16[16,72,128]{2,1,0:T(8,128)(2,1)}), bf16[16,72,128]{2,1,0:T(8,128)(2,1)S(1)}, u32[]{:S(2)}, u32[]{:S(2)}) async-start(bf16[16,72,128]{2,1,0:T(8,128)(2,1)} %get-tuple-element.18), calls=%async_computation | async-start | bytes 589824 | tf_op jit(solution)/shard_map/all_to_all | solution.py:390
  15.7 0.0 collective-permute-done.1.next_ref
  15.7 0.4 collective-permute-start.2
  16.1 3.8 %first_local.1 = (f32[16,128]{1,0:T(8,128)}, bf16[2,2,528,256]{3,2,1,0:T(8,128)(2,1)}) custom-call(s32[2]{0:T(128)} %ids_ref.1, f32[2]{0:T(128)} %prior_ref.1, f32[64,128]{1,0:T(8,128)} %get-tuple-element.19.q_ref, bf16[2,2,2,256]{3,2,1,0:T(2,128)(2,1)} %kv_ref.3, f32[16,128]{1,0:T(8,128)} %bitcast.1, bf16[2,2,512,256]{3,2,1,0:T(8,128)(2,1)} %cache_hbm), custom_call_target="tpu_custom_call" | custom-call | flops 20000000000 | bytes 80000000 | tf_op jit(solution)/shard_map/first_local/pallas_call | solution.py:392
  19.9 3.0 %collective-permute-start.4 = (bf16[2,2,528,256]{3,2,1,0:T(8,128)(2,1)}, bf16[2,2,528,256]{3,2,1,0:T(8,128)(2,1)}, u32[]{:S(2)}, u32[]{:S(2)}) collective-permute-start(bf16[2,2,528,256]{3,2,1,0:T(8,128)(2,1)} %get-tuple-element.23.own_hbm), channel_id=1, source_target_pairs={{4,8},{12,16},{20,24},{28,32},{36,40},{44,48},{52,56},{60,64},{68,... | collective-permute-start | bytes 3244040 | tf_op jit(solution)/shard_map/ppermute | solution.py:407
  23.0 0.1 collective-permute-start.3
  23.1 0.0 collective-permute-done.pair_ref
  23.1 3.9 %all-to-all-done.q_ref = bf16[16,72,128]{2,1,0:T(8,128)(2,1)S(1)} async-done(((bf16[16,72,128]{2,1,0:T(8,128)(2,1)}), bf16[16,72,128]{2,1,0:T(8,128)(2,1)S(1)}, u32[]{:S(2)}, u32[]{:S(2)}) %all-to-all-start) | async-done | bytes 294944 | tf_op jit(solution)/shard_map/all_to_all | solution.py:390
  26.9 0.0 collective-permute-done.2.cross_ref
  26.9 0.0 copy-done.2
  27.0 0.0 copy-start.6
  27.0 0.7 %copy-done.6 = f32[16,128]{1,0:T(8,128)S(1)} copy-done((f32[16,128]{1,0:T(8,128)S(1)}, f32[16,128]{1,0:T(8,128)}, u32[]{:S(2)}) %copy-start.6) | copy-done | bytes 8216
  27.7 3.1 %prefix.1 = bf16[16,56,128]{2,1,0:T(8,128)(2,1)} custom-call(bf16[16,72,128]{2,1,0:T(8,128)(2,1)S(1)} %all-to-all-done.q_ref, bf16[4,2,128,256]{3,2,1,0:T(8,128)(2,1)S(1)} %copy-done.5, bf16[4,2,128,256]{3,2,1,0:T(8,128)(2,1)S(1)} %collective-permute-done.pair_ref, bf16[4,2,128,256]{3,2,1,0:T(8,128)(2,1)S(1)} %collective-permute-done.1.next_ref, ...), custom_call_target="tpu_custom_call" | custom-call | flops 20000000000 | bytes 80000000 | tf_op jit(solution)/shard_map/prefix/pallas_call | solution.py:408
  30.8 6.6 %all-to-all-start.1 = ((bf16[16,56,128]{2,1,0:T(8,128)(2,1)}), bf16[16,56,128]{2,1,0:T(8,128)(2,1)S(1)}, u32[]{:S(2)}, u32[]{:S(2)}) async-start(bf16[16,56,128]{2,1,0:T(8,128)(2,1)} %prefix.1), calls=%async_computation.1 | async-start | bytes 458752 | tf_op jit(solution)/shard_map/all_to_all | solution.py:419
  37.4 0.0 collective-permute-done.4.far_hbm
  37.4 0.0 collective-permute-done.3.pair_hbm
  37.4 3.8 %second_local.1 = (bf16[2,2,512,256]{3,2,1,0:T(8,128)(2,1)}, bf16[2,2,256]{2,1,0:T(2,128)(2,1)}, f32[40,128]{1,0:T(8,128)S(1)}) custom-call(s32[2]{0:T(128)S(1)} %copy-done.4, f32[64,128]{1,0:T(8,128)S(1)} %copy-done.1, bf16[2,2,528,256]{3,2,1,0:T(8,128)(2,1)S(1)} %copy-done, bf16[2,2,528,256]{3,2,1,0:T(8,128)(2,1)} %collective-permute-done.3.pair_hbm, ...), custom_call_target="tpu_custom_call" | custom-call | tf_op jit(solution)/shard_map/second_local/pallas_call | solution.py:420
  41.2 5.4 %all-to-all-done.1.part_ref = bf16[16,56,128]{2,1,0:T(8,128)(2,1)S(1)} async-done(((bf16[16,56,128]{2,1,0:T(8,128)(2,1)}), bf16[16,56,128]{2,1,0:T(8,128)(2,1)S(1)}, u32[]{:S(2)}, u32[]{:S(2)}) %all-to-all-start.1) | async-done | bytes 229408 | tf_op jit(solution)/shard_map/all_to_all | solution.py:419
  46.6 1.0 %finish.1 = (bf16[2,2048]{1,0:T(2,128)(2,1)}, f32[16,8,128]{2,1,0:T(8,128)S(1)}) custom-call(bf16[16,56,128]{2,1,0:T(8,128)(2,1)S(1)} %all-to-all-done.1.part_ref, f32[40,128]{1,0:T(8,128)S(1)} %get-tuple-element.24.mean_ref, f32[16,128]{1,0:T(8,128)S(1)} %bitcast.3), custom_call_target="tpu_custom_call" | custom-call | tf_op jit(solution)/shard_map/finish/pallas_call | solution.py:433
  47.6 13.3 %all_to_all.15.all_ref = f32[16,8,128]{2,1,0:T(8,128)S(1)} all-to-all(f32[16,8,128]{2,1,0:T(8,128)S(1)} %get-tuple-element.25), channel_id=1, replica_groups=mesh['z2'=2,'z1'=2,'z0'=2,'x1'=2,'x0'=2,'core'=2,'tp'=4] {'x0','core','tp'}, dimensions={0} | all-to-all | bytes 131072 | tf_op jit(solution)/shard_map/all_to_all | solution.py:445
  61.0 1.3 %weights.1 = (f32[2]{0:T(128)}, f32[2]{0:T(128)}) custom-call(f32[16,8,128]{2,1,0:T(8,128)S(1)} %all_to_all.15.all_ref), custom_call_target="tpu_custom_call" | custom-call | tf_op jit(solution)/shard_map/weights/pallas_call | solution.py:446
  (11 shorter events, 0.0 us)
Async XLA Ops:
  0.6 15.1 %collective-permute-start.1 = (bf16[4,2,128,256]{3,2,1,0:T(8,128)(2,1)}, bf16[4,2,128,256]{3,2,1,0:T(8,128)(2,1)S(1)}, u32[]{:S(2)}, u32[]{:S(2)}) collective-permute-start(bf16[4,2,128,256]{3,2,1,0:T(8,128)(2,1)} %own_ref.1), channel_id=1, source_target_pairs={{0,8},{8,0},{1,9},{9,1},{2,10},{10,2},{3,11},{11,3},{4,12},{12,4},... | collective-permute-start | bytes 1572872 | tf_op jit(solution)/shard_map/ppermute | solution.py:368
  2.8 20.3 %collective-permute-start = (bf16[4,2,128,256]{3,2,1,0:T(8,128)(2,1)}, bf16[4,2,128,256]{3,2,1,0:T(8,128)(2,1)S(1)}, u32[]{:S(2)}, u32[]{:S(2)}) collective-permute-start(bf16[4,2,128,256]{3,2,1,0:T(8,128)(2,1)} %own_ref.1), channel_id=1, source_target_pairs={{0,4},{4,0},{1,5},{5,1},{2,6},{6,2},{3,7},{7,3},{8,12},{12,8},{9,1... | collective-permute-start | bytes 1572872 | tf_op jit(solution)/shard_map/ppermute | solution.py:369
  5.6 21.4 %all-to-all-start = ((bf16[16,72,128]{2,1,0:T(8,128)(2,1)}), bf16[16,72,128]{2,1,0:T(8,128)(2,1)S(1)}, u32[]{:S(2)}, u32[]{:S(2)}) async-start(bf16[16,72,128]{2,1,0:T(8,128)(2,1)} %get-tuple-element.18), calls=%async_computation | async-start | bytes 589824 | tf_op jit(solution)/shard_map/all_to_all | solution.py:390
  15.7 11.2 %collective-permute-start.2 = (bf16[4,2,128,256]{3,2,1,0:T(8,128)(2,1)S(1)}, bf16[4,2,128,256]{3,2,1,0:T(8,128)(2,1)S(1)}, u32[]{:S(2)}, u32[]{:S(2)}) collective-permute-start(bf16[4,2,128,256]{3,2,1,0:T(8,128)(2,1)S(1)} %collective-permute-done.1.next_ref), channel_id=1, source_target_pairs={{0,4},{4,0},{1,5},{5,1},{2,6},{6,2},{3,7},{7,3},{8,12},{12,8},{9,1... | collective-permute-start | bytes 1572872 | tf_op jit(solution)/shard_map/ppermute | solution.py:370
  16.1 10.9 %copy-start.2 = (f32[2048]{0:T(1024)S(1)}, f32[2048]{0:T(1024)}, u32[]{:S(2)}) copy-start(f32[2048]{0:T(1024)} %param.12) | copy-start | bytes 24580
  16.1 10.9 %copy-start.5 = (bf16[4,2,128,256]{3,2,1,0:T(8,128)(2,1)S(1)}, bf16[4,2,128,256]{3,2,1,0:T(8,128)(2,1)}, u32[]{:S(2)}) copy-start(bf16[4,2,128,256]{3,2,1,0:T(8,128)(2,1)} %own_ref.1) | copy-start | bytes 1572868
  19.9 17.5 %collective-permute-start.4 = (bf16[2,2,528,256]{3,2,1,0:T(8,128)(2,1)}, bf16[2,2,528,256]{3,2,1,0:T(8,128)(2,1)}, u32[]{:S(2)}, u32[]{:S(2)}) collective-permute-start(bf16[2,2,528,256]{3,2,1,0:T(8,128)(2,1)} %get-tuple-element.23.own_hbm), channel_id=1, source_target_pairs={{4,8},{12,16},{20,24},{28,32},{36,40},{44,48},{52,56},{60,64},{68,... | collective-permute-start | bytes 3244040 | tf_op jit(solution)/shard_map/ppermute | solution.py:407
  23.0 14.4 %collective-permute-start.3 = (bf16[2,2,528,256]{3,2,1,0:T(8,128)(2,1)}, bf16[2,2,528,256]{3,2,1,0:T(8,128)(2,1)}, u32[]{:S(2)}, u32[]{:S(2)}) collective-permute-start(bf16[2,2,528,256]{3,2,1,0:T(8,128)(2,1)} %get-tuple-element.23.own_hbm), channel_id=1, source_target_pairs={{0,4},{4,0},{1,5},{5,1},{2,6},{6,2},{3,7},{7,3},{8,12},{12,8},{9,1... | collective-permute-start | bytes 3244040 | tf_op jit(solution)/shard_map/ppermute | solution.py:406
  27.0 0.7 %copy-start.6 = (f32[16,128]{1,0:T(8,128)S(1)}, f32[16,128]{1,0:T(8,128)}, u32[]{:S(2)}) copy-start(f32[16,128]{1,0:T(8,128)} %get-tuple-element.21.local_ref) | copy-start | bytes 24580
  27.7 9.8 %copy-start = (bf16[2,2,528,256]{3,2,1,0:T(8,128)(2,1)S(1)}, bf16[2,2,528,256]{3,2,1,0:T(8,128)(2,1)}, u32[]{:S(2)}) copy-start(bf16[2,2,528,256]{3,2,1,0:T(8,128)(2,1)} %get-tuple-element.23.own_hbm) | copy-start | bytes 3244036
  27.7 9.8 %copy-start.1 = (f32[64,128]{1,0:T(8,128)S(1)}, f32[64,128]{1,0:T(8,128)}, u32[]{:S(2)}) copy-start(f32[64,128]{1,0:T(8,128)} %get-tuple-element.19.q_ref) | copy-start | bytes 98308
  27.7 9.8 %copy-start.3 = (bf16[2,2,2,256]{3,2,1,0:T(2,128)(2,1)S(1)}, bf16[2,2,2,256]{3,2,1,0:T(2,128)(2,1)}, u32[]{:S(2)}) copy-start(bf16[2,2,2,256]{3,2,1,0:T(2,128)(2,1)} %kv_ref.3) | copy-start | bytes 12292
  27.7 9.8 %copy-start.4 = (s32[2]{0:T(128)S(1)}, s32[2]{0:T(128)}, u32[]{:S(2)}) copy-start(s32[2]{0:T(128)} %anc_ref.1) | copy-start | bytes 28
  30.8 15.8 %all-to-all-start.1 = ((bf16[16,56,128]{2,1,0:T(8,128)(2,1)}), bf16[16,56,128]{2,1,0:T(8,128)(2,1)S(1)}, u32[]{:S(2)}, u32[]{:S(2)}) async-start(bf16[16,56,128]{2,1,0:T(8,128)(2,1)} %prefix.1), calls=%async_computation.1 | async-start | bytes 458752 | tf_op jit(solution)/shard_map/all_to_all | solution.py:419

commit v5 on v4

--- a/solution.py
+++ b/solution.py
@@ -177,9 +177,22 @@
     return num / total, top * FACTOR + jnp.log(total)
 
 
-def first_kernel(ids_ref, prior_ref, q_ref, kv_ref, w_ref, cache_hbm, out_ref, wide_hbm, wide_ref, sems):
-    taken = pltpu.make_async_copy(cache_hbm, wide_ref.at[:, :, 0:SUF, :], sems.at[0])
-    taken.start()
+def first_kernel(
+    ids_hbm, prior_hbm, q_hbm, kv_hbm, w_hbm, cache_hbm, out_ref, wide_hbm,
+    ids_ref, prior_ref, q_ref, kv_ref, w_ref, wide_ref, sems, in_sems, out_sems,
+):
+    taken = [
+        pltpu.make_async_copy(cache_hbm.at[p], wide_ref.at[p, :, 0:SUF, :], in_sems.at[p]) for p in range(2)
+    ]
+    given = [pltpu.make_async_copy(wide_ref.at[p], wide_hbm.at[p], out_sems.at[p]) for p in range(2)]
+    pairs = ((kv_hbm, kv_ref), (q_hbm, q_ref), (w_hbm, w_ref), (ids_hbm, ids_ref), (prior_hbm, prior_ref))
+    small = [pltpu.make_async_copy(src, dst, sems.at[n]) for n, (src, dst) in enumerate(pairs)]
+    taken[0].start()
+    for copy in small:
+        copy.start()
+    taken[1].start()
+    for copy in small:
+        copy.wait()
     queries = q_ref[...]
     step_kv = kv_ref[...].astype(F32)
     tail_row = lax.broadcasted_iota(jnp.int32, (TAIL, kv_ref.shape[-1]), 0)
@@ -187,9 +200,9 @@
         for kind in range(2):
             line = step_kv[p, 0, kind : kind + 1, :]
             wide_ref[p, kind, SUF : SUF + TAIL, :] = jnp.where(tail_row == 0, line, 0.0).astype(BF16)
-    taken.wait()
-    given = pltpu.make_async_copy(wide_ref, wide_hbm, sems.at[1])
-    given.start()
+    for p in range(2):
+        taken[p].wait()
+        given[p].start()
     means, tops = [], []
     for p in range(2):
         for kv in range(2):
@@ -224,11 +237,12 @@
     for r, part in enumerate(split(prior)):
         facts = jnp.where(row_id == r + 1, part, facts)
     out_ref[0:8, :] = facts
-    given.wait()
+    for copy in given:
+        copy.wait()
 
 
 def second_kernel(
-    anc_ref, q_ref, own_hbm, pair_hbm, far_hbm, kv_ref, copied_ref, carried_ref, mean_ref, wide_ref, sems
+    anc_ref, q_ref, own_hbm, pair_hbm, far_hbm, kv_ref, copied_hbm, carried_ref, mean_ref, wide_ref, sems, out_sems
 ):
     core = lax.axis_index("core")
     base = 0
@@ -250,8 +264,12 @@
         pl.when(flag)(copy.start)
     for flag, copy in choices:
         pl.when(flag)(copy.wait)
+    results = [
+        pltpu.make_async_copy(wide_ref.at[slot, :, 0:SUF, :], copied_hbm.at[slot], out_sems.at[slot])
+        for slot in range(2)
+    ]
     for slot in range(2):
-        copied_ref[slot] = wide_ref[slot, :, 0:SUF, :]
+        results[slot].start()
         for kind in range(2):
             tail = wide_ref[slot, kind, SUF : SUF + TAIL, :].astype(F32)
             carried_ref[slot, kind : kind + 1, :] = tail[0:1].astype(BF16)
@@ -278,6 +296,8 @@
     row_id = lax.broadcasted_iota(jnp.int32, (32, 128), 0)
     row = jnp.sum(jnp.where(lanes((32, 128)) == row_id, top, 0.0), axis=0, keepdims=True)
     mean_ref[32:40, :] = jnp.broadcast_to(row, (8, 128))
+    for result in results:
+        result.wait()
 
 
 def finish_kernel(part_ref, mean_ref, w_ref, out_ref, send_ref, wide_ref):
@@ -367,7 +387,6 @@
     cross = cross + [(b, a) for a, b in cross]
     next_prefix = lax.ppermute(prefix_cache, "x0", swap)
     pair_prefix = lax.ppermute(prefix_cache, "core", swap)
-    cross_prefix = lax.ppermute(next_prefix, "core", swap)
     weight_rows = twist_weight.reshape(16, 128)
 
     blocks, rows = pl.pallas_call(
@@ -395,14 +414,26 @@
             jax.ShapeDtypeStruct((8 + 2 * PLANE, 128), F32),
             jax.ShapeDtypeStruct((2, 2, SUF + TAIL, 256), BF16),
         ),
-        in_specs=[SMEM] * 2 + [VMEM] * 3 + [HBM],
+        in_specs=[HBM] * 6,
         out_specs=(VMEM, HBM),
-        scratch_shapes=[pltpu.VMEM((2, 2, SUF + TAIL, 256), BF16), pltpu.SemaphoreType.DMA((2,))],
+        scratch_shapes=[
+            pltpu.SMEM((2,), jnp.int32),
+            pltpu.SMEM((2,), F32),
+            pltpu.VMEM((Q_ROWS, 128), F32),
+            pltpu.VMEM(step_kv.shape, BF16),
+            pltpu.VMEM((16, 128), F32),
+            pltpu.VMEM((2, 2, SUF + TAIL, 256), BF16),
+            pltpu.SemaphoreType.DMA((5,)),
+            pltpu.SemaphoreType.DMA((2,)),
+            pltpu.SemaphoreType.DMA((2,)),
+        ],
         compiler_params=WHOLE,
         cost_estimate=LONG,
         name="first_local",
     )(prompt_ids, prior_weights, rows, step_kv, weight_rows, late_cache)
     held = lax.optimization_barrier((wide_cache, blocks))[0]
+    after = lax.optimization_barrier((next_prefix, local))[0]
+    cross_prefix = lax.ppermute(after, "core", swap)
     pair_cache = lax.ppermute(held, "core", swap)
     far_cache = lax.ppermute(held, DOM, cross)
     parts = pl.pallas_call(
@@ -425,8 +456,12 @@
             jax.ShapeDtypeStruct((40, 128), F32),
         ),
         in_specs=[SMEM, VMEM] + [HBM] * 3 + [VMEM],
-        out_specs=(VMEM,) * 3,
-        scratch_shapes=[pltpu.VMEM((2, 2, SUF + TAIL, 256), BF16), pltpu.SemaphoreType.DMA((2,))],
+        out_specs=(HBM, VMEM, VMEM),
+        scratch_shapes=[
+            pltpu.VMEM((2, 2, SUF + TAIL, 256), BF16),
+            pltpu.SemaphoreType.DMA((2,)),
+            pltpu.SemaphoreType.DMA((2,)),
+        ],
         compiler_params=MOST,
         name="second_local",
     )(ancestors, rows, wide_cache, pair_cache, far_cache, step_kv)

time: 62.8 us -> 60.6 us (0.965)
  starting transfers between devices: 23.7 us -> 21.7 us
  waiting for transfers between devices: 9.25 us -> 10.5 us
  Pallas kernels: 14.5 us -> 13.5 us
    ppermute x1, starting transfers between devices: 2.13 us -> 0.01 us  [body(): next_prefix = lax.ppermute(prefix_cache, 'x0', swap)]
    ppermute x1, starting transfers between devices: 1.3 us -> 3.33 us  [body(): pair_prefix = lax.ppermute(prefix_cache, 'core', swap)]
    all_to_all x1, starting transfers between devices: 6.62 us -> 5.5 us  [body(): received = lax.all_to_all(parts, PEERS, 0, 0, tiled=True)]
    all_to_all x1, waiting for transfers between devices: 3.86 us -> 4.97 us  [body(): gathered = lax.all_to_all(blocks, PEERS, 0, 0, tiled=True)]
    ppermute x1, starting transfers between devices: 3.03 us -> 2.04 us  [body(): far_cache = lax.ppermute(held, DOM, cross)]
    ppermute x1, waiting for transfers between devices: 0.01 us -> 0.77 us  [body(): far_cache = lax.ppermute(held, DOM, cross)]
    pallas_call x1, Pallas kernels: 3.84 us -> 3.15 us  [body(): pl.pallas_call(first_kernel, out_shape=(jax.ShapeDtypeStruct((8 + 2 * PLA...]
  transfers between devices with their start and end apart: 7 -> 7, of which waited for: 2 -> 3; matrix products, arithmetic and copies ran while one was open for 0% -> 0% of each run, Pallas kernels for 20% -> 19%
where the time goes in v5:
time: 60.6 us; the launch traced here: 60.1 us
  starting transfers between devices  21.7 us (36%)
  Pallas kernels  13.5 us (22%)
  blocking collectives  12.9 us (21%)
  waiting for transfers between devices  10.5 us (17%)
  between operations  0.76 us (1%)
  local copies, waits for them, and re-layouts  0.72 us (1%)
    all_to_all x1, blocking collectives, body(): lines = lax.all_to_all(send, SHARE + ('tp',), 0, 0, tiled=True)  12.9 us
    all_to_all x1, starting transfers between devices, body(): gathered = lax.all_to_all(blocks, PEERS, 0, 0, tiled=True)  9.96 us
    all_to_all x1, starting transfers between devices, body(): received = lax.all_to_all(parts, PEERS, 0, 0, tiled=True)  5.5 us
    all_to_all x1, waiting for transfers between devices, body(): gathered = lax.all_to_all(blocks, PEERS, 0, 0, tiled=True)  4.97 us
    all_to_all x1, waiting for transfers between devices, body(): received = lax.all_to_all(parts, PEERS, 0, 0, tiled=True)  4.78 us
    pallas_call x1, Pallas kernels, body(): pl.pallas_call(second_kernel, out_shape=(jax.ShapeDtypeStruct(suffix_cach...  3.45 us
    ppermute x1, starting transfers between devices, body(): pair_prefix = lax.ppermute(prefix_cache, 'core', swap)  3.33 us
    pallas_call x1, Pallas kernels, body(): pl.pallas_call(first_kernel, out_shape=(jax.ShapeDtypeStruct((8 + 2 * PLA...  3.15 us
  transfers between devices with their start and end apart: 7, of which 3 were waited for; matrix products, arithmetic and copies ran while one was open for 0% of the time, Pallas kernels for 19%

profile of v5, /device:TPU:1, one launch (start us, length us, event | category | flops | bytes accessed | tf_op | source)
XLA Modules:
  0.0 60.1 jit_solution(2724617044846535875)
XLA Ops:
  0.6 3.3 %collective-permute-start = (bf16[4,2,128,256]{3,2,1,0:T(8,128)(2,1)}, bf16[4,2,128,256]{3,2,1,0:T(8,128)(2,1)S(1)}, u32[]{:S(2)}, u32[]{:S(2)}) collective-permute-start(bf16[4,2,128,256]{3,2,1,0:T(8,128)(2,1)} %own_ref.1), channel_id=1, source_target_pairs={{0,4},{4,0},{1,5},{5,1},{2,6},{6,2},{3,7},{7,3},{8,12},{12,8},{9,1... | collective-permute-start | bytes 1572872 | tf_op jit(solution)/shard_map/ppermute | solution.py:389
  4.0 0.0 collective-permute-start.1
  4.0 1.5 %prep.1 = (bf16[16,72,128]{2,1,0:T(8,128)(2,1)}, f32[64,128]{1,0:T(8,128)}) custom-call(s32[2]{0:T(128)} %ids_hbm.3, bf16[2,2,2048]{2,1,0:T(2,128)(2,1)} %q_hbm.1), custom_call_target="tpu_custom_call" | custom-call | tf_op jit(solution)/shard_map/prep/pallas_call | solution.py:392
  5.5 10.0 %all-to-all-start = ((bf16[16,72,128]{2,1,0:T(8,128)(2,1)}), bf16[16,72,128]{2,1,0:T(8,128)(2,1)S(1)}, u32[]{:S(2)}, u32[]{:S(2)}) async-start(bf16[16,72,128]{2,1,0:T(8,128)(2,1)} %get-tuple-element.19), calls=%async_computation | async-start | bytes 589824 | tf_op jit(solution)/shard_map/all_to_all | solution.py:409
  15.4 0.0 copy-start.2
  15.5 0.0 copy-start.5
  15.5 3.1 %first_local.1 = (f32[16,128]{1,0:T(8,128)}, bf16[2,2,528,256]{3,2,1,0:T(8,128)(2,1)}) custom-call(s32[2]{0:T(128)} %ids_hbm.3, f32[2]{0:T(128)} %prior_hbm.1, f32[64,128]{1,0:T(8,128)} %get-tuple-element.20.q_hbm.q_ref, bf16[2,2,2,256]{3,2,1,0:T(2,128)(2,1)} %kv_ref.1, f32[16,128]{1,0:T(8,128)} %bitcast.1, bf16[2,2,512,256]{3,2,1,0:T(8,128)(2,1)} %cache_hbm), custom_call_target="tpu_custom_call" | custom-call | flops 20000000000 | bytes 80000000 | tf_op jit(solution)/shard_map/first_local/pallas_call | solution.py:411
  18.6 0.0 collective-permute-done.1.next_ref
  18.6 0.7 %collective-permute-start.2 = (bf16[4,2,128,256]{3,2,1,0:T(8,128)(2,1)S(1)}, bf16[4,2,128,256]{3,2,1,0:T(8,128)(2,1)S(1)}, u32[]{:S(2)}, u32[]{:S(2)}) collective-permute-start(bf16[4,2,128,256]{3,2,1,0:T(8,128)(2,1)S(1)} %collective-permute-done.1.next_ref), channel_id=1, source_target_pairs={{0,4},{4,0},{1,5},{5,1},{2,6},{6,2},{3,7},{7,3},{8,12},{12,8},{9,1... | collective-permute-start | bytes 1572872 | tf_op jit(solution)/shard_map/ppermute | solution.py:436
  19.4 2.0 %collective-permute-start.4 = (bf16[2,2,528,256]{3,2,1,0:T(8,128)(2,1)}, bf16[2,2,528,256]{3,2,1,0:T(8,128)(2,1)}, u32[]{:S(2)}, u32[]{:S(2)}) collective-permute-start(bf16[2,2,528,256]{3,2,1,0:T(8,128)(2,1)} %get-tuple-element.25.own_hbm), channel_id=1, source_target_pairs={{4,8},{12,16},{20,24},{28,32},{36,40},{44,48},{52,56},{60,64},{68,... | collective-permute-start | bytes 3244040 | tf_op jit(solution)/shard_map/ppermute | solution.py:438
  21.4 0.1 collective-permute-start.3
  21.5 0.0 collective-permute-done.pair_ref
  21.5 5.0 %all-to-all-done.q_ref = bf16[16,72,128]{2,1,0:T(8,128)(2,1)S(1)} async-done(((bf16[16,72,128]{2,1,0:T(8,128)(2,1)}), bf16[16,72,128]{2,1,0:T(8,128)(2,1)S(1)}, u32[]{:S(2)}, u32[]{:S(2)}) %all-to-all-start) | async-done | bytes 294944 | tf_op jit(solution)/shard_map/all_to_all | solution.py:409
  26.5 0.0 collective-permute-done.2.cross_ref
  26.5 0.0 copy-start.6
  26.5 0.7 %copy-done.6 = f32[16,128]{1,0:T(8,128)S(1)} copy-done((f32[16,128]{1,0:T(8,128)S(1)}, f32[16,128]{1,0:T(8,128)}, u32[]{:S(2)}) %copy-start.6) | copy-done | bytes 8216
  27.2 3.1 %prefix.1 = bf16[16,56,128]{2,1,0:T(8,128)(2,1)} custom-call(bf16[16,72,128]{2,1,0:T(8,128)(2,1)S(1)} %all-to-all-done.q_ref, bf16[4,2,128,256]{3,2,1,0:T(8,128)(2,1)S(1)} %copy-done.5, bf16[4,2,128,256]{3,2,1,0:T(8,128)(2,1)S(1)} %collective-permute-done.pair_ref, bf16[4,2,128,256]{3,2,1,0:T(8,128)(2,1)S(1)} %collective-permute-done.1.next_ref, ...), custom_call_target="tpu_custom_call" | custom-call | flops 20000000000 | bytes 80000000 | tf_op jit(solution)/shard_map/prefix/pallas_call | solution.py:439
  30.3 5.5 %all-to-all-start.1 = ((bf16[16,56,128]{2,1,0:T(8,128)(2,1)}), bf16[16,56,128]{2,1,0:T(8,128)(2,1)S(1)}, u32[]{:S(2)}, u32[]{:S(2)}) async-start(bf16[16,56,128]{2,1,0:T(8,128)(2,1)} %prefix.1), calls=%async_computation.1 | async-start | bytes 458752 | tf_op jit(solution)/shard_map/all_to_all | solution.py:450
  35.8 0.8 %collective-permute-done.4.far_hbm = bf16[2,2,528,256]{3,2,1,0:T(8,128)(2,1)} collective-permute-done((bf16[2,2,528,256]{3,2,1,0:T(8,128)(2,1)}, bf16[2,2,528,256]{3,2,1,0:T(8,128)(2,1)}, u32[]{:S(2)}, u32[]{:S(2)}) %collective-permute-start.4) | collective-permute-done | bytes 1081376 | tf_op jit(solution)/shard_map/ppermute | solution.py:438
  36.6 3.4 %second_local.1 = (bf16[2,2,512,256]{3,2,1,0:T(8,128)(2,1)}, bf16[2,2,256]{2,1,0:T(2,128)(2,1)}, f32[40,128]{1,0:T(8,128)S(1)}) custom-call(s32[2]{0:T(128)S(1)} %copy-done.4, f32[64,128]{1,0:T(8,128)S(1)} %copy-done.1, bf16[2,2,528,256]{3,2,1,0:T(8,128)(2,1)S(1)} %copy-done, bf16[2,2,528,256]{3,2,1,0:T(8,128)(2,1)} %collective-permute-done.3.pair_hbm, ...), custom_call_target="tpu_custom_call" | custom-call | tf_op jit(solution)/shard_map/second_local/pallas_call | solution.py:451
  40.0 4.8 %all-to-all-done.1.part_ref = bf16[16,56,128]{2,1,0:T(8,128)(2,1)S(1)} async-done(((bf16[16,56,128]{2,1,0:T(8,128)(2,1)}), bf16[16,56,128]{2,1,0:T(8,128)(2,1)S(1)}, u32[]{:S(2)}, u32[]{:S(2)}) %all-to-all-start.1) | async-done | bytes 229408 | tf_op jit(solution)/shard_map/all_to_all | solution.py:450
  44.8 1.0 %finish.1 = (bf16[2,2048]{1,0:T(2,128)(2,1)}, f32[16,8,128]{2,1,0:T(8,128)S(1)}) custom-call(bf16[16,56,128]{2,1,0:T(8,128)(2,1)S(1)} %all-to-all-done.1.part_ref, f32[40,128]{1,0:T(8,128)S(1)} %get-tuple-element.26.mean_ref, f32[16,128]{1,0:T(8,128)S(1)} %bitcast.3), custom_call_target="tpu_custom_call" | custom-call | tf_op jit(solution)/shard_map/finish/pallas_call | solution.py:468
  45.8 12.9 %all_to_all.15.all_ref = f32[16,8,128]{2,1,0:T(8,128)S(1)} all-to-all(f32[16,8,128]{2,1,0:T(8,128)S(1)} %get-tuple-element.27), channel_id=1, replica_groups=mesh['z2'=2,'z1'=2,'z0'=2,'x1'=2,'x0'=2,'core'=2,'tp'=4] {'x0','core','tp'}, dimensions={0} | all-to-all | bytes 131072 | tf_op jit(solution)/shard_map/all_to_all | solution.py:480
  58.8 1.3 %weights.1 = (f32[2]{0:T(128)}, f32[2]{0:T(128)}) custom-call(f32[16,8,128]{2,1,0:T(8,128)S(1)} %all_to_all.15.all_ref), custom_call_target="tpu_custom_call" | custom-call | tf_op jit(solution)/shard_map/weights/pallas_call | solution.py:481
  (11 shorter events, 0.0 us)
Async XLA Ops:
  0.6 20.9 %collective-permute-start = (bf16[4,2,128,256]{3,2,1,0:T(8,128)(2,1)}, bf16[4,2,128,256]{3,2,1,0:T(8,128)(2,1)S(1)}, u32[]{:S(2)}, u32[]{:S(2)}) collective-permute-start(bf16[4,2,128,256]{3,2,1,0:T(8,128)(2,1)} %own_ref.1), channel_id=1, source_target_pairs={{0,4},{4,0},{1,5},{5,1},{2,6},{6,2},{3,7},{7,3},{8,12},{12,8},{9,1... | collective-permute-start | bytes 1572872 | tf_op jit(solution)/shard_map/ppermute | solution.py:389
  4.0 14.7 %collective-permute-start.1 = (bf16[4,2,128,256]{3,2,1,0:T(8,128)(2,1)}, bf16[4,2,128,256]{3,2,1,0:T(8,128)(2,1)S(1)}, u32[]{:S(2)}, u32[]{:S(2)}) collective-permute-start(bf16[4,2,128,256]{3,2,1,0:T(8,128)(2,1)} %own_ref.1), channel_id=1, source_target_pairs={{0,8},{8,0},{1,9},{9,1},{2,10},{10,2},{3,11},{11,3},{4,12},{12,4},... | collective-permute-start | bytes 1572872 | tf_op jit(solution)/shard_map/ppermute | solution.py:388
  5.5 21.0 %all-to-all-start = ((bf16[16,72,128]{2,1,0:T(8,128)(2,1)}), bf16[16,72,128]{2,1,0:T(8,128)(2,1)S(1)}, u32[]{:S(2)}, u32[]{:S(2)}) async-start(bf16[16,72,128]{2,1,0:T(8,128)(2,1)} %get-tuple-element.19), calls=%async_computation | async-start | bytes 589824 | tf_op jit(solution)/shard_map/all_to_all | solution.py:409
  15.4 11.1 %copy-start.2 = (f32[2048]{0:T(1024)S(1)}, f32[2048]{0:T(1024)}, u32[]{:S(2)}) copy-start(f32[2048]{0:T(1024)} %param.12) | copy-start | bytes 24580
  15.5 11.1 %copy-start.5 = (bf16[4,2,128,256]{3,2,1,0:T(8,128)(2,1)S(1)}, bf16[4,2,128,256]{3,2,1,0:T(8,128)(2,1)}, u32[]{:S(2)}) copy-start(bf16[4,2,128,256]{3,2,1,0:T(8,128)(2,1)} %own_ref.1) | copy-start | bytes 1572868
  18.6 7.9 %collective-permute-start.2 = (bf16[4,2,128,256]{3,2,1,0:T(8,128)(2,1)S(1)}, bf16[4,2,128,256]{3,2,1,0:T(8,128)(2,1)S(1)}, u32[]{:S(2)}, u32[]{:S(2)}) collective-permute-start(bf16[4,2,128,256]{3,2,1,0:T(8,128)(2,1)S(1)} %collective-permute-done.1.next_ref), channel_id=1, source_target_pairs={{0,4},{4,0},{1,5},{5,1},{2,6},{6,2},{3,7},{7,3},{8,12},{12,8},{9,1... | collective-permute-start | bytes 1572872 | tf_op jit(solution)/shard_map/ppermute | solution.py:436
  19.4 17.2 %copy-start.1 = (f32[64,128]{1,0:T(8,128)S(1)}, f32[64,128]{1,0:T(8,128)}, u32[]{:S(2)}) copy-start(f32[64,128]{1,0:T(8,128)} %get-tuple-element.20.q_hbm.q_ref) | copy-start | bytes 98308
  19.4 17.2 %copy-start.3 = (bf16[2,2,2,256]{3,2,1,0:T(2,128)(2,1)S(1)}, bf16[2,2,2,256]{3,2,1,0:T(2,128)(2,1)}, u32[]{:S(2)}) copy-start(bf16[2,2,2,256]{3,2,1,0:T(2,128)(2,1)} %kv_ref.1) | copy-start | bytes 12292
  19.4 17.2 %copy-start.4 = (s32[2]{0:T(128)S(1)}, s32[2]{0:T(128)}, u32[]{:S(2)}) copy-start(s32[2]{0:T(128)} %anc_ref.1) | copy-start | bytes 28
  19.4 17.2 %collective-permute-start.4 = (bf16[2,2,528,256]{3,2,1,0:T(8,128)(2,1)}, bf16[2,2,528,256]{3,2,1,0:T(8,128)(2,1)}, u32[]{:S(2)}, u32[]{:S(2)}) collective-permute-start(bf16[2,2,528,256]{3,2,1,0:T(8,128)(2,1)} %get-tuple-element.25.own_hbm), channel_id=1, source_target_pairs={{4,8},{12,16},{20,24},{28,32},{36,40},{44,48},{52,56},{60,64},{68,... | collective-permute-start | bytes 3244040 | tf_op jit(solution)/shard_map/ppermute | solution.py:438
  21.4 15.1 %collective-permute-start.3 = (bf16[2,2,528,256]{3,2,1,0:T(8,128)(2,1)}, bf16[2,2,528,256]{3,2,1,0:T(8,128)(2,1)}, u32[]{:S(2)}, u32[]{:S(2)}) collective-permute-start(bf16[2,2,528,256]{3,2,1,0:T(8,128)(2,1)} %get-tuple-element.25.own_hbm), channel_id=1, source_target_pairs={{0,4},{4,0},{1,5},{5,1},{2,6},{6,2},{3,7},{7,3},{8,12},{12,8},{9,1... | collective-permute-start | bytes 3244040 | tf_op jit(solution)/shard_map/ppermute | solution.py:437
  26.5 0.7 %copy-start.6 = (f32[16,128]{1,0:T(8,128)S(1)}, f32[16,128]{1,0:T(8,128)}, u32[]{:S(2)}) copy-start(f32[16,128]{1,0:T(8,128)} %get-tuple-element.22.local_ref) | copy-start | bytes 24580
  27.2 9.4 %copy-start = (bf16[2,2,528,256]{3,2,1,0:T(8,128)(2,1)S(1)}, bf16[2,2,528,256]{3,2,1,0:T(8,128)(2,1)}, u32[]{:S(2)}) copy-start(bf16[2,2,528,256]{3,2,1,0:T(8,128)(2,1)} %get-tuple-element.25.own_hbm) | copy-start | bytes 3244036
  30.3 14.5 %all-to-all-start.1 = ((bf16[16,56,128]{2,1,0:T(8,128)(2,1)}), bf16[16,56,128]{2,1,0:T(8,128)(2,1)S(1)}, u32[]{:S(2)}, u32[]{:S(2)}) async-start(bf16[16,56,128]{2,1,0:T(8,128)(2,1)} %prefix.1), calls=%async_computation.1 | async-start | bytes 458752 | tf_op jit(solution)/shard_map/all_to_all | solution.py:450

commit v6 on v5

--- a/solution.py
+++ b/solution.py
@@ -436,6 +436,7 @@
     cross_prefix = lax.ppermute(after, "core", swap)
     pair_cache = lax.ppermute(held, "core", swap)
     far_cache = lax.ppermute(held, DOM, cross)
+    local = jnp.maximum(local, -3e38)
     parts = pl.pallas_call(
         prefix_kernel,
         out_shape=jax.ShapeDtypeStruct((RING, PART_ROWS, 128), BF16),

time: 60.6 us -> 60.2 us (level)
  Pallas kernels: 13.5 us -> 12.5 us
  other arithmetic: 0 us -> 0.7 us
  local copies, waits for them, and re-layouts: 0.72 us -> 0.03 us
    pallas_call x1, Pallas kernels: 3.45 us -> 2.47 us  [body(): pl.pallas_call(second_kernel, out_shape=(jax.ShapeDtypeStruct(suffix_cach...]
    max x0 -> x1, other arithmetic: none -> 0.7 us  [body(): local = jnp.maximum(local, -3e+38)]
    unnamed x14 -> x12, local copies, waits for them, and re-layouts: 0.72 us -> 0.03 us
  transfers between devices with their start and end apart: 7 -> 7, of which waited for: 3 -> 3; matrix products, arithmetic and copies ran while one was open for 0% -> 1% of each run, Pallas kernels for 19% -> 17%
where the time goes in v6:
time: 60.2 us; the launch traced here: 59.7 us
  starting transfers between devices  21.5 us (36%)
  blocking collectives  13.2 us (22%)
  Pallas kernels  12.5 us (21%)
  waiting for transfers between devices  10.9 us (18%)
  between operations  0.75 us (1%)
  other arithmetic  0.7 us (1%)
    all_to_all x1, blocking collectives, body(): lines = lax.all_to_all(send, SHARE + ('tp',), 0, 0, tiled=True)  13.2 us
    all_to_all x1, starting transfers between devices, body(): gathered = lax.all_to_all(blocks, PEERS, 0, 0, tiled=True)  9.96 us
    all_to_all x1, starting transfers between devices, body(): received = lax.all_to_all(parts, PEERS, 0, 0, tiled=True)  5.5 us
    all_to_all x1, waiting for transfers between devices, body(): received = lax.all_to_all(parts, PEERS, 0, 0, tiled=True)  5.2 us
    all_to_all x1, waiting for transfers between devices, body(): gathered = lax.all_to_all(blocks, PEERS, 0, 0, tiled=True)  4.4 us
    ppermute x1, starting transfers between devices, body(): pair_prefix = lax.ppermute(prefix_cache, 'core', swap)  3.33 us
    pallas_call x1, Pallas kernels, body(): pl.pallas_call(first_kernel, out_shape=(jax.ShapeDtypeStruct((8 + 2 * PLA...  3.15 us
    pallas_call x1, Pallas kernels, body(): pl.pallas_call(prefix_kernel, out_shape=jax.ShapeDtypeStruct((RING, PART_...  3.07 us
  transfers between devices with their start and end apart: 7, of which 3 were waited for; matrix products, arithmetic and copies ran while one was open for 1% of the time, Pallas kernels for 17%

profile of v6, /device:TPU:1, one launch (start us, length us, event | category | flops | bytes accessed | tf_op | source)
XLA Modules:
  0.0 59.7 jit_solution(2072606564570902881)
XLA Ops:
  0.6 3.3 %collective-permute-start = (bf16[4,2,128,256]{3,2,1,0:T(8,128)(2,1)}, bf16[4,2,128,256]{3,2,1,0:T(8,128)(2,1)S(1)}, u32[]{:S(2)}, u32[]{:S(2)}) collective-permute-start(bf16[4,2,128,256]{3,2,1,0:T(8,128)(2,1)} %own_ref.1), channel_id=1, source_target_pairs={{0,4},{4,0},{1,5},{5,1},{2,6},{6,2},{3,7},{7,3},{8,12},{12,8},{9,1... | collective-permute-start | bytes 1572872 | tf_op jit(solution)/shard_map/ppermute | solution.py:389
  4.0 0.0 collective-permute-start.1
  4.0 1.5 %prep.1 = (bf16[16,72,128]{2,1,0:T(8,128)(2,1)}, f32[64,128]{1,0:T(8,128)}) custom-call(s32[2]{0:T(128)} %ids_hbm.3, bf16[2,2,2048]{2,1,0:T(2,128)(2,1)} %q_hbm.1), custom_call_target="tpu_custom_call" | custom-call | tf_op jit(solution)/shard_map/prep/pallas_call | solution.py:392
  5.5 10.0 %all-to-all-start = ((bf16[16,72,128]{2,1,0:T(8,128)(2,1)}), bf16[16,72,128]{2,1,0:T(8,128)(2,1)S(1)}, u32[]{:S(2)}, u32[]{:S(2)}) async-start(bf16[16,72,128]{2,1,0:T(8,128)(2,1)} %get-tuple-element.19), calls=%async_computation | async-start | bytes 589824 | tf_op jit(solution)/shard_map/all_to_all | solution.py:409
  15.4 0.0 copy-start.2
  15.5 0.0 copy-start.5
  15.5 3.1 %first_local.1 = (f32[16,128]{1,0:T(8,128)}, bf16[2,2,528,256]{3,2,1,0:T(8,128)(2,1)}) custom-call(s32[2]{0:T(128)} %ids_hbm.3, f32[2]{0:T(128)} %prior_hbm.1, f32[64,128]{1,0:T(8,128)} %get-tuple-element.20.q_hbm.q_ref, bf16[2,2,2,256]{3,2,1,0:T(2,128)(2,1)} %kv_ref.1, f32[16,128]{1,0:T(8,128)} %bitcast.1, bf16[2,2,512,256]{3,2,1,0:T(8,128)(2,1)} %cache_hbm), custom_call_target="tpu_custom_call" | custom-call | flops 20000000000 | bytes 80000000 | tf_op jit(solution)/shard_map/first_local/pallas_call | solution.py:411
  18.6 0.0 collective-permute-done.1.next_ref
  18.6 0.7 %collective-permute-start.2 = (bf16[4,2,128,256]{3,2,1,0:T(8,128)(2,1)S(1)}, bf16[4,2,128,256]{3,2,1,0:T(8,128)(2,1)S(1)}, u32[]{:S(2)}, u32[]{:S(2)}) collective-permute-start(bf16[4,2,128,256]{3,2,1,0:T(8,128)(2,1)S(1)} %collective-permute-done.1.next_ref), channel_id=1, source_target_pairs={{0,4},{4,0},{1,5},{5,1},{2,6},{6,2},{3,7},{7,3},{8,12},{12,8},{9,1... | collective-permute-start | bytes 1572872 | tf_op jit(solution)/shard_map/ppermute | solution.py:436
  19.4 1.9 %collective-permute-start.4 = (bf16[2,2,528,256]{3,2,1,0:T(8,128)(2,1)}, bf16[2,2,528,256]{3,2,1,0:T(8,128)(2,1)}, u32[]{:S(2)}, u32[]{:S(2)}) collective-permute-start(bf16[2,2,528,256]{3,2,1,0:T(8,128)(2,1)} %get-tuple-element.25.own_hbm), channel_id=1, source_target_pairs={{4,8},{12,16},{20,24},{28,32},{36,40},{44,48},{52,56},{60,64},{68,... | collective-permute-start | bytes 3244040 | tf_op jit(solution)/shard_map/ppermute | solution.py:438
  21.3 0.1 collective-permute-start.3
  21.4 0.7 %broadcast_maximum_fusion.local_ref = f32[16,128]{1,0:T(8,128)S(1)} fusion(f32[16,128]{1,0:T(8,128)} %get-tuple-element.22), kind=kLoop, calls=%fused_computation | loop fusion | flops 2048 | bytes 16384 | tf_op jit(solution)/shard_map/max | solution.py:439
  22.1 0.0 collective-permute-done.pair_ref
  22.1 4.4 %all-to-all-done.q_ref = bf16[16,72,128]{2,1,0:T(8,128)(2,1)S(1)} async-done(((bf16[16,72,128]{2,1,0:T(8,128)(2,1)}), bf16[16,72,128]{2,1,0:T(8,128)(2,1)S(1)}, u32[]{:S(2)}, u32[]{:S(2)}) %all-to-all-start) | async-done | bytes 294944 | tf_op jit(solution)/shard_map/all_to_all | solution.py:409
  26.5 0.0 collective-permute-done.2.cross_ref
  26.5 3.1 %prefix.1 = bf16[16,56,128]{2,1,0:T(8,128)(2,1)} custom-call(bf16[16,72,128]{2,1,0:T(8,128)(2,1)S(1)} %all-to-all-done.q_ref, bf16[4,2,128,256]{3,2,1,0:T(8,128)(2,1)S(1)} %copy-done.5, bf16[4,2,128,256]{3,2,1,0:T(8,128)(2,1)S(1)} %collective-permute-done.pair_ref, bf16[4,2,128,256]{3,2,1,0:T(8,128)(2,1)S(1)} %collective-permute-done.1.next_ref, ...), custom_call_target="tpu_custom_call" | custom-call | flops 20000000000 | bytes 80000000 | tf_op jit(solution)/shard_map/prefix/pallas_call | solution.py:440
  29.6 5.5 %all-to-all-start.1 = ((bf16[16,56,128]{2,1,0:T(8,128)(2,1)}), bf16[16,56,128]{2,1,0:T(8,128)(2,1)S(1)}, u32[]{:S(2)}, u32[]{:S(2)}) async-start(bf16[16,56,128]{2,1,0:T(8,128)(2,1)} %prefix.1), calls=%async_computation.1 | async-start | bytes 458752 | tf_op jit(solution)/shard_map/all_to_all | solution.py:451
  35.1 1.3 %collective-permute-done.4.far_hbm = bf16[2,2,528,256]{3,2,1,0:T(8,128)(2,1)} collective-permute-done((bf16[2,2,528,256]{3,2,1,0:T(8,128)(2,1)}, bf16[2,2,528,256]{3,2,1,0:T(8,128)(2,1)}, u32[]{:S(2)}, u32[]{:S(2)}) %collective-permute-start.4) | collective-permute-done | bytes 1081376 | tf_op jit(solution)/shard_map/ppermute | solution.py:438
  36.4 0.0 collective-permute-done.3.pair_hbm
  36.4 2.5 %second_local.1 = (bf16[2,2,512,256]{3,2,1,0:T(8,128)(2,1)}, bf16[2,2,256]{2,1,0:T(2,128)(2,1)}, f32[40,128]{1,0:T(8,128)S(1)}) custom-call(s32[2]{0:T(128)S(1)} %copy-done.4, f32[64,128]{1,0:T(8,128)S(1)} %copy-done.1, bf16[2,2,528,256]{3,2,1,0:T(8,128)(2,1)S(1)} %copy-done, bf16[2,2,528,256]{3,2,1,0:T(8,128)(2,1)} %collective-permute-done.3.pair_hbm, ...), custom_call_target="tpu_custom_call" | custom-call | tf_op jit(solution)/shard_map/second_local/pallas_call | solution.py:452
  38.9 5.2 %all-to-all-done.1.part_ref = bf16[16,56,128]{2,1,0:T(8,128)(2,1)S(1)} async-done(((bf16[16,56,128]{2,1,0:T(8,128)(2,1)}), bf16[16,56,128]{2,1,0:T(8,128)(2,1)S(1)}, u32[]{:S(2)}, u32[]{:S(2)}) %all-to-all-start.1) | async-done | bytes 229408 | tf_op jit(solution)/shard_map/all_to_all | solution.py:451
  44.1 1.0 %finish.1 = (bf16[2,2048]{1,0:T(2,128)(2,1)}, f32[16,8,128]{2,1,0:T(8,128)S(1)}) custom-call(bf16[16,56,128]{2,1,0:T(8,128)(2,1)S(1)} %all-to-all-done.1.part_ref, f32[40,128]{1,0:T(8,128)S(1)} %get-tuple-element.26.mean_ref, f32[16,128]{1,0:T(8,128)S(1)} %bitcast.3), custom_call_target="tpu_custom_call" | custom-call | tf_op jit(solution)/shard_map/finish/pallas_call | solution.py:469
  45.2 13.2 %all_to_all.15.all_ref = f32[16,8,128]{2,1,0:T(8,128)S(1)} all-to-all(f32[16,8,128]{2,1,0:T(8,128)S(1)} %get-tuple-element.27), channel_id=1, replica_groups=mesh['z2'=2,'z1'=2,'z0'=2,'x1'=2,'x0'=2,'core'=2,'tp'=4] {'x0','core','tp'}, dimensions={0} | all-to-all | bytes 131072 | tf_op jit(solution)/shard_map/all_to_all | solution.py:481
  58.4 1.3 %weights.1 = (f32[2]{0:T(128)}, f32[2]{0:T(128)}) custom-call(f32[16,8,128]{2,1,0:T(8,128)S(1)} %all_to_all.15.all_ref), custom_call_target="tpu_custom_call" | custom-call | tf_op jit(solution)/shard_map/weights/pallas_call | solution.py:482
  (10 shorter events, 0.0 us)
Async XLA Ops:
  0.6 21.5 %collective-permute-start = (bf16[4,2,128,256]{3,2,1,0:T(8,128)(2,1)}, bf16[4,2,128,256]{3,2,1,0:T(8,128)(2,1)S(1)}, u32[]{:S(2)}, u32[]{:S(2)}) collective-permute-start(bf16[4,2,128,256]{3,2,1,0:T(8,128)(2,1)} %own_ref.1), channel_id=1, source_target_pairs={{0,4},{4,0},{1,5},{5,1},{2,6},{6,2},{3,7},{7,3},{8,12},{12,8},{9,1... | collective-permute-start | bytes 1572872 | tf_op jit(solution)/shard_map/ppermute | solution.py:389
  4.0 14.7 %collective-permute-start.1 = (bf16[4,2,128,256]{3,2,1,0:T(8,128)(2,1)}, bf16[4,2,128,256]{3,2,1,0:T(8,128)(2,1)S(1)}, u32[]{:S(2)}, u32[]{:S(2)}) collective-permute-start(bf16[4,2,128,256]{3,2,1,0:T(8,128)(2,1)} %own_ref.1), channel_id=1, source_target_pairs={{0,8},{8,0},{1,9},{9,1},{2,10},{10,2},{3,11},{11,3},{4,12},{12,4},... | collective-permute-start | bytes 1572872 | tf_op jit(solution)/shard_map/ppermute | solution.py:388
  5.5 21.0 %all-to-all-start = ((bf16[16,72,128]{2,1,0:T(8,128)(2,1)}), bf16[16,72,128]{2,1,0:T(8,128)(2,1)S(1)}, u32[]{:S(2)}, u32[]{:S(2)}) async-start(bf16[16,72,128]{2,1,0:T(8,128)(2,1)} %get-tuple-element.19), calls=%async_computation | async-start | bytes 589824 | tf_op jit(solution)/shard_map/all_to_all | solution.py:409
  15.4 11.1 %copy-start.2 = (f32[2048]{0:T(1024)S(1)}, f32[2048]{0:T(1024)}, u32[]{:S(2)}) copy-start(f32[2048]{0:T(1024)} %param.12) | copy-start | bytes 24580
  15.5 11.1 %copy-start.5 = (bf16[4,2,128,256]{3,2,1,0:T(8,128)(2,1)S(1)}, bf16[4,2,128,256]{3,2,1,0:T(8,128)(2,1)}, u32[]{:S(2)}) copy-start(bf16[4,2,128,256]{3,2,1,0:T(8,128)(2,1)} %own_ref.1) | copy-start | bytes 1572868
  18.6 7.9 %collective-permute-start.2 = (bf16[4,2,128,256]{3,2,1,0:T(8,128)(2,1)S(1)}, bf16[4,2,128,256]{3,2,1,0:T(8,128)(2,1)S(1)}, u32[]{:S(2)}, u32[]{:S(2)}) collective-permute-start(bf16[4,2,128,256]{3,2,1,0:T(8,128)(2,1)S(1)} %collective-permute-done.1.next_ref), channel_id=1, source_target_pairs={{0,4},{4,0},{1,5},{5,1},{2,6},{6,2},{3,7},{7,3},{8,12},{12,8},{9,1... | collective-permute-start | bytes 1572872 | tf_op jit(solution)/shard_map/ppermute | solution.py:436
  19.4 17.1 %collective-permute-start.4 = (bf16[2,2,528,256]{3,2,1,0:T(8,128)(2,1)}, bf16[2,2,528,256]{3,2,1,0:T(8,128)(2,1)}, u32[]{:S(2)}, u32[]{:S(2)}) collective-permute-start(bf16[2,2,528,256]{3,2,1,0:T(8,128)(2,1)} %get-tuple-element.25.own_hbm), channel_id=1, source_target_pairs={{4,8},{12,16},{20,24},{28,32},{36,40},{44,48},{52,56},{60,64},{68,... | collective-permute-start | bytes 3244040 | tf_op jit(solution)/shard_map/ppermute | solution.py:438
  21.3 15.1 %collective-permute-start.3 = (bf16[2,2,528,256]{3,2,1,0:T(8,128)(2,1)}, bf16[2,2,528,256]{3,2,1,0:T(8,128)(2,1)}, u32[]{:S(2)}, u32[]{:S(2)}) collective-permute-start(bf16[2,2,528,256]{3,2,1,0:T(8,128)(2,1)} %get-tuple-element.25.own_hbm), channel_id=1, source_target_pairs={{0,4},{4,0},{1,5},{5,1},{2,6},{6,2},{3,7},{7,3},{8,12},{12,8},{9,1... | collective-permute-start | bytes 3244040 | tf_op jit(solution)/shard_map/ppermute | solution.py:437
  22.1 14.3 %copy-start.1 = (f32[64,128]{1,0:T(8,128)S(1)}, f32[64,128]{1,0:T(8,128)}, u32[]{:S(2)}) copy-start(f32[64,128]{1,0:T(8,128)} %get-tuple-element.20.q_hbm.q_ref) | copy-start | bytes 98308
  22.1 14.3 %copy-start.3 = (bf16[2,2,2,256]{3,2,1,0:T(2,128)(2,1)S(1)}, bf16[2,2,2,256]{3,2,1,0:T(2,128)(2,1)}, u32[]{:S(2)}) copy-start(bf16[2,2,2,256]{3,2,1,0:T(2,128)(2,1)} %kv_ref.1) | copy-start | bytes 12292
  22.1 14.3 %copy-start.4 = (s32[2]{0:T(128)S(1)}, s32[2]{0:T(128)}, u32[]{:S(2)}) copy-start(s32[2]{0:T(128)} %anc_ref.1) | copy-start | bytes 28
  26.5 9.9 %copy-start = (bf16[2,2,528,256]{3,2,1,0:T(8,128)(2,1)S(1)}, bf16[2,2,528,256]{3,2,1,0:T(8,128)(2,1)}, u32[]{:S(2)}) copy-start(bf16[2,2,528,256]{3,2,1,0:T(8,128)(2,1)} %get-tuple-element.25.own_hbm) | copy-start | bytes 3244036
  29.6 14.5 %all-to-all-start.1 = ((bf16[16,56,128]{2,1,0:T(8,128)(2,1)}), bf16[16,56,128]{2,1,0:T(8,128)(2,1)S(1)}, u32[]{:S(2)}, u32[]{:S(2)}) async-start(bf16[16,56,128]{2,1,0:T(8,128)(2,1)} %prefix.1), calls=%async_computation.1 | async-start | bytes 458752 | tf_op jit(solution)/shard_map/all_to_all | solution.py:451

commit v7 on v6

--- a/solution.py
+++ b/solution.py
@@ -352,7 +352,7 @@
     row_id = lax.broadcasted_iota(jnp.int32, (8, 128), 0)
     lane_id = lanes((8, 128))
     valid = (lane_id % 16 == 0) & (row_id < PLANE)
-    raised, ids = [], []
+    raised, ids, values, twists = [], [], [], []
     own = jnp.zeros((8, 128), F32)
     own_ids = jnp.zeros((8, 128), F32)
     for m in range(4):
@@ -374,9 +374,12 @@
         amount = jnp.sum(shares[0] + shares[1] + shares[2] + shares[3], keepdims=True)
         mine = jnp.sum(jnp.where(here, own, 0.0), keepdims=True)
         value = mine - (jnp.log(amount) + top)
-        log_ref[p] = value[0, 0]
+        values.append(value)
         twist = jnp.sum(jnp.where((row_id == PLANE) & (lane_id == p), own, 0.0), keepdims=True)
-        twist_ref[p] = twist[0, 0]
+        twists.append(twist)
+    one = lanes((1, 128))
+    log_ref[...] = jnp.where(one == 0, values[0], values[1])[:, 0:2]
+    twist_ref[...] = jnp.where(one == 0, twists[0], twists[1])[:, 0:2]
 
 
 def body(
@@ -481,13 +484,13 @@
     lines = lax.all_to_all(send, SHARE + ("tp",), 0, 0, tiled=True)
     log_weights, twist_two = pl.pallas_call(
         weight_kernel,
-        out_shape=(jax.ShapeDtypeStruct((2,), F32), jax.ShapeDtypeStruct((2,), F32)),
+        out_shape=(jax.ShapeDtypeStruct((1, 2), F32), jax.ShapeDtypeStruct((1, 2), F32)),
         in_specs=[VMEM],
-        out_specs=(SMEM, SMEM),
+        out_specs=(VMEM, VMEM),
         compiler_params=PARAMS,
         name="weights",
     )(lines)
-    return (log_weights, copied, carried, attn, twist_two)
+    return (log_weights.reshape(2), copied, carried, attn, twist_two.reshape(2))
 
 
 def solution(mesh):

time: 60.2 us -> 60.1 us (level)
  waiting for transfers between devices: 10.9 us -> 10 us
  Pallas kernels: 12.5 us -> 13.3 us
    all_to_all x1, waiting for transfers between devices: 5.2 us -> 4.29 us  [body(): received = lax.all_to_all(parts, PEERS, 0, 0, tiled=True)]
    pallas_call x1, Pallas kernels: 2.47 us -> 3.39 us  [body(): pl.pallas_call(second_kernel, out_shape=(jax.ShapeDtypeStruct(suffix_cach...]
  transfers between devices with their start and end apart: 7 -> 7, of which waited for: 3 -> 3; matrix products, arithmetic and copies ran while one was open for 1% -> 1% of each run, Pallas kernels for 17% -> 19%
where the time goes in v7:
time: 60.1 us; the launch traced here: 59.6 us
  starting transfers between devices  21.5 us (36%)
  Pallas kernels  13.3 us (22%)
  blocking collectives  13.2 us (22%)
  waiting for transfers between devices  10 us (17%)
  between operations  0.75 us (1%)
  other arithmetic  0.7 us (1%)
    all_to_all x1, blocking collectives, body(): lines = lax.all_to_all(send, SHARE + ('tp',), 0, 0, tiled=True)  13.2 us
    all_to_all x1, starting transfers between devices, body(): gathered = lax.all_to_all(blocks, PEERS, 0, 0, tiled=True)  9.96 us
    all_to_all x1, starting transfers between devices, body(): received = lax.all_to_all(parts, PEERS, 0, 0, tiled=True)  5.5 us
    all_to_all x1, waiting for transfers between devices, body(): gathered = lax.all_to_all(blocks, PEERS, 0, 0, tiled=True)  4.4 us
    all_to_all x1, waiting for transfers between devices, body(): received = lax.all_to_all(parts, PEERS, 0, 0, tiled=True)  4.29 us
    pallas_call x1, Pallas kernels, body(): pl.pallas_call(second_kernel, out_shape=(jax.ShapeDtypeStruct(suffix_cach...  3.39 us
    ppermute x1, starting transfers between devices, body(): pair_prefix = lax.ppermute(prefix_cache, 'core', swap)  3.33 us
    pallas_call x1, Pallas kernels, body(): pl.pallas_call(first_kernel, out_shape=(jax.ShapeDtypeStruct((8 + 2 * PLA...  3.15 us
  transfers between devices with their start and end apart: 7, of which 3 were waited for; matrix products, arithmetic and copies ran while one was open for 1% of the time, Pallas kernels for 19%

profile of v7, /device:TPU:1, one launch (start us, length us, event | category | flops | bytes accessed | tf_op | source)
XLA Modules:
  0.0 59.6 jit_solution(1603529888564259421)
XLA Ops:
  0.6 3.3 %collective-permute-start = (bf16[4,2,128,256]{3,2,1,0:T(8,128)(2,1)}, bf16[4,2,128,256]{3,2,1,0:T(8,128)(2,1)S(1)}, u32[]{:S(2)}, u32[]{:S(2)}) collective-permute-start(bf16[4,2,128,256]{3,2,1,0:T(8,128)(2,1)} %own_ref.1), channel_id=1, source_target_pairs={{0,4},{4,0},{1,5},{5,1},{2,6},{6,2},{3,7},{7,3},{8,12},{12,8},{9,1... | collective-permute-start | bytes 1572872 | tf_op jit(solution)/shard_map/ppermute | solution.py:392
  4.0 0.0 collective-permute-start.1
  4.0 1.5 %prep.1 = (bf16[16,72,128]{2,1,0:T(8,128)(2,1)}, f32[64,128]{1,0:T(8,128)}) custom-call(s32[2]{0:T(128)} %ids_hbm.3, bf16[2,2,2048]{2,1,0:T(2,128)(2,1)} %q_hbm.1), custom_call_target="tpu_custom_call" | custom-call | tf_op jit(solution)/shard_map/prep/pallas_call | solution.py:395
  5.5 10.0 %all-to-all-start = ((bf16[16,72,128]{2,1,0:T(8,128)(2,1)}), bf16[16,72,128]{2,1,0:T(8,128)(2,1)S(1)}, u32[]{:S(2)}, u32[]{:S(2)}) async-start(bf16[16,72,128]{2,1,0:T(8,128)(2,1)} %get-tuple-element.19), calls=%async_computation | async-start | bytes 589824 | tf_op jit(solution)/shard_map/all_to_all | solution.py:412
  15.4 0.0 copy-start.2
  15.5 0.0 copy-start.5
  15.5 3.1 %first_local.1 = (f32[16,128]{1,0:T(8,128)}, bf16[2,2,528,256]{3,2,1,0:T(8,128)(2,1)}) custom-call(s32[2]{0:T(128)} %ids_hbm.3, f32[2]{0:T(128)} %prior_hbm.1, f32[64,128]{1,0:T(8,128)} %get-tuple-element.20.q_hbm.q_ref, bf16[2,2,2,256]{3,2,1,0:T(2,128)(2,1)} %kv_ref.1, f32[16,128]{1,0:T(8,128)} %bitcast.3, bf16[2,2,512,256]{3,2,1,0:T(8,128)(2,1)} %cache_hbm), custom_call_target="tpu_custom_call" | custom-call | flops 20000000000 | bytes 80000000 | tf_op jit(solution)/shard_map/first_local/pallas_call | solution.py:414
  18.6 0.0 collective-permute-done.1.next_ref
  18.6 0.7 %collective-permute-start.2 = (bf16[4,2,128,256]{3,2,1,0:T(8,128)(2,1)S(1)}, bf16[4,2,128,256]{3,2,1,0:T(8,128)(2,1)S(1)}, u32[]{:S(2)}, u32[]{:S(2)}) collective-permute-start(bf16[4,2,128,256]{3,2,1,0:T(8,128)(2,1)S(1)} %collective-permute-done.1.next_ref), channel_id=1, source_target_pairs={{0,4},{4,0},{1,5},{5,1},{2,6},{6,2},{3,7},{7,3},{8,12},{12,8},{9,1... | collective-permute-start | bytes 1572872 | tf_op jit(solution)/shard_map/ppermute | solution.py:439
  19.4 1.9 %collective-permute-start.4 = (bf16[2,2,528,256]{3,2,1,0:T(8,128)(2,1)}, bf16[2,2,528,256]{3,2,1,0:T(8,128)(2,1)}, u32[]{:S(2)}, u32[]{:S(2)}) collective-permute-start(bf16[2,2,528,256]{3,2,1,0:T(8,128)(2,1)} %get-tuple-element.25.own_hbm), channel_id=1, source_target_pairs={{4,8},{12,16},{20,24},{28,32},{36,40},{44,48},{52,56},{60,64},{68,... | collective-permute-start | bytes 3244040 | tf_op jit(solution)/shard_map/ppermute | solution.py:441
  21.3 0.1 collective-permute-start.3
  21.4 0.7 %broadcast_maximum_fusion.local_ref = f32[16,128]{1,0:T(8,128)S(1)} fusion(f32[16,128]{1,0:T(8,128)} %get-tuple-element.22), kind=kLoop, calls=%fused_computation | loop fusion | flops 2048 | bytes 16384 | tf_op jit(solution)/shard_map/max | solution.py:442
  22.1 0.0 collective-permute-done.pair_ref
  22.1 4.4 %all-to-all-done.q_ref = bf16[16,72,128]{2,1,0:T(8,128)(2,1)S(1)} async-done(((bf16[16,72,128]{2,1,0:T(8,128)(2,1)}), bf16[16,72,128]{2,1,0:T(8,128)(2,1)S(1)}, u32[]{:S(2)}, u32[]{:S(2)}) %all-to-all-start) | async-done | bytes 294944 | tf_op jit(solution)/shard_map/all_to_all | solution.py:412
  26.5 0.0 collective-permute-done.2.cross_ref
  26.5 3.1 %prefix.1 = bf16[16,56,128]{2,1,0:T(8,128)(2,1)} custom-call(bf16[16,72,128]{2,1,0:T(8,128)(2,1)S(1)} %all-to-all-done.q_ref, bf16[4,2,128,256]{3,2,1,0:T(8,128)(2,1)S(1)} %copy-done.5, bf16[4,2,128,256]{3,2,1,0:T(8,128)(2,1)S(1)} %collective-permute-done.pair_ref, bf16[4,2,128,256]{3,2,1,0:T(8,128)(2,1)S(1)} %collective-permute-done.1.next_ref, ...), custom_call_target="tpu_custom_call" | custom-call | flops 20000000000 | bytes 80000000 | tf_op jit(solution)/shard_map/prefix/pallas_call | solution.py:443
  29.6 5.5 %all-to-all-start.1 = ((bf16[16,56,128]{2,1,0:T(8,128)(2,1)}), bf16[16,56,128]{2,1,0:T(8,128)(2,1)S(1)}, u32[]{:S(2)}, u32[]{:S(2)}) async-start(bf16[16,56,128]{2,1,0:T(8,128)(2,1)} %prefix.1), calls=%async_computation.1 | async-start | bytes 458752 | tf_op jit(solution)/shard_map/all_to_all | solution.py:454
  35.1 1.3 %collective-permute-done.4.far_hbm = bf16[2,2,528,256]{3,2,1,0:T(8,128)(2,1)} collective-permute-done((bf16[2,2,528,256]{3,2,1,0:T(8,128)(2,1)}, bf16[2,2,528,256]{3,2,1,0:T(8,128)(2,1)}, u32[]{:S(2)}, u32[]{:S(2)}) %collective-permute-start.4) | collective-permute-done | bytes 1081376 | tf_op jit(solution)/shard_map/ppermute | solution.py:441
  36.4 0.0 collective-permute-done.3.pair_hbm
  36.4 3.4 %second_local.1 = (bf16[2,2,512,256]{3,2,1,0:T(8,128)(2,1)}, bf16[2,2,256]{2,1,0:T(2,128)(2,1)}, f32[40,128]{1,0:T(8,128)S(1)}) custom-call(s32[2]{0:T(128)S(1)} %copy-done.4, f32[64,128]{1,0:T(8,128)S(1)} %copy-done.1, bf16[2,2,528,256]{3,2,1,0:T(8,128)(2,1)S(1)} %copy-done, bf16[2,2,528,256]{3,2,1,0:T(8,128)(2,1)} %collective-permute-done.3.pair_hbm, ...), custom_call_target="tpu_custom_call" | custom-call | tf_op jit(solution)/shard_map/second_local/pallas_call | solution.py:455
  39.8 4.3 %all-to-all-done.1.part_ref = bf16[16,56,128]{2,1,0:T(8,128)(2,1)S(1)} async-done(((bf16[16,56,128]{2,1,0:T(8,128)(2,1)}), bf16[16,56,128]{2,1,0:T(8,128)(2,1)S(1)}, u32[]{:S(2)}, u32[]{:S(2)}) %all-to-all-start.1) | async-done | bytes 229408 | tf_op jit(solution)/shard_map/all_to_all | solution.py:454
  44.1 1.0 %finish.1 = (bf16[2,2048]{1,0:T(2,128)(2,1)}, f32[16,8,128]{2,1,0:T(8,128)S(1)}) custom-call(bf16[16,56,128]{2,1,0:T(8,128)(2,1)S(1)} %all-to-all-done.1.part_ref, f32[40,128]{1,0:T(8,128)S(1)} %get-tuple-element.26.mean_ref, f32[16,128]{1,0:T(8,128)S(1)} %bitcast.5), custom_call_target="tpu_custom_call" | custom-call | tf_op jit(solution)/shard_map/finish/pallas_call | solution.py:472
  45.2 13.2 %all_to_all.15.all_ref = f32[16,8,128]{2,1,0:T(8,128)S(1)} all-to-all(f32[16,8,128]{2,1,0:T(8,128)S(1)} %get-tuple-element.27), channel_id=1, replica_groups=mesh['z2'=2,'z1'=2,'z0'=2,'x1'=2,'x0'=2,'core'=2,'tp'=4] {'x0','core','tp'}, dimensions={0} | all-to-all | bytes 131072 | tf_op jit(solution)/shard_map/all_to_all | solution.py:484
  58.4 1.2 %weights.1 = (f32[1,2]{1,0:T(1,128)}, f32[1,2]{1,0:T(1,128)}) custom-call(f32[16,8,128]{2,1,0:T(8,128)S(1)} %all_to_all.15.all_ref), custom_call_target="tpu_custom_call" | custom-call | tf_op jit(solution)/shard_map/weights/pallas_call | solution.py:485
  (10 shorter events, 0.0 us)
Async XLA Ops:
  0.6 21.5 %collective-permute-start = (bf16[4,2,128,256]{3,2,1,0:T(8,128)(2,1)}, bf16[4,2,128,256]{3,2,1,0:T(8,128)(2,1)S(1)}, u32[]{:S(2)}, u32[]{:S(2)}) collective-permute-start(bf16[4,2,128,256]{3,2,1,0:T(8,128)(2,1)} %own_ref.1), channel_id=1, source_target_pairs={{0,4},{4,0},{1,5},{5,1},{2,6},{6,2},{3,7},{7,3},{8,12},{12,8},{9,1... | collective-permute-start | bytes 1572872 | tf_op jit(solution)/shard_map/ppermute | solution.py:392
  4.0 14.7 %collective-permute-start.1 = (bf16[4,2,128,256]{3,2,1,0:T(8,128)(2,1)}, bf16[4,2,128,256]{3,2,1,0:T(8,128)(2,1)S(1)}, u32[]{:S(2)}, u32[]{:S(2)}) collective-permute-start(bf16[4,2,128,256]{3,2,1,0:T(8,128)(2,1)} %own_ref.1), channel_id=1, source_target_pairs={{0,8},{8,0},{1,9},{9,1},{2,10},{10,2},{3,11},{11,3},{4,12},{12,4},... | collective-permute-start | bytes 1572872 | tf_op jit(solution)/shard_map/ppermute | solution.py:391
  5.5 21.0 %all-to-all-start = ((bf16[16,72,128]{2,1,0:T(8,128)(2,1)}), bf16[16,72,128]{2,1,0:T(8,128)(2,1)S(1)}, u32[]{:S(2)}, u32[]{:S(2)}) async-start(bf16[16,72,128]{2,1,0:T(8,128)(2,1)} %get-tuple-element.19), calls=%async_computation | async-start | bytes 589824 | tf_op jit(solution)/shard_map/all_to_all | solution.py:412
  15.4 11.1 %copy-start.2 = (f32[2048]{0:T(1024)S(1)}, f32[2048]{0:T(1024)}, u32[]{:S(2)}) copy-start(f32[2048]{0:T(1024)} %param.12) | copy-start | bytes 24580
  15.5 11.1 %copy-start.5 = (bf16[4,2,128,256]{3,2,1,0:T(8,128)(2,1)S(1)}, bf16[4,2,128,256]{3,2,1,0:T(8,128)(2,1)}, u32[]{:S(2)}) copy-start(bf16[4,2,128,256]{3,2,1,0:T(8,128)(2,1)} %own_ref.1) | copy-start | bytes 1572868
  18.6 7.9 %collective-permute-start.2 = (bf16[4,2,128,256]{3,2,1,0:T(8,128)(2,1)S(1)}, bf16[4,2,128,256]{3,2,1,0:T(8,128)(2,1)S(1)}, u32[]{:S(2)}, u32[]{:S(2)}) collective-permute-start(bf16[4,2,128,256]{3,2,1,0:T(8,128)(2,1)S(1)} %collective-permute-done.1.next_ref), channel_id=1, source_target_pairs={{0,4},{4,0},{1,5},{5,1},{2,6},{6,2},{3,7},{7,3},{8,12},{12,8},{9,1... | collective-permute-start | bytes 1572872 | tf_op jit(solution)/shard_map/ppermute | solution.py:439
  19.4 17.1 %collective-permute-start.4 = (bf16[2,2,528,256]{3,2,1,0:T(8,128)(2,1)}, bf16[2,2,528,256]{3,2,1,0:T(8,128)(2,1)}, u32[]{:S(2)}, u32[]{:S(2)}) collective-permute-start(bf16[2,2,528,256]{3,2,1,0:T(8,128)(2,1)} %get-tuple-element.25.own_hbm), channel_id=1, source_target_pairs={{4,8},{12,16},{20,24},{28,32},{36,40},{44,48},{52,56},{60,64},{68,... | collective-permute-start | bytes 3244040 | tf_op jit(solution)/shard_map/ppermute | solution.py:441
  21.3 15.1 %collective-permute-start.3 = (bf16[2,2,528,256]{3,2,1,0:T(8,128)(2,1)}, bf16[2,2,528,256]{3,2,1,0:T(8,128)(2,1)}, u32[]{:S(2)}, u32[]{:S(2)}) collective-permute-start(bf16[2,2,528,256]{3,2,1,0:T(8,128)(2,1)} %get-tuple-element.25.own_hbm), channel_id=1, source_target_pairs={{0,4},{4,0},{1,5},{5,1},{2,6},{6,2},{3,7},{7,3},{8,12},{12,8},{9,1... | collective-permute-start | bytes 3244040 | tf_op jit(solution)/shard_map/ppermute | solution.py:440
  22.1 14.3 %copy-start.1 = (f32[64,128]{1,0:T(8,128)S(1)}, f32[64,128]{1,0:T(8,128)}, u32[]{:S(2)}) copy-start(f32[64,128]{1,0:T(8,128)} %get-tuple-element.20.q_hbm.q_ref) | copy-start | bytes 98308
  22.1 14.3 %copy-start.3 = (bf16[2,2,2,256]{3,2,1,0:T(2,128)(2,1)S(1)}, bf16[2,2,2,256]{3,2,1,0:T(2,128)(2,1)}, u32[]{:S(2)}) copy-start(bf16[2,2,2,256]{3,2,1,0:T(2,128)(2,1)} %kv_ref.1) | copy-start | bytes 12292
  22.1 14.3 %copy-start.4 = (s32[2]{0:T(128)S(1)}, s32[2]{0:T(128)}, u32[]{:S(2)}) copy-start(s32[2]{0:T(128)} %anc_ref.1) | copy-start | bytes 28
  26.5 9.9 %copy-start = (bf16[2,2,528,256]{3,2,1,0:T(8,128)(2,1)S(1)}, bf16[2,2,528,256]{3,2,1,0:T(8,128)(2,1)}, u32[]{:S(2)}) copy-start(bf16[2,2,528,256]{3,2,1,0:T(8,128)(2,1)} %get-tuple-element.25.own_hbm) | copy-start | bytes 3244036
  29.6 14.5 %all-to-all-start.1 = ((bf16[16,56,128]{2,1,0:T(8,128)(2,1)}), bf16[16,56,128]{2,1,0:T(8,128)(2,1)S(1)}, u32[]{:S(2)}, u32[]{:S(2)}) async-start(bf16[16,56,128]{2,1,0:T(8,128)(2,1)} %prefix.1), calls=%async_computation.1 | async-start | bytes 458752 | tf_op jit(solution)/shard_map/all_to_all | solution.py:454
